TPU v7x, 128 devices: a whole 4x4x4 slice. The times are simulated.
128 devices in a mesh: fsdp: 16 (over x_hi, z, core), tp: 8 (over y, x_lo).
Axes of the slice: x: 4 (x_hi: 2, x_lo: 2; x = x_hi * 2 + x_lo), y: 4, z: 4, core: 2. Of those that a mesh axis runs over, the one named last changes fastest.
Arguments:
- inputs: bfloat16 [16384, 1024], P(('fsdp', 'tp')), may hold values from -6 to 6
- lengths: int32 [16, 3], P('fsdp'), may hold values from 1 to 1024, as said below
- routes: int32 [16384, 8], P('fsdp'), may hold values from 0 to 31, all different within a row; in each aligned block of 1024 rows (0 to 1023, 1024 to 2047, ...) at most 341 rows name the same one
- attn_gain: bfloat16 [1024], P('fsdp'), may hold values from 0.5 to 1.5
- query_weight: bfloat16 [1024, 1024], P('fsdp', 'tp'), may hold values from -0.5 to 0.5
- key_weight: bfloat16 [1024, 512], P('fsdp', 'tp'), may hold values from -0.5 to 0.5
- value_weight: bfloat16 [1024, 512], P('fsdp', 'tp'), may hold values from -0.1875 to 0.1875
- output_weight: bfloat16 [1024, 1024], P('tp', 'fsdp'), may hold values from -2 to 2
- moe_gain: bfloat16 [1024], P('fsdp'), may hold values from 0.5 to 1.5
- router_weight: bfloat16 [1024, 32], P('fsdp'), may hold values from -0.09375 to 0.09375
- gate_weight: bfloat16 [32, 1024, 512], P('tp', 'fsdp'), may hold values from -0.1875 to 0.1875
- up_weight: bfloat16 [32, 1024, 512], P('tp', 'fsdp'), may hold values from -0.1875 to 0.1875
- down_weight: bfloat16 [32, 512, 1024], P('tp', None, 'fsdp'), may hold values from -1 to 1
- cotangent: bfloat16 [16384, 1024], P(('fsdp', 'tp')), may hold values from -6 to 6
Outputs:
- outputs: bfloat16 [16384, 1024], P(('fsdp', 'tp'))
- input_grad: float32 [16384, 1024], P(('fsdp', 'tp'))
- attn_gain_grad: float32 [1024], P(('fsdp', 'tp'))
- query_grad: float32 [1024, 1024], P('fsdp', 'tp')
- key_grad: float32 [1024, 512], P('fsdp', 'tp')
- value_grad: float32 [1024, 512], P('fsdp', 'tp')
- output_grad: float32 [1024, 1024], P('tp', 'fsdp')
- moe_gain_grad: float32 [1024], P(('fsdp', 'tp'))
- router_grad: float32 [1024, 32], P(('fsdp', 'tp'))
- gate_grad: float32 [32, 1024, 512], P('tp', 'fsdp')
- up_grad: float32 [32, 1024, 512], P('tp', 'fsdp')
- down_grad: float32 [32, 512, 1024], P('tp', None, 'fsdp')
Inputs may be any that keep to these rules, and one draw needn't show every extreme that they name: `lengths`: each row sums to 1024; one length in each row is at least 896, the others are at most 64. `routes`: in each aligned block of 1024 rows no expert is named by more than 341 rows, and in some block one is named by exactly 341.
All inputs are finite; a program needn't handle non-finite values.
Results may differ from a plain program's by a relative error of at most 0.025.
Values may be sent and summed in bfloat16 or wider, within the bound.
A program may use at most 128 MiB of HBM per device.

v0:
```python
import jax
import jax.numpy as jnp
from jax import lax
from jax.sharding import PartitionSpec as P

D = 1024
HEADS = 16
KV_HEADS = 8
HEAD_DIM = 64
EXPERTS = 32
TOPK = 8
GROUP = 1024
SEQS = 3
CAP = 341


eps_norm = 1e-06
rope_base = 10000.0


def rms_parts(values, gain):
    mean_square = jnp.mean(values * values, axis=-1, keepdims=True)
    inverse = lax.rsqrt(mean_square + eps_norm)
    unit_rows = values * inverse
    return (unit_rows * gain, unit_rows, inverse)


def rms_back(grad_out, unit_rows, inverse, gain):
    grad_unit = grad_out * gain
    grad_in = inverse * (
        grad_unit - unit_rows * jnp.mean(grad_unit * unit_rows, axis=-1, keepdims=True)
    )
    return (grad_in, jnp.sum(grad_out * unit_rows, axis=0))


def rotate(values, cosine, sine):
    half_dim = values.shape[-1] // 2
    turned = jnp.concatenate([-values[..., half_dim:], values[..., :half_dim]], axis=-1)
    return values * cosine + turned * sine


def rotate_back(grads, cosine, sine):
    half_dim = grads.shape[-1] // 2
    turned = grads * sine
    return grads * cosine + jnp.concatenate(
        [turned[..., half_dim:], -turned[..., :half_dim]], axis=-1
    )


def doc_layout(lengths_row):
    seq_ends = jnp.cumsum(lengths_row)
    positions = jnp.arange(GROUP, dtype=jnp.int32)
    doc_index = jnp.sum((positions[:, None] >= seq_ends[None, :]).astype(jnp.int32), axis=1)
    starts = seq_ends - lengths_row
    match = doc_index[:, None] == jnp.arange(SEQS, dtype=jnp.int32)[None, :]
    doc_start = jnp.sum(jnp.where(match, starts[None, :], 0), axis=1)
    return (doc_index, positions - doc_start)


def rope_tables(offset):
    frequency = rope_base ** (-jnp.arange(0, HEAD_DIM // 2, dtype=jnp.float32) * 2.0 / HEAD_DIM)
    angles = offset.astype(jnp.float32)[:, None] * frequency[None, :]
    angles = jnp.concatenate([angles, angles], axis=1)
    return (jnp.cos(angles), jnp.sin(angles))


def slot_tables(route_rows):
    flat_expert = route_rows.reshape(-1)
    onehot = (flat_expert[:, None] == jnp.arange(EXPERTS, dtype=jnp.int32)[None, :]).astype(
        jnp.int32
    )
    running = jnp.cumsum(onehot, axis=0)
    slot_index = jnp.sum(onehot * (running - 1), axis=1)
    where_to = flat_expert * CAP + slot_index
    entries = jnp.arange(GROUP * TOPK, dtype=jnp.int32)
    token_of = jnp.full((EXPERTS * CAP,), GROUP, jnp.int32).at[where_to].set(entries // TOPK)
    entry_of = jnp.full((EXPERTS * CAP,), GROUP * TOPK, jnp.int32).at[where_to].set(entries)
    return (token_of, entry_of)


def block_mask(block_start, block_rows, doc_index):
    positions = jnp.arange(doc_index.shape[0], dtype=jnp.int32)
    place_block = block_start + jnp.arange(block_rows, dtype=jnp.int32)
    doc_block = lax.dynamic_slice_in_dim(doc_index, block_start, block_rows, 0)
    allowed = (place_block[:, None] >= positions[None, :]) & (
        doc_block[:, None] == doc_index[None, :]
    )
    return allowed[None, None]


def attend_forward(query_low, key_low, value_low, doc_index, score_scale):
    total_rows = query_low.shape[0]
    block_rows = min(512, total_rows)

    def one_block(block_start):
        query_block = lax.dynamic_slice_in_dim(query_low, block_start, block_rows, 0)
        scores = (
            jnp.einsum("qgrd,kgd->grqk", query_block, key_low, preferred_element_type=jnp.float32)
            * score_scale
        )
        scores = jnp.where(block_mask(block_start, block_rows, doc_index), scores, -1e30)
        top_score = jnp.max(scores, axis=-1, keepdims=True)
        raised = jnp.exp(scores - top_score)
        row_total = jnp.sum(raised, axis=-1, keepdims=True)
        weights = raised / row_total
        mixed_block = jnp.einsum(
            "grqk,kgd->qgrd",
            weights.astype(jnp.bfloat16),
            value_low,
            preferred_element_type=jnp.float32,
        )
        return (mixed_block, (top_score + jnp.log(row_total))[..., 0])

    starts = jnp.arange(total_rows // block_rows, dtype=jnp.int32) * block_rows
    mixed_blocks, log_total = lax.map(one_block, starts)
    return (mixed_blocks.reshape(query_low.shape), log_total)


def attend_backward(query_low, key_low, value_low, grad_mixed, log_total, doc_index, score_scale):
    total_rows = query_low.shape[0]
    block_rows = min(512, total_rows)

    def one_block(carry, block_index):
        grad_keys, grad_values = carry
        block_start = block_index * block_rows
        query_block = lax.dynamic_slice_in_dim(query_low, block_start, block_rows, 0)
        grad_block = lax.dynamic_slice_in_dim(grad_mixed, block_start, block_rows, 0)
        scores = (
            jnp.einsum("qgrd,kgd->grqk", query_block, key_low, preferred_element_type=jnp.float32)
            * score_scale
        )
        scores = jnp.where(block_mask(block_start, block_rows, doc_index), scores, -1e30)
        weights = jnp.exp(scores - log_total[block_index][..., None])
        grad_weights = jnp.einsum(
            "qgrd,kgd->grqk", grad_block, value_low, preferred_element_type=jnp.float32
        )
        inner = jnp.sum(weights * grad_weights, axis=-1, keepdims=True)
        grad_scores = (weights * (grad_weights - inner)).astype(jnp.bfloat16)
        grad_query = (
            jnp.einsum("grqk,kgd->qgrd", grad_scores, key_low, preferred_element_type=jnp.float32)
            * score_scale
        )
        grad_keys = (
            grad_keys
            + jnp.einsum(
                "grqk,qgrd->kgd", grad_scores, query_block, preferred_element_type=jnp.float32
            )
            * score_scale
        )
        grad_values = grad_values + jnp.einsum(
            "grqk,qgrd->kgd",
            weights.astype(jnp.bfloat16),
            grad_block,
            preferred_element_type=jnp.float32,
        )
        return ((grad_keys, grad_values), grad_query)

    empty = jnp.zeros(key_low.shape, jnp.float32)
    indices = jnp.arange(total_rows // block_rows, dtype=jnp.int32)
    (grad_keys, grad_values), grad_query = lax.scan(one_block, (empty, empty), indices)
    return (grad_query.reshape(query_low.shape), grad_keys, grad_values)


def per_device(
    inputs,
    lengths,
    routes,
    attn_gain,
    query_weight,
    key_weight,
    value_weight,
    output_weight,
    moe_gain,
    router_weight,
    gate_weight,
    up_weight,
    down_weight,
    cotangent,
):
    tp_rank = lax.axis_index("tp")
    local_rows = inputs.shape[0]
    row_start = tp_rank * local_rows
    score_scale = 1.0 / HEAD_DIM
    repeat = HEADS // KV_HEADS
    gain_one, query_all, key_all, value_all, output_all = (
        lax.all_gather(attn_gain, "fsdp", axis=0, tiled=True),
        lax.all_gather(query_weight, "fsdp", axis=0, tiled=True),
        lax.all_gather(key_weight, "fsdp", axis=0, tiled=True),
        lax.all_gather(value_weight, "fsdp", axis=0, tiled=True),
        lax.all_gather(output_weight, "fsdp", axis=1, tiled=True),
    )
    gain_one = gain_one.astype(jnp.float32)
    block_in = inputs.astype(jnp.float32)
    normed, unit_one, inverse_one = rms_parts(block_in, gain_one)
    normed_low = normed.astype(jnp.bfloat16)
    gathered = lax.all_gather(normed_low, "tp", axis=0, tiled=True)
    doc_index, offset = doc_layout(lengths[0])
    cosine, sine = rope_tables(offset)
    kv_local = key_all.shape[1] // HEAD_DIM
    query_raw = jnp.dot(gathered, query_all, preferred_element_type=jnp.float32).reshape(
        GROUP, kv_local, repeat, HEAD_DIM
    )
    key_raw = jnp.dot(gathered, key_all, preferred_element_type=jnp.float32).reshape(
        GROUP, kv_local, HEAD_DIM
    )
    value_low = (
        jnp.dot(gathered, value_all, preferred_element_type=jnp.float32)
        .astype(jnp.bfloat16)
        .reshape(GROUP, kv_local, HEAD_DIM)
    )
    query_low = rotate(query_raw, cosine[:, None, None, :], sine[:, None, None, :]).astype(
        jnp.bfloat16
    )
    key_low = rotate(key_raw, cosine[:, None, :], sine[:, None, :]).astype(jnp.bfloat16)
    mixed, log_total = attend_forward(query_low, key_low, value_low, doc_index, score_scale)
    mixed_low = mixed.reshape(GROUP, -1).astype(jnp.bfloat16)
    attended = lax.psum_scatter(
        jnp.dot(mixed_low, output_all, preferred_element_type=jnp.float32),
        "tp",
        scatter_dimension=0,
        tiled=True,
    )
    middle = block_in + attended
    gain_two, router_all, gate_all, up_all, down_all = (
        lax.all_gather(moe_gain, "fsdp", axis=0, tiled=True),
        lax.all_gather(router_weight, "fsdp", axis=0, tiled=True),
        lax.all_gather(gate_weight, "fsdp", axis=1, tiled=True),
        lax.all_gather(up_weight, "fsdp", axis=1, tiled=True),
        lax.all_gather(down_weight, "fsdp", axis=2, tiled=True),
    )
    gain_two_f32 = gain_two.astype(jnp.float32)
    normed_two, unit_two, inverse_two = rms_parts(middle, gain_two_f32)
    normed_two_low = normed_two.astype(jnp.bfloat16)
    gathered_two = lax.all_gather(normed_two_low, "tp", axis=0, tiled=True)
    logits = jnp.dot(gathered_two, router_all, preferred_element_type=jnp.float32)
    chosen_mask = (
        routes[:, :, None] == jnp.arange(EXPERTS, dtype=jnp.int32)[None, None, :]
    ).astype(jnp.float32)
    chosen = jnp.sum(chosen_mask * logits[:, None, :], axis=-1)
    gates = jax.nn.softmax(chosen, axis=-1)
    token_of, entry_of = slot_tables(routes)
    local_experts = gate_all.shape[0]
    slot_start = tp_rank * local_experts * CAP
    token_own = lax.dynamic_slice_in_dim(token_of, slot_start, local_experts * CAP, 0)
    entry_own = lax.dynamic_slice_in_dim(entry_of, slot_start, local_experts * CAP, 0)
    padded = jnp.concatenate([gathered_two, jnp.zeros((1, D), jnp.bfloat16)], axis=0)
    dispatched = padded[token_own].reshape(local_experts, CAP, D)
    gate_part = jnp.einsum("ecd,edh->ech", dispatched, gate_all, preferred_element_type=jnp.float32)
    up_part = jnp.einsum("ecd,edh->ech", dispatched, up_all, preferred_element_type=jnp.float32)
    sigmoid_gate = jax.nn.sigmoid(gate_part)
    silu_gate = gate_part * sigmoid_gate
    hidden_low = (silu_gate * up_part).astype(jnp.bfloat16)
    expert_out = jnp.einsum(
        "ech,ehd->ecd", hidden_low, down_all, preferred_element_type=jnp.float32
    ).reshape(-1, D)
    gate_pad = jnp.concatenate([gates.reshape(-1), jnp.zeros((1,), jnp.float32)])
    slot_gate = gate_pad[entry_own]
    combined = (
        jnp.zeros((GROUP + 1, D), jnp.float32)
        .at[token_own]
        .add(slot_gate[:, None] * expert_out)[:GROUP]
    )
    moe_out = lax.psum_scatter(
        combined.astype(jnp.bfloat16), "tp", scatter_dimension=0, tiled=True
    ).astype(jnp.float32)
    outputs = (middle + moe_out).astype(jnp.bfloat16)
    grad_rows = lax.all_gather(cotangent, "tp", axis=0, tiled=True)
    grad_padded = jnp.concatenate([grad_rows, jnp.zeros((1, D), jnp.bfloat16)], axis=0)
    grad_slots = grad_padded[token_own].astype(jnp.float32)
    slot_grad_gate = jnp.sum(grad_slots * expert_out, axis=-1)
    grad_expert_out = (
        (slot_gate[:, None] * grad_slots).astype(jnp.bfloat16).reshape(local_experts, CAP, D)
    )
    grad_hidden = jnp.einsum(
        "ecd,ehd->ech", grad_expert_out, down_all, preferred_element_type=jnp.float32
    )
    down_grad_part = jnp.einsum(
        "ech,ecd->ehd", hidden_low, grad_expert_out, preferred_element_type=jnp.float32
    )
    grad_gate_low = (
        grad_hidden * up_part * sigmoid_gate * (1.0 + gate_part * (1.0 - sigmoid_gate))
    ).astype(jnp.bfloat16)
    grad_up_low = (grad_hidden * silu_gate).astype(jnp.bfloat16)
    gate_grad_part = jnp.einsum(
        "ecd,ech->edh", dispatched, grad_gate_low, preferred_element_type=jnp.float32
    )
    up_grad_part = jnp.einsum(
        "ecd,ech->edh", dispatched, grad_up_low, preferred_element_type=jnp.float32
    )
    grad_dispatched = jnp.einsum(
        "ech,edh->ecd", grad_gate_low, gate_all, preferred_element_type=jnp.float32
    )
    grad_dispatched = grad_dispatched + jnp.einsum(
        "ech,edh->ecd", grad_up_low, up_all, preferred_element_type=jnp.float32
    )
    grad_normed_part = (
        jnp.zeros((GROUP + 1, D), jnp.float32)
        .at[token_own]
        .add(grad_dispatched.reshape(-1, D))[:GROUP]
    )
    grad_gate_part = (
        jnp.zeros((GROUP * TOPK + 1,), jnp.float32)
        .at[entry_own]
        .add(slot_grad_gate)[: GROUP * TOPK]
        .reshape(GROUP, TOPK)
    )
    grad_normed_two, grad_gates = (
        lax.psum_scatter(
            grad_normed_part.astype(jnp.bfloat16), "tp", scatter_dimension=0, tiled=True
        ).astype(jnp.float32),
        lax.psum_scatter(
            grad_gate_part.astype(jnp.bfloat16), "tp", scatter_dimension=0, tiled=True
        ).astype(jnp.float32),
    )
    gates_own = lax.dynamic_slice_in_dim(gates, row_start, local_rows, 0)
    mask_own = lax.dynamic_slice_in_dim(chosen_mask, row_start, local_rows, 0)
    grad_chosen = gates_own * (grad_gates - jnp.sum(gates_own * grad_gates, axis=-1, keepdims=True))
    grad_logits = jnp.sum(mask_own * grad_chosen[:, :, None], axis=1).astype(jnp.bfloat16)
    grad_normed_two = grad_normed_two + jnp.einsum(
        "te,de->td", grad_logits, router_all, preferred_element_type=jnp.float32
    )
    router_grad_part = jnp.einsum(
        "td,te->de", normed_two_low, grad_logits, preferred_element_type=jnp.float32
    )
    grad_middle, gain_two_grad = rms_back(grad_normed_two, unit_two, inverse_two, gain_two_f32)
    grad_middle = grad_middle + cotangent.astype(jnp.float32)
    grad_attended_low = grad_middle.astype(jnp.bfloat16)
    grad_mixed_rows = lax.all_gather(grad_attended_low, "tp", axis=0, tiled=True)
    output_grad_part = jnp.einsum(
        "tc,td->cd", mixed_low, grad_mixed_rows, preferred_element_type=jnp.float32
    )
    grad_mixed = jnp.einsum(
        "td,cd->tc", grad_mixed_rows, output_all, preferred_element_type=jnp.float32
    )
    grad_mixed = grad_mixed.astype(jnp.bfloat16).reshape(GROUP, kv_local, repeat, HEAD_DIM)
    grad_query, grad_keys, grad_values = attend_backward(
        query_low, key_low, value_low, grad_mixed, log_total, doc_index, score_scale
    )
    grad_query_low = (
        rotate_back(grad_query, cosine[:, None, None, :], sine[:, None, None, :])
        .reshape(GROUP, -1)
        .astype(jnp.bfloat16)
    )
    grad_key_low = (
        rotate_back(grad_keys, cosine[:, None, :], sine[:, None, :])
        .reshape(GROUP, -1)
        .astype(jnp.bfloat16)
    )
    grad_value_low = grad_values.reshape(GROUP, -1).astype(jnp.bfloat16)
    term = jnp.einsum("tc,dc->td", grad_query_low, query_all, preferred_element_type=jnp.float32)
    term = term + jnp.einsum("tc,dc->td", grad_key_low, key_all, preferred_element_type=jnp.float32)
    grad_normed = lax.psum_scatter(
        (
            term
            + jnp.einsum("tc,dc->td", grad_value_low, value_all, preferred_element_type=jnp.float32)
        ).astype(jnp.bfloat16),
        "tp",
        scatter_dimension=0,
        tiled=True,
    ).astype(jnp.float32)
    query_grad_part = jnp.einsum(
        "td,tc->dc", gathered, grad_query_low, preferred_element_type=jnp.float32
    )
    key_grad_part = jnp.einsum(
        "td,tc->dc", gathered, grad_key_low, preferred_element_type=jnp.float32
    )
    value_grad_part = jnp.einsum(
        "td,tc->dc", gathered, grad_value_low, preferred_element_type=jnp.float32
    )
    grad_input, gain_one_grad = rms_back(grad_normed, unit_one, inverse_one, gain_one)
    grad_input = grad_input + grad_middle
    query_grad, key_grad, value_grad, output_grad = (
        lax.psum_scatter(
            query_grad_part.astype(jnp.bfloat16), "fsdp", scatter_dimension=0, tiled=True
        ).astype(jnp.float32),
        lax.psum_scatter(
            key_grad_part.astype(jnp.bfloat16), "fsdp", scatter_dimension=0, tiled=True
        ).astype(jnp.float32),
        lax.psum_scatter(
            value_grad_part.astype(jnp.bfloat16), "fsdp", scatter_dimension=0, tiled=True
        ).astype(jnp.float32),
        lax.psum_scatter(
            output_grad_part.astype(jnp.bfloat16), "fsdp", scatter_dimension=1, tiled=True
        ).astype(jnp.float32),
    )
    gate_grad, up_grad, down_grad = (
        lax.psum_scatter(
            gate_grad_part.astype(jnp.bfloat16), "fsdp", scatter_dimension=1, tiled=True
        ).astype(jnp.float32),
        lax.psum_scatter(
            up_grad_part.astype(jnp.bfloat16), "fsdp", scatter_dimension=1, tiled=True
        ).astype(jnp.float32),
        lax.psum_scatter(
            down_grad_part.astype(jnp.bfloat16), "fsdp", scatter_dimension=2, tiled=True
        ).astype(jnp.float32),
    )
    attn_gain_grad, moe_gain_grad, router_grad = (
        lax.psum_scatter(gain_one_grad, ("fsdp", "tp"), scatter_dimension=0, tiled=True),
        lax.psum_scatter(gain_two_grad, ("fsdp", "tp"), scatter_dimension=0, tiled=True),
        lax.psum_scatter(router_grad_part, ("fsdp", "tp"), scatter_dimension=0, tiled=True),
    )
    return (
        outputs,
        grad_input,
        attn_gain_grad,
        query_grad,
        key_grad,
        value_grad,
        output_grad,
        moe_gain_grad,
        router_grad,
        gate_grad,
        up_grad,
        down_grad,
    )


def solution(mesh):
    return jax.shard_map(
        per_device,
        mesh=mesh,
        in_specs=(
            P(("fsdp", "tp"), None),
            P("fsdp", None),
            P("fsdp", None),
            P("fsdp"),
            P("fsdp", "tp"),
            P("fsdp", "tp"),
            P("fsdp", "tp"),
            P("tp", "fsdp"),
            P("fsdp"),
            P("fsdp", None),
            P("tp", "fsdp", None),
            P("tp", "fsdp", None),
            P("tp", None, "fsdp"),
            P(("fsdp", "tp"), None),
        ),
        out_specs=(
            P(("fsdp", "tp"), None),
            P(("fsdp", "tp"), None),
            P(("fsdp", "tp")),
            P("fsdp", "tp"),
            P("fsdp", "tp"),
            P("fsdp", "tp"),
            P("tp", "fsdp"),
            P(("fsdp", "tp")),
            P(("fsdp", "tp"), None),
            P("tp", "fsdp", None),
            P("tp", "fsdp", None),
            P("tp", None, "fsdp"),
        ),
        check_vma=False,
    )
```

profile of v0, /device:TPU:0, one launch (start us, length us, event | category | flops | bytes accessed | tf_op | source)
XLA Modules:
  0.0 1516.0 jit_solution(9103484293301756725)
XLA Ops:
  10.8 39.2 %all-reduce.8 = (bf16[1024]{0:T(1024)(128)(2,1)S(1)}, bf16[1024]{0:T(1024)(128)(2,1)S(1)}) all-reduce(bf16[1024]{0:T(1024)(128)(2,1)S(1)} %dynamic-update-slice, bf16[1024]{0:T(1024)(128)(2,1)S(1)} %dynamic-update-slice.1), channel_id=1, replica_groups=mesh['fsdp'=16,'tp'=8] {'fsdp'}, use_global_device_ids=true, to_apply=%add.2 | all-reduce | flops 2048 | bytes 8192
  54.3 20.5 %all_gather.45 = bf16[1024,64]{1,0:T(8,128)(2,1)S(1)} all-gather(bf16[64,64]{1,0:T(8,128)(2,1)} %param.23), channel_id=1, replica_groups=mesh['fsdp'=16,'tp'=8] {'fsdp'}, dimensions={0}, use_global_device_ids=true | all-gather | bytes 139264 | tf_op jit(solution)/shard_map/all_gather | solution.py:188
  74.8 22.5 %all_gather.46 = bf16[1024,64]{1,0:T(8,128)(2,1)S(1)} all-gather(bf16[64,64]{1,0:T(8,128)(2,1)} %param.24), channel_id=1, replica_groups=mesh['fsdp'=16,'tp'=8] {'fsdp'}, dimensions={0}, use_global_device_ids=true | all-gather | bytes 139264 | tf_op jit(solution)/shard_map/all_gather | solution.py:189
  98.2 20.2 %all_gather.44 = bf16[1024,128]{1,0:T(8,128)(2,1)S(1)} all-gather(bf16[64,128]{1,0:T(8,128)(2,1)} %param.22), channel_id=1, replica_groups=mesh['fsdp'=16,'tp'=8] {'fsdp'}, dimensions={0}, use_global_device_ids=true | all-gather | bytes 278528 | tf_op jit(solution)/shard_map/all_gather | solution.py:187
  118.5 21.6 %all_gather.47 = bf16[128,1024]{0,1:T(8,128)(2,1)S(1)} all-gather(bf16[128,64]{0,1:T(8,128)(2,1)} %param.25), channel_id=1, replica_groups=mesh['fsdp'=16,'tp'=8] {'fsdp'}, dimensions={1}, use_global_device_ids=true | all-gather | bytes 278528 | tf_op jit(solution)/shard_map/all_gather | solution.py:190
  148.4 15.2 %while.27 = (s32[]{:T(128)}, bf16[2,512,1,2,64]{1,4,3,2,0:T(8,128)(2,1)S(1)}, f32[2,1,2,512]{3,2,1,0:T(2,128)S(1)}, s32[2]{0:T(128)S(1)}, s32[1024]{0:T(1024)S(1...) while((s32[]{:T(128)}, ...), condition=%wide.region_7.8_spmd, body=%wide.region_4.7_spmd.sunk | while | flops 282590720 | bytes 15382703 | solution.py:115
  167.8 88.2 %reduce-scatter.15.cloned.1.call-done = f32[128,1024]{1,0:T(8,128)} async-done(((f32[1024,1024]{1,0:T(8,128)}), f32[128,1024]{1,0:T(8,128)}) %reduce-scatter.15.cloned.1.call-update) | async-done | bytes 524304 | tf_op jit(solution)/shard_map/reduce_scatter | solution.py:217
  260.7 24.9 %all-gather = bf16[16,64,32]{1,2,0:T(8,128)(2,1)S(1)} all-gather(bf16[1,64,32]{1,2,0:T(8,128)(2,1)S(1)} %bitcast.353), channel_id=1, replica_groups=mesh['fsdp'=16,'tp'=8] {'fsdp'}, dimensions={0}, use_global_device_ids=true | all-gather | bytes 69632 | tf_op jit(solution)/shard_map/all_gather | solution.py:226
  285.9 9.5 reduce-window.11
  298.3 30.5 %scatter_custom_fusion = s32[10912]{0:T(1024)S(1)} fusion(s32[8192]{0:T(1024)S(1)} %bitcast.351, s32[8192]{0:T(1024)S(1)} %add_select_fusion, s32[]{:T(128)} %constant.66.clone.1), kind=kCustom, calls=%fused_computation.188 | custom fusion | bytes 43652 | tf_op jit(solution)/shard_map/scatter | solution.py:76
  328.7 30.5 %scatter_custom_fusion.1 = s32[10912]{0:T(1024)S(1)} fusion(s32[8192]{0:T(1024)S(1)} %bitcast.352, s32[8192]{0:T(1024)S(1)} %iota.70, s32[]{:T(128)} %constant.124.clone.1), kind=kCustom, calls=%fused_computation.186 | custom fusion | bytes 43652 | tf_op jit(solution)/shard_map/scatter | solution.py:77
  393.4 27.3 %all-gather.13.cloned.1.call-done = bf16[4,1024,512]{2,1,0:T(8,128)(2,1)} async-done(((bf16[4,64,512]{2,1,0:T(8,128)(2,1)}), bf16[4,1024,512]{2,1,0:T(8,128)(2,1)}) %all-gather.13.cloned.1.call-update) | async-done | bytes 4194320 | tf_op jit(solution)/shard_map/all_gather | solution.py:227
  426.1 50.2 %all-gather.15.cloned.1.call-done = bf16[4,1024,512]{2,1,0:T(8,128)(2,1)} async-done(((bf16[4,64,512]{2,1,0:T(8,128)(2,1)}), bf16[4,1024,512]{2,1,0:T(8,128)(2,1)}) %all-gather.15.cloned.1.call-update) | async-done | bytes 4194320 | tf_op jit(solution)/shard_map/all_gather | solution.py:228
  481.6 50.4 %all-gather.17.cloned.1.call-done = bf16[4,512,1024]{1,2,0:T(8,128)(2,1)} async-done(((bf16[4,512,64]{1,2,0:T(8,128)(2,1)}), bf16[4,512,1024]{1,2,0:T(8,128)(2,1)}) %all-gather.17.cloned.1.call-update) | async-done | bytes 4194320 | tf_op jit(solution)/shard_map/all_gather | solution.py:229
  532.0 9.6 multiply_convert_fusion.1
  541.6 7.9 multiply_reduce_fusion
  550.9 11.9 scatter_custom_fusion.4
  580.3 16.9 %scatter_custom_fusion.3 = f32[1025,1024]{1,0:T(8,128)} fusion(s32[1364]{0:T(1024)} %copy-done.44, f32[1364,1024]{1,0:T(8,128)} %reshape.694, f32[]{:T(128)} %constant.59.clone.1), kind=kCustom, calls=%fused_computation.90 | custom fusion | flops 1396736 | bytes 4198912 | tf_op jit(solution)/shard_map/scatter-add | solution.py:299
  606.3 48.4 %reduce-scatter.19.cloned.1.call-done = bf16[128,1024]{1,0:T(8,128)(2,1)} async-done(((bf16[1024,1024]{1,0:T(8,128)(2,1)}), bf16[128,1024]{1,0:T(8,128)(2,1)}) %reduce-scatter.19.cloned.1.call-update) | async-done | bytes 262160 | tf_op jit(solution)/shard_map/reduce_scatter | solution.py:308
  680.4 30.0 %all-gather.21.cloned.1.call-done = bf16[1024,1024]{1,0:T(8,128)(2,1)} async-done(((bf16[128,1024]{1,0:T(8,128)(2,1)}), bf16[1024,1024]{1,0:T(8,128)(2,1)}) %all-gather.21.cloned.1.call-update) | async-done | bytes 2097168 | tf_op jit(solution)/shard_map/all_gather | solution.py:328
  713.3 54.7 %while.28 = (s32[]{:T(128)}, f32[1024,1,64]{0,2,1:T(8,128)}, f32[1024,1,64]{0,2,1:T(8,128)}, f32[2,512,1,2,64]{1,0,4,3,2:T(2,128)}, s32[2]{0:T(128)}, /*index=5*...) while((s32[]{:T(128)}, f32[1024,1,64]{0,2,1:T(8,128)}, ...), condition=%wide.region_30.31_spmd.clone, body=%wide.region_28.30_spmd.clone.sunk | while | flops 688782848 | bytes 56273296 | solution.py:160
  801.5 17.7 %scatter_custom_fusion.2 = f32[1025,1024]{1,0:T(8,128)} fusion(s32[1364]{0:T(1024)} %copy-done.44, f32[1364,1024]{1,0:T(8,128)} %reshape.636, f32[1364]{0:T(1024)S(1)} %copy-done.40, f32[]{:T(128)} %constant.59.clone.1), kind=kCustom, calls=%fused_computation.75 | custom fusion | flops 2793472 | bytes 9807696 | tf_op jit(solution)/shard_map/scatter-add | solution.py:261
  823.3 37.1 %all-reduce.11.cloned.1.call-done = f32[1024,32]{1,0:T(8,128)} async-done(((f32[1024,32]{1,0:T(8,128)}), f32[1024,32]{1,0:T(8,128)}) %all-reduce.11.cloned.1.call-update) | async-done | bytes 131088
  861.6 82.5 %reduce-scatter.35.cloned.1.call-done = bf16[4,512,64]{1,2,0:T(8,128)(2,1)} async-done(((bf16[4,512,1024]{1,2,0:T(8,128)(2,1)}), bf16[4,512,64]{1,2,0:T(8,128)(2,1)}) %reduce-scatter.35.cloned.1.call-update) | async-done | bytes 262160 | tf_op jit(solution)/shard_map/reduce_scatter | solution.py:393
  945.9 82.2 %reduce-scatter.31.cloned.1.call-done = bf16[4,64,512]{2,1,0:T(8,128)(2,1)} async-done(((bf16[4,1024,512]{2,1,0:T(8,128)(2,1)}), bf16[4,64,512]{2,1,0:T(8,128)(2,1)}) %reduce-scatter.31.cloned.1.call-update) | async-done | bytes 262160 | tf_op jit(solution)/shard_map/reduce_scatter | solution.py:387
  1030.0 81.5 %reduce-scatter.33.cloned.1.call-done = bf16[4,64,512]{2,1,0:T(8,128)(2,1)} async-done(((bf16[4,1024,512]{2,1,0:T(8,128)(2,1)}), bf16[4,64,512]{2,1,0:T(8,128)(2,1)}) %reduce-scatter.33.cloned.1.call-update) | async-done | bytes 262160 | tf_op jit(solution)/shard_map/reduce_scatter | solution.py:390
  1113.3 66.1 %reduce-scatter.25.cloned.1.call-done = bf16[64,64]{1,0:T(8,128)(2,1)} async-done(((bf16[1024,64]{1,0:T(8,128)(2,1)}), bf16[64,64]{1,0:T(8,128)(2,1)}) %reduce-scatter.25.cloned.1.call-update) | async-done | bytes 8208 | tf_op jit(solution)/shard_map/reduce_scatter | solution.py:376
  1180.7 66.9 %reduce-scatter.27.cloned.1.call-done = bf16[64,64]{1,0:T(8,128)(2,1)} async-done(((bf16[1024,64]{1,0:T(8,128)(2,1)}), bf16[64,64]{1,0:T(8,128)(2,1)}) %reduce-scatter.27.cloned.1.call-update) | async-done | bytes 8208 | tf_op jit(solution)/shard_map/reduce_scatter | solution.py:379
  1248.9 66.9 %reduce-scatter.29.cloned.1.call-done = bf16[128,64]{0,1:T(8,128)(2,1)} async-done(((bf16[128,1024]{0,1:T(8,128)(2,1)}), bf16[128,64]{0,1:T(8,128)(2,1)}) %reduce-scatter.29.cloned.1.call-update) | async-done | bytes 16400 | tf_op jit(solution)/shard_map/reduce_scatter | solution.py:382
  1317.1 67.4 %reduce-scatter.23.cloned.1.call-done = bf16[64,128]{1,0:T(8,128)(2,1)} async-done(((bf16[1024,128]{1,0:T(8,128)(2,1)}), bf16[64,128]{1,0:T(8,128)(2,1)}) %reduce-scatter.23.cloned.1.call-update) | async-done | bytes 16400 | tf_op jit(solution)/shard_map/reduce_scatter | solution.py:373
  1385.9 52.7 %reduce-scatter.21.cloned.1.call-done = bf16[128,1024]{1,0:T(8,128)(2,1)} async-done(((bf16[1024,1024]{1,0:T(8,128)(2,1)}), bf16[128,1024]{1,0:T(8,128)(2,1)}) %reduce-scatter.21.cloned.1.call-update) | async-done | bytes 262160 | tf_op jit(solution)/shard_map/reduce_scatter | solution.py:352
  1439.8 65.8 %all-reduce.7 = (f32[1024]{0:T(1024)S(1)}, f32[1024]{0:T(1024)S(1)}) all-reduce(f32[1024]{0:T(1024)S(1)} %get-tuple-element.157, f32[1024]{0:T(1024)S(1)} %get-tuple-element.155), channel_id=7, replica_groups=mesh['fsdp'=16,'tp'=8] {'fsdp','tp'}, use_global_device_ids=true, to_apply=%region_34.35.clone | all-reduce | flops 2048 | bytes 16384
  (327 shorter events, 243.9 us)
Async XLA Ops:
  7.2 133.6 %all-gather.9.cloned.1.call-start = ((), (), s32[]{:S(2)}) async-start(), calls=%async_computation.12 | async-start | bytes 2359296 | tf_op jit(solution)/shard_map/all_gather | solution.py:196
  53.4 202.5 %reduce-scatter.15.cloned.1.call-start = ((), (), s32[]{:S(2)}) async-start(), calls=%async_computation.13 | async-start | bytes 4718592 | tf_op jit(solution)/shard_map/reduce_scatter | solution.py:217
  74.8 71.9 %copy-start.21 = (bf16[1024,64]{1,0:T(8,128)(2,1)}, bf16[1024,64]{1,0:T(8,128)(2,1)S(1)}, u32[]{:S(2)}) copy-start(bf16[1024,64]{1,0:T(8,128)(2,1)S(1)} %all_gather.45) | copy-start | bytes 393220
  97.4 50.2 %copy-start.19 = (bf16[1024,64]{1,0:T(8,128)(2,1)}, bf16[1024,64]{1,0:T(8,128)(2,1)S(1)}, u32[]{:S(2)}) copy-start(bf16[1024,64]{1,0:T(8,128)(2,1)S(1)} %all_gather.46) | copy-start | bytes 393220
  164.2 91.7 %copy-start.6 = (bf16[128,1024]{1,0:T(8,128)(2,1)S(1)}, bf16[128,1024]{1,0:T(8,128)(2,1)}, u32[]{:S(2)}) copy-start(bf16[128,1024]{1,0:T(8,128)(2,1)} %param.18) | copy-start | bytes 786436
  166.9 93.1 %copy-start.36 = (s32[1024,8]{0,1:T(8,128)S(1)}, s32[1024,8]{0,1:T(8,128)}, u32[]{:S(2)}) copy-start(s32[1024,8]{0,1:T(8,128)} %param.20) | copy-start | bytes 98308
  166.9 93.8 %copy-start.46 = (bf16[64,32]{0,1:T(8,128)(2,1)S(1)}, bf16[64,32]{0,1:T(8,128)(2,1)}, u32[]{:S(2)}) copy-start(bf16[64,32]{0,1:T(8,128)(2,1)} %param.27) | copy-start | bytes 12292
  167.0 192.5 %all-gather.19.cloned.1.call-start = ((), (), s32[]{:S(2)}) async-start(), calls=%async_computation.19 | async-start | bytes 2359296 | tf_op jit(solution)/shard_map/all_gather | solution.py:267
  167.7 204.1 %all-gather.11.cloned.1.call-start = ((), (), s32[]{:S(2)}) async-start(), calls=%async_computation.14 | async-start | bytes 2359296 | tf_op jit(solution)/shard_map/all_gather | solution.py:234
  258.0 162.6 %all-gather.13.cloned.1.call-start = ((), (), s32[]{:S(2)}) async-start(), calls=%async_computation.15 | async-start | bytes 4456448 | tf_op jit(solution)/shard_map/all_gather | solution.py:227
  258.6 217.6 %all-gather.15.cloned.1.call-start = ((), (), s32[]{:S(2)}) async-start(), calls=%async_computation.16 | async-start | bytes 4456448 | tf_op jit(solution)/shard_map/all_gather | solution.py:228
  259.2 272.8 %all-gather.17.cloned.1.call-start = ((), (), s32[]{:S(2)}) async-start(), calls=%async_computation.17 | async-start | bytes 4456448 | tf_op jit(solution)/shard_map/all_gather | solution.py:229
  259.9 342.8 %reduce-scatter.37.cloned.1.call-start = ((), (), s32[]{:S(2)}) async-start(), calls=%async_computation.30 | async-start | bytes 294912
  565.9 88.8 %reduce-scatter.19.cloned.1.call-start = ((), (), s32[]{:S(2)}) async-start(), calls=%async_computation.20 | async-start | bytes 2359296 | tf_op jit(solution)/shard_map/reduce_scatter | solution.py:308
  601.0 109.3 %all-gather.21.cloned.1.call-start = ((), (), s32[]{:S(2)}) async-start(), calls=%async_computation.21 | async-start | bytes 2359296 | tf_op jit(solution)/shard_map/all_gather | solution.py:328
  658.8 201.6 %all-reduce.11.cloned.1.call-start = ((), (), s32[]{:S(2)}) async-start(), calls=%async_computation.31 | async-start | bytes 1048576
  660.8 283.3 %reduce-scatter.35.cloned.1.call-start = ((), (), s32[]{:S(2)}) async-start(), calls=%async_computation.29 | async-start | bytes 4456448 | tf_op jit(solution)/shard_map/reduce_scatter | solution.py:393
  668.4 359.7 %reduce-scatter.31.cloned.1.call-start = ((), (), s32[]{:S(2)}) async-start(), calls=%async_computation.27 | async-start | bytes 4456448 | tf_op jit(solution)/shard_map/reduce_scatter | solution.py:387
  674.2 437.2 %reduce-scatter.33.cloned.1.call-start = ((), (), s32[]{:S(2)}) async-start(), calls=%async_computation.28 | async-start | bytes 4456448 | tf_op jit(solution)/shard_map/reduce_scatter | solution.py:390
  680.1 499.3 %reduce-scatter.25.cloned.1.call-start = ((), (), s32[]{:S(2)}) async-start(), calls=%async_computation.24 | async-start | bytes 278528 | tf_op jit(solution)/shard_map/reduce_scatter | solution.py:376
  780.5 467.1 %reduce-scatter.27.cloned.1.call-start = ((), (), s32[]{:S(2)}) async-start(), calls=%async_computation.25 | async-start | bytes 278528 | tf_op jit(solution)/shard_map/reduce_scatter | solution.py:379
  782.1 533.7 %reduce-scatter.29.cloned.1.call-start = ((), (), s32[]{:S(2)}) async-start(), calls=%async_computation.26 | async-start | bytes 278528 | tf_op jit(solution)/shard_map/reduce_scatter | solution.py:382
  785.4 599.2 %reduce-scatter.23.cloned.1.call-start = ((), (), s32[]{:S(2)}) async-start(), calls=%async_computation.23 | async-start | bytes 278528 | tf_op jit(solution)/shard_map/reduce_scatter | solution.py:373
  790.0 648.6 %reduce-scatter.21.cloned.1.call-start = ((), (), s32[]{:S(2)}) async-start(), calls=%async_computation.22 | async-start | bytes 2359296 | tf_op jit(solution)/shard_map/reduce_scatter | solution.py:352
  795.7 711.0 %reduce-scatter.17.cloned.1.call-start = ((), (), s32[]{:S(2)}) async-start(), calls=%async_computation.18 | async-start | bytes 2359296 | tf_op jit(solution)/shard_map/reduce_scatter | solution.py:263
  819.3 619.3 %copy-start.7 = (bf16[128,1024]{1,0:T(8,128)(2,1)S(1)}, bf16[128,1024]{1,0:T(8,128)(2,1)}, u32[]{:S(2)}) copy-start(bf16[128,1024]{1,0:T(8,128)(2,1)} %param.18) | copy-start | bytes 786436
  819.3 619.3 %copy-start.42 = (f32[1024]{0:T(1024)S(1)}, f32[1024]{0:T(1024)}, u32[]{:S(2)}) copy-start(f32[1024]{0:T(1024)} %copy-done.41) | copy-start | bytes 12292
  819.3 619.3 %copy-start.50 = (f32[128]{0:T(128)S(1)}, f32[128]{0:T(128)}, u32[]{:S(2)}) copy-start(f32[128]{0:T(128)} %copy-done.49) | copy-start | bytes 1540
  819.3 687.5 %copy-start.14 = (f32[128,1024]{1,0:T(8,128)S(1)}, f32[128,1024]{1,0:T(8,128)}, u32[]{:S(2)}) copy-start(f32[128,1024]{1,0:T(8,128)} %copy-done.13) | copy-start | bytes 1572868
  819.3 687.5 %copy-start.30 = (bf16[128,1024]{1,0:T(8,128)(2,1)S(1)}, bf16[128,1024]{1,0:T(8,128)(2,1)}, u32[]{:S(2)}) copy-start(bf16[128,1024]{1,0:T(8,128)(2,1)} %param.31) | copy-start | bytes 786436
  819.3 687.5 %copy-start.48 = (f32[128]{0:T(128)S(1)}, f32[128]{0:T(128)}, u32[]{:S(2)}) copy-start(f32[128]{0:T(128)} %copy-done.47) | copy-start | bytes 1540
  819.3 687.5 %copy-start.52 = (f32[128]{0:T(128)S(1)}, f32[128]{0:T(128)}, u32[]{:S(2)}) copy-start(f32[128]{0:T(128)} %copy-done.51) | copy-start | bytes 1540
  (45 other events, 348.9 us)
Sparse Core Ops, SparseCore 0:
  53.5 50.7 all-gather.8
  167.1 88.8 reduce-scatter.14
  257.6 52.3 all-gather.18
  312.1 51.4 all-gather.10
  365.9 54.6 all-gather.12
  423.0 53.1 all-gather.14
  478.8 53.1 all-gather.16
  566.1 35.0 reduce-scatter.36
  603.7 50.9 reduce-scatter.18
  658.9 51.4 all-gather.20
  716.4 143.9 all-reduce.10
  864.2 79.8 reduce-scatter.34
  948.7 79.4 reduce-scatter.30
  1032.0 79.3 reduce-scatter.32
  1115.4 63.9 reduce-scatter.24
  1183.4 64.1 reduce-scatter.26
  1251.6 64.2 reduce-scatter.28
  1320.4 64.1 reduce-scatter.22
  1387.1 51.4 reduce-scatter.20
  1441.0 52.2 reduce-scatter.16
where the time goes:
time: 1530 us; the launch traced here: 1520 us
  waiting for transfers between devices  900 us (59%)
  blocking collectives  215 us (14%)
  local copies, waits for them, and re-layouts  149 us (10%)
  matrix products  127 us (8%)
  other arithmetic  98.2 us (6%)
  between operations  16 us (1%)
    unnamed x2, blocking collectives  105 us
    reduce_scatter x1, waiting for transfers between devices, per_device(): lax.psum_scatter(jnp.dot(mixed_low, output_all, preferred_element_type=jn...  88.2 us
    reduce_scatter x1, waiting for transfers between devices, per_device(): lax.psum_scatter(down_grad_part.astype(jnp.bfloat16), 'fsdp', scatter_dim...  82.5 us
    reduce_scatter x1, waiting for transfers between devices, per_device(): lax.psum_scatter(gate_grad_part.astype(jnp.bfloat16), 'fsdp', scatter_dim...  82.2 us
    reduce_scatter x1, waiting for transfers between devices, per_device(): lax.psum_scatter(up_grad_part.astype(jnp.bfloat16), 'fsdp', scatter_dimen...  81.5 us
    reduce_scatter x1, waiting for transfers between devices, per_device(): lax.psum_scatter(query_grad_part.astype(jnp.bfloat16), 'fsdp', scatter_di...  67.4 us
    reduce_scatter x1, waiting for transfers between devices, per_device(): lax.psum_scatter(output_grad_part.astype(jnp.bfloat16), 'fsdp', scatter_d...  66.9 us
    reduce_scatter x1, waiting for transfers between devices, per_device(): lax.psum_scatter(value_grad_part.astype(jnp.bfloat16), 'fsdp', scatter_di...  66.9 us
  transfers between devices with their start and end apart: 20, of which 15 were waited for; matrix products, arithmetic and copies ran while one was open for 20% of the time, Pallas kernels for 0%

commit v1 on v0

v1 whole, which is shorter than its diff:
```python
import functools

import jax
import jax.numpy as jnp
from jax import lax
from jax.experimental import pallas as pl
from jax.experimental.pallas import tpu as pltpu
from jax.sharding import PartitionSpec as P

MESH = pl.DeviceIdType.MESH
D = 1024
HEAD_DIM = 64
EXPERTS = 32
HIDDEN = 512
GROUP = 1024
SEQS = 3
ROWS = 128
SLOTS = 352
LOCAL = 4
BLOCK = 64
WIDE = D + 128

eps_norm = 1e-06
rope_base = 10000.0
score_scale = 1.0 / HEAD_DIM
F32 = jnp.float32
BF16 = jnp.bfloat16
TP_STEPS = ((2, 0), (2, 1), (1, 1), (3, 1), (1, 0), (3, 0), (0, 1))
CHIP_STEPS = ((1, 2), (0, 2), (1, 1), (1, 3), (0, 1), (0, 3), (1, 0))


def tp_peer(step):
    tp = lax.axis_index("tp")
    along_y, along_x = step
    return lax.rem(tp // 2 + along_y, 4) * 2 + lax.rem(tp + along_x, 2)


def chip_at(step):
    chip = lax.axis_index("fsdp") // 2
    along_x, along_z = step
    return lax.rem(chip // 4 + along_x, 2) * 4 + lax.rem(chip + along_z, 4)


def own_core():
    return lax.rem(lax.axis_index("fsdp"), 2)


def core_partner():
    return (lax.axis_index("fsdp") // 2) * 2 + 1 - own_core()


def send(src, dst, send_sem, recv_sem, device):
    copy = pltpu.make_async_remote_copy(
        src_ref=src,
        dst_ref=dst,
        send_sem=send_sem,
        recv_sem=recv_sem,
        device_id=device,
        device_id_type=MESH,
    )
    copy.start()
    return copy


def greet():
    barrier = pltpu.get_barrier_semaphore()
    for step in TP_STEPS:
        pl.semaphore_signal(barrier, inc=1, device_id={"tp": tp_peer(step)}, device_id_type=MESH)
    for step in CHIP_STEPS:
        pl.semaphore_signal(
            barrier,
            inc=1,
            device_id={"fsdp": chip_at(step) * 2 + own_core()},
            device_id_type=MESH,
        )
    pl.semaphore_signal(barrier, inc=1, device_id={"fsdp": core_partner()}, device_id_type=MESH)
    pl.semaphore_wait(barrier, 15)


class GatherTp:
    def __init__(self, rows, columns):
        self.rows = rows
        self.out = jax.ShapeDtypeStruct((8 * rows, columns), BF16)
        self.out_space = pltpu.VMEM
        self.scratch = [pltpu.SemaphoreType.DMA((7,)), pltpu.SemaphoreType.DMA((7,)), pltpu.SemaphoreType.DMA(())]

    def start(self, src, out, send_sem, recv_sem, own_sem):
        here = out.at[pl.ds(pl.multiple_of(lax.axis_index("tp") * self.rows, self.rows), self.rows)]
        self.copies = [
            send(src, here, send_sem.at[k], recv_sem.at[k], {"tp": tp_peer(step)})
            for k, step in enumerate(TP_STEPS)
        ]
        self.own = pltpu.make_async_copy(src, here, own_sem)
        self.own.start()

    def progress(self, k):
        pass

    def finish(self):
        for copy in self.copies:
            copy.wait()
        self.own.wait()


class SumTp:
    def __init__(self, rows, columns):
        self.rows = rows
        self.out = jax.ShapeDtypeStruct((rows, columns), F32)
        self.out_space = pltpu.VMEM
        self.scratch = [
            pltpu.SemaphoreType.DMA((7,)),
            pltpu.SemaphoreType.DMA((7,)),
            pltpu.VMEM((7, rows, columns), BF16),
        ]

    def start(self, src, out, send_sem, recv_sem, landed):
        self.src, self.out_ref, self.landed = src, out, landed
        self.copies = []
        for k, step in enumerate(TP_STEPS):
            peer = tp_peer(step)
            part = src.at[pl.ds(pl.multiple_of(peer * self.rows, self.rows), self.rows)]
            self.copies.append(send(part, landed.at[k], send_sem.at[k], recv_sem.at[k], {"tp": peer}))

    def progress(self, k):
        pass

    def finish(self):
        for copy in self.copies:
            copy.wait()
        first = lax.axis_index("tp") * self.rows

        @pl.loop(0, self.rows // 16)
        def _(i):
            at = pl.multiple_of(i * 16, 16)
            total = self.src[pl.ds(pl.multiple_of(first + at, 16), 16), :].astype(F32)
            for k in range(7):
                total = total + self.landed[k, pl.ds(at, 16), :].astype(F32)
            self.out_ref[pl.ds(at, 16), :] = total


class GatherFsdp:
    def __init__(self, experts, columns):
        self.out = jax.ShapeDtypeStruct((experts, D, columns), BF16)
        self.out_space = pl.ANY
        self.scratch = [pltpu.SemaphoreType.DMA((7,)), pltpu.SemaphoreType.DMA((7,)), pltpu.SemaphoreType.DMA((8,)), pltpu.SemaphoreType.DMA((8,)), pltpu.SemaphoreType.DMA(())]

    def block(self, fsdp):
        return self.out_ref.at[:, pl.ds(pl.multiple_of(fsdp * BLOCK, BLOCK), BLOCK)]

    def start(self, src, out, send_sem, recv_sem, core_send, core_recv, own_sem):
        self.out_ref, self.core_send, self.core_recv = out, core_send, core_recv
        here = self.block(lax.axis_index("fsdp"))
        self.copies = [
            send(src, here, send_sem.at[k], recv_sem.at[k], {"fsdp": chip_at(step) * 2 + own_core()})
            for k, step in enumerate(CHIP_STEPS)
        ]
        self.across = [send(src, here, core_send.at[7], core_recv.at[7], {"fsdp": core_partner()})]
        self.own = pltpu.make_async_copy(src, here, own_sem)
        self.own.start()

    def progress(self, k):
        if k == 7:
            return
        along_x, along_z = CHIP_STEPS[k]
        self.copies[k].wait_recv()
        block = self.block(chip_at((along_x, (4 - along_z) % 4)) * 2 + own_core())
        self.across.append(
            send(block, block, self.core_send.at[k], self.core_recv.at[k], {"fsdp": core_partner()})
        )

    def finish(self):
        for copy in self.copies:
            copy.wait_send()
        for copy in self.across:
            copy.wait()
        self.own.wait()


class SumFsdp:
    def __init__(self, experts, columns, dtype=BF16):
        self.experts = experts
        self.out = jax.ShapeDtypeStruct((experts, BLOCK, columns), F32)
        self.out_space = pltpu.VMEM
        self.scratch = [
            pltpu.SemaphoreType.DMA((7,)),
            pltpu.SemaphoreType.DMA((7,)),
            pltpu.SemaphoreType.DMA((8,)),
            pltpu.SemaphoreType.DMA((8,)),
            pltpu.VMEM((8, experts, BLOCK, columns), dtype),
            pltpu.VMEM((7, experts, BLOCK, columns), dtype),
        ]

    def start(self, src, out, send_sem, recv_sem, core_send, core_recv, pair, landed):
        self.src, self.out_ref, self.pair, self.landed = src, out, pair, landed
        self.send_sem, self.recv_sem = send_sem, recv_sem
        self.across, self.copies = [], []
        for k, step in enumerate(CHIP_STEPS + ((0, 0),)):
            first = (chip_at(step) * 2 + 1 - own_core()) * BLOCK
            part = src.at[:, pl.ds(pl.multiple_of(first, BLOCK), BLOCK)]
            self.across.append(
                send(part, pair.at[k], core_send.at[k], core_recv.at[k], {"fsdp": core_partner()})
            )

    def progress(self, k):
        self.across[k].wait_recv()
        step = (CHIP_STEPS + ((0, 0),))[k]
        owner = chip_at(step) * 2 + own_core()

        @pl.loop(0, self.experts * (BLOCK // 16))
        def _(i):
            expert = i // (BLOCK // 16)
            at = pl.multiple_of(lax.rem(i, BLOCK // 16) * 16, 16)
            mine = self.src[expert, pl.ds(pl.multiple_of(owner * BLOCK + at, 16), 16), :].astype(F32)
            total = mine + self.pair[k, expert, pl.ds(at, 16), :].astype(F32)
            self.pair[k, expert, pl.ds(at, 16), :] = total.astype(self.pair.dtype)

        if k < 7:
            self.copies.append(
                send(self.pair.at[k], self.landed.at[k], self.send_sem.at[k], self.recv_sem.at[k], {"fsdp": owner})
            )

    def finish(self):
        for copy in self.across:
            copy.wait_send()
        for copy in self.copies:
            copy.wait()

        @pl.loop(0, self.experts * (BLOCK // 16))
        def _(i):
            expert = i // (BLOCK // 16)
            at = pl.multiple_of(lax.rem(i, BLOCK // 16) * 16, 16)
            total = self.pair[7, expert, pl.ds(at, 16), :].astype(F32)
            for k in range(7):
                total = total + self.landed[k, expert, pl.ds(at, 16), :].astype(F32)
            self.out_ref[expert, pl.ds(at, 16), :] = total


class SumAll:
    def __init__(self, columns):
        self.over_fsdp = SumFsdp(1, columns, F32)
        self.out = jax.ShapeDtypeStruct((8, columns), F32)
        self.out_space = pltpu.VMEM
        self.scratch = self.over_fsdp.scratch + [
            pltpu.VMEM((1, BLOCK, columns), F32),
            pltpu.SemaphoreType.DMA((7,)),
            pltpu.SemaphoreType.DMA((7,)),
            pltpu.VMEM((7, 8, columns), F32),
        ]

    def start(self, src, out, *scratch):
        self.out_ref = out
        self.total, self.send_sem, self.recv_sem, self.landed = scratch[-4:]
        self.over_fsdp.start(src, self.total, *scratch[:-4])

    def progress(self, k):
        self.over_fsdp.progress(k)

    def middle(self):
        self.over_fsdp.finish()
        self.copies = []
        for k, step in enumerate(TP_STEPS):
            peer = tp_peer(step)
            part = self.total.at[0, pl.ds(pl.multiple_of(peer * 8, 8), 8)]
            self.copies.append(
                send(part, self.landed.at[k], self.send_sem.at[k], self.recv_sem.at[k], {"tp": peer})
            )

    def finish(self):
        for copy in self.copies:
            copy.wait()
        total = self.total[0, pl.ds(pl.multiple_of(lax.axis_index("tp") * 8, 8), 8), :]
        for k in range(7):
            total = total + self.landed[k]
        self.out_ref[...] = total


def exchange(name, number, tasks, arrays):
    n = len(tasks)
    counts = [len(task.scratch) for task in tasks]

    def body(*refs):
        sources, outs, scratch = refs[:n], refs[n : 2 * n], list(refs[2 * n :])
        greet()
        for task, source, out, count in zip(tasks, sources, outs, counts):
            task.start(source, out, *scratch[:count])
            scratch = scratch[count:]
        for k in range(8):
            for task in tasks:
                task.progress(k)
        for task in tasks:
            if isinstance(task, SumAll):
                task.middle()
        for task in tasks:
            task.finish()

    return pl.pallas_call(
        body,
        name=name,
        out_shape=[task.out for task in tasks],
        in_specs=[pl.BlockSpec(memory_space=pltpu.VMEM)] * n,
        out_specs=[pl.BlockSpec(memory_space=task.out_space) for task in tasks],
        scratch_shapes=[shape for task in tasks for shape in task.scratch],
        compiler_params=pltpu.CompilerParams(
            collective_id=number, has_side_effects=True, vmem_limit_bytes=48 * 2**20
        ),
    )(*arrays)


def dot(a, b, dims=((1,), (0,))):
    return lax.dot_general(a, b, (dims, ((), ())), preferred_element_type=F32)


def lanes(rows):
    return lax.broadcasted_iota(jnp.int32, (rows, 128), 1)


def turn(values):
    low_half = lax.rem(lanes(values.shape[0]), HEAD_DIM) < HEAD_DIM // 2
    return jnp.where(low_half, pltpu.roll(values, 96, 1), pltpu.roll(values, 32, 1))


def both_halves(pair):
    low = lanes(pair.shape[0]) < HEAD_DIM
    other = pltpu.roll(pair, HEAD_DIM, 1)
    return jnp.where(low, pair, other), jnp.where(low, other, pair)


def head_lanes(values, head):
    return jnp.where(lanes(values.shape[0]) // HEAD_DIM == head, values, 0.0)


def allowed(keys, first, queries, doc_column, doc_row):
    key_at = lax.broadcasted_iota(jnp.int32, (keys, queries), 0)
    query_at = first + lax.broadcasted_iota(jnp.int32, (keys, queries), 1)
    return (key_at <= query_at) & (doc_column[:keys, :] == doc_row[:, first : first + queries])


def unit_rows(values):
    return values * lax.rsqrt(jnp.mean(values * values, axis=-1, keepdims=True) + eps_norm)


QUERIES = 256


def attention_body(
    x_ref, w_ref, gain_ref, cos_q, sin_q, cos_k, sin_k, doc_column, doc_row,
    normed_ref, query_ref, pair_ref, lse_ref, mixed_ref, attended_ref, mixed_t,
):
    @pl.loop(0, GROUP // 128)
    def _(i):
        rows = pl.ds(pl.multiple_of(i * 128, 128), 128)
        normed = (unit_rows(x_ref[rows, :].astype(F32)) * gain_ref[...]).astype(BF16)
        normed_ref[rows, :] = normed
        raw = dot(normed, w_ref[:, 0:256])
        query, pair = raw[:, 0:128], raw[:, 128:256]
        query_ref[rows, :] = (query * cos_q[rows, :] + turn(query) * sin_q[rows, :]).astype(BF16)
        pair_ref[rows, :] = (pair * cos_k[rows, :] + turn(pair) * sin_k[rows, :]).astype(BF16)

    keys, values = both_halves(pair_ref[...].astype(F32))
    keys, values_t = keys.astype(BF16), values.T.astype(BF16)

    for first in range(0, GROUP, QUERIES):
        count = first + QUERIES
        mask = allowed(count, first, QUERIES, doc_column, doc_row)
        parts = []
        for head in range(2):
            query = head_lanes(query_ref[first : first + QUERIES, :].astype(F32), head).astype(BF16)
            scores = dot(keys[:count], query, ((1,), (1,))) * score_scale
            scores = jnp.where(mask, scores, -1e30)
            top = jnp.max(scores, axis=0, keepdims=True)
            raised = jnp.exp(scores - top)
            total = jnp.sum(raised, axis=0, keepdims=True)
            lse_ref[head : head + 1, first : first + QUERIES] = top + jnp.log(total)
            weights = (raised * (1.0 / total)).astype(BF16)
            parts.append(dot(values_t[HEAD_DIM * head : HEAD_DIM * (head + 1), :count], weights))
        for head in range(2):
            mixed_t[HEAD_DIM * head : HEAD_DIM * (head + 1), first : first + QUERIES] = parts[head]
    mixed_ref[...] = mixed_t[...].astype(BF16)

    @pl.loop(0, GROUP // 128)
    def _(i):
        at = pl.multiple_of(i * 128, 128)
        mixed = mixed_t[:, pl.ds(at, 128)].T.astype(BF16)
        attended_ref[pl.ds(at, 128), :] = dot(mixed, w_ref[:, 256:384], ((1,), (1,))).astype(BF16)


def attention(x, w, gain, tables, doc_column, doc_row):
    return pl.pallas_call(
        attention_body,
        name="attention",
        out_shape=[
            jax.ShapeDtypeStruct((GROUP, D), BF16),
            jax.ShapeDtypeStruct((GROUP, 128), BF16),
            jax.ShapeDtypeStruct((GROUP, 128), BF16),
            jax.ShapeDtypeStruct((2, GROUP), F32),
            jax.ShapeDtypeStruct((128, GROUP), BF16),
            jax.ShapeDtypeStruct((GROUP, D), BF16),
        ],
        scratch_shapes=[pltpu.VMEM((128, GROUP), F32)],
        compiler_params=pltpu.CompilerParams(vmem_limit_bytes=48 * 2**20),
    )(x, w, gain, *tables, doc_column, doc_row)


def attention_back_body(
    datt_ref, x_ref, normed_ref, w_ref, query_ref, pair_ref, lse_ref, mixed_ref,
    cos_q, sin_q, cos_k, sin_k, doc_column, doc_row,
    grad_ref, weights_ref, gain_ref, dmixed_ref, dquery_t, dpair_ref, raw_ref, raw_t,
):
    @pl.loop(0, GROUP // 128)
    def _(i):
        rows = pl.ds(pl.multiple_of(i * 128, 128), 128)
        dmixed_ref[rows, :] = dot(datt_ref[rows, :], w_ref[:, 256:384]).astype(BF16)

    keys, values = both_halves(pair_ref[...].astype(F32))
    keys_t = keys.T.astype(BF16)
    keys, values = keys.astype(BF16), values.astype(BF16)
    dpair_ref[...] = jnp.zeros_like(dpair_ref)

    for first in range(0, GROUP, QUERIES):
        count = first + QUERIES
        mask = allowed(count, first, QUERIES, doc_column, doc_row)
        for head in range(2):
            query = head_lanes(query_ref[first : first + QUERIES, :].astype(F32), head).astype(BF16)
            dmixed = head_lanes(dmixed_ref[first : first + QUERIES, :].astype(F32), head).astype(BF16)
            scores = dot(keys[:count], query, ((1,), (1,))) * score_scale
            scores = jnp.where(mask, scores, -1e30)
            weights = jnp.exp(scores - lse_ref[head : head + 1, first : first + QUERIES])
            dweights = dot(values[:count], dmixed, ((1,), (1,)))
            inner = jnp.sum(weights * dweights, axis=0, keepdims=True)
            dscores = (weights * (dweights - inner)).astype(BF16)
            dquery_t[HEAD_DIM * head : HEAD_DIM * (head + 1), first : first + QUERIES] = (
                dot(keys_t[HEAD_DIM * head : HEAD_DIM * (head + 1), :count], dscores) * score_scale
            )
            dpair_ref[0, :count, :] += dot(dscores, query) * score_scale
            dpair_ref[1, :count, :] += dot(weights.astype(BF16), dmixed)

    gain_ref[...] = jnp.zeros_like(gain_ref)

    @pl.loop(0, GROUP // 128)
    def _(i):
        at = pl.multiple_of(i * 128, 128)
        rows = pl.ds(at, 128)
        dquery = dquery_t[:, rows].T
        dkey, dvalue = dpair_ref[0, rows, :], dpair_ref[1, rows, :]
        dkey = dkey + pltpu.roll(dkey, HEAD_DIM, 1)
        dvalue = dvalue + pltpu.roll(dvalue, HEAD_DIM, 1)
        dpair = jnp.where(lanes(128) < HEAD_DIM, dkey, dvalue)
        dquery = dquery * cos_q[rows, :] + turn(dquery * sin_q[rows, :])
        dpair = dpair * cos_k[rows, :] + turn(dpair * sin_k[rows, :])
        raw_ref[rows, 0:128] = dquery.astype(BF16)
        raw_ref[rows, 128:256] = dpair.astype(BF16)
        raw_t[0:128, rows] = dquery.T.astype(BF16)
        raw_t[128:256, rows] = dpair.T.astype(BF16)
        dnormed = dot(raw_ref[rows, :], w_ref[:, 0:256], ((1,), (1,)))
        grad_ref[rows, :] = dnormed.astype(BF16)
        unit = unit_rows(x_ref[rows, :].astype(F32))
        gain_ref[...] += jnp.sum(dnormed * unit, axis=0, keepdims=True)

    @pl.loop(0, D // 256)
    def _(i):
        at = pl.ds(pl.multiple_of(i * 256, 256), 256)
        weights_ref[at, 0:256] = dot(raw_t[...], normed_ref[:, at]).T.astype(BF16)
        weights_ref[at, 256:384] = dot(mixed_ref[...], datt_ref[:, at]).T.astype(BF16)


def attention_back(datt, x, normed, w, query, pair, lse, mixed, tables, doc_column, doc_row):
    return pl.pallas_call(
        attention_back_body,
        name="attention_back",
        out_shape=[
            jax.ShapeDtypeStruct((GROUP, D), BF16),
            jax.ShapeDtypeStruct((D, 384), BF16),
            jax.ShapeDtypeStruct((1, D), F32),
        ],
        scratch_shapes=[
            pltpu.VMEM((GROUP, 128), BF16),
            pltpu.VMEM((128, GROUP), F32),
            pltpu.VMEM((2, GROUP, 128), F32),
            pltpu.VMEM((GROUP, 256), BF16),
            pltpu.VMEM((256, GROUP), BF16),
        ],
        compiler_params=pltpu.CompilerParams(vmem_limit_bytes=48 * 2**20),
    )(datt, x, normed, w, query, pair, lse, mixed, *tables, doc_column, doc_row)


def experts_body(
    tp_ref, tokens_ref, dy_ref, router_ref, chosen_ref, rank_row, rank_column,
    gate_ref, up_ref, down_ref,
    combined_ref, grad_ref, gate_grad, up_grad, down_grad, combined_sum, grad_sum, gate_sum, gates_ref,
):
    step = pl.program_id(0)
    lane = lax.broadcasted_iota(jnp.int32, (1, 128), 1)

    @pl.when(step == 0)
    def _():
        combined_sum[...] = jnp.zeros_like(combined_sum)
        grad_sum[...] = jnp.zeros_like(grad_sum)
        gate_sum[...] = jnp.zeros_like(gate_sum)
        logits = jnp.where(chosen_ref[...] > 0, dot(tokens_ref[...], router_ref[...]), -1e30)
        raised = jnp.exp(logits - jnp.max(logits, axis=-1, keepdims=True))
        gates = raised / jnp.sum(raised, axis=-1, keepdims=True)
        high = gates.astype(BF16)
        gates_ref[:, 0:128] = high
        gates_ref[:, 128:256] = (gates - high.astype(F32)).astype(BF16)

    expert_lane = lane == tp_ref[0] * LOCAL + step
    slot = lax.broadcasted_iota(jnp.int32, (SLOTS, GROUP), 0)
    take = jnp.where(slot == rank_row[0], 1.0, 0.0).astype(BF16)
    slot_gates = dot(take, gates_ref[...])
    slot_gates = slot_gates[:, 0:128] + slot_gates[:, 128:256]
    slot_gate = jnp.sum(jnp.where(expert_lane, slot_gates, 0.0), axis=1, keepdims=True)
    picked = dot(take, tokens_ref[...]).astype(BF16)
    dy = dot(take, dy_ref[...]).astype(BF16)

    gate_part = dot(picked, gate_ref[0])
    up_part = dot(picked, up_ref[0])
    sigmoid = 1.0 / (1.0 + jnp.exp(-gate_part))
    silu = gate_part * sigmoid
    hidden = silu * up_part
    dhidden = dot(dy, down_ref[0])
    dgate = jnp.sum(hidden * dhidden, axis=1, keepdims=True)
    weighted = (hidden * slot_gate).astype(BF16)
    dhidden = dhidden * slot_gate
    dgate_part = (dhidden * up_part * (sigmoid * (1.0 + gate_part * (1.0 - sigmoid)))).astype(BF16)
    dup_part = (dhidden * silu).astype(BF16)

    down_grad[0] = dot(dy, weighted, ((0,), (0,))).astype(BF16)
    gate_grad[0] = dot(picked, dgate_part, ((0,), (0,))).astype(BF16)
    up_grad[0] = dot(picked, dup_part, ((0,), (0,))).astype(BF16)

    out = dot(weighted, down_ref[0], ((1,), (1,))).astype(BF16)
    dpicked = dot(dgate_part, gate_ref[0], ((1,), (1,)))
    dpicked = (dpicked + dot(dup_part, up_ref[0], ((1,), (1,)))).astype(BF16)
    dgate = jnp.where(expert_lane, dgate, 0.0).astype(BF16)

    give = jnp.where(
        lax.broadcasted_iota(jnp.int32, (GROUP, SLOTS), 1) == rank_column[0], 1.0, 0.0
    ).astype(BF16)
    combined_sum[...] += dot(give, out)
    grad_sum[...] += dot(give, dpicked)
    gate_sum[...] += dot(give, dgate)

    @pl.when(step == LOCAL - 1)
    def _():
        combined_ref[...] = combined_sum[...].astype(BF16)
        grad_ref[:, 0:D] = grad_sum[...].astype(BF16)
        grad_ref[:, D:WIDE] = gate_sum[...].astype(BF16)


def experts(tp, tokens, dy, router, chosen, rank_row, rank_column, gate, up, down):
    def whole(*shape):
        return pl.BlockSpec(shape, lambda i, tp: (0,) * len(shape))

    def own(*shape):
        return pl.BlockSpec((1,) + shape, lambda i, tp: (i,) + (0,) * len(shape))

    weight = jax.ShapeDtypeStruct((LOCAL, D, HIDDEN), BF16)
    return pl.pallas_call(
        experts_body,
        name="experts",
        grid_spec=pltpu.PrefetchScalarGridSpec(
            num_scalar_prefetch=1,
            grid=(LOCAL,),
            in_specs=[
                whole(GROUP, D),
                whole(GROUP, D),
                whole(D, 128),
                whole(GROUP, 128),
                own(1, GROUP),
                own(GROUP, 1),
                own(D, HIDDEN),
                own(D, HIDDEN),
                own(D, HIDDEN),
            ],
            out_specs=[
                whole(GROUP, D),
                whole(GROUP, WIDE),
                own(D, HIDDEN),
                own(D, HIDDEN),
                own(D, HIDDEN),
            ],
            scratch_shapes=[
                pltpu.VMEM((GROUP, D), F32),
                pltpu.VMEM((GROUP, D), F32),
                pltpu.VMEM((GROUP, 128), F32),
                pltpu.VMEM((GROUP, 256), BF16),
            ],
        ),
        out_shape=[
            jax.ShapeDtypeStruct((GROUP, D), BF16),
            jax.ShapeDtypeStruct((GROUP, WIDE), BF16),
            weight,
            weight,
            weight,
        ],
        compiler_params=pltpu.CompilerParams(vmem_limit_bytes=60 * 2**20),
    )(tp, tokens, dy, router, chosen, rank_row, rank_column, gate, up, down)


def doc_layout(lengths_row):
    seq_ends = jnp.cumsum(lengths_row)
    positions = jnp.arange(GROUP, dtype=jnp.int32)
    doc_index = jnp.sum((positions[:, None] >= seq_ends[None, :]).astype(jnp.int32), axis=1)
    starts = seq_ends - lengths_row
    match = doc_index[:, None] == jnp.arange(SEQS, dtype=jnp.int32)[None, :]
    doc_start = jnp.sum(jnp.where(match, starts[None, :], 0), axis=1)
    return (doc_index, positions - doc_start)


def rope_tables(offset):
    lane = jnp.arange(128, dtype=jnp.int32)
    frequency = rope_base ** (-(lane % 32).astype(F32) * 2.0 / HEAD_DIM)
    angles = offset.astype(F32)[:, None] * frequency[None, :]
    cosine, sine = jnp.cos(angles), jnp.sin(angles)
    sine = jnp.where(lane % 64 < 32, -sine, sine)
    key = lane < HEAD_DIM
    return (cosine, sine, jnp.where(key, cosine, 1.0), jnp.where(key, sine, 0.0))


def rms_parts(values, gain):
    inverse = lax.rsqrt(jnp.mean(values * values, axis=-1, keepdims=True) + eps_norm)
    unit = values * inverse
    return (unit * gain, unit, inverse)


def rms_back(grad_out, unit, inverse, gain):
    grad_unit = grad_out * gain
    return inverse * (grad_unit - unit * jnp.mean(grad_unit * unit, axis=-1, keepdims=True))


def per_device(
    inputs,
    lengths,
    routes,
    attn_gain,
    query_weight,
    key_weight,
    value_weight,
    output_weight,
    moe_gain,
    router_weight,
    gate_weight,
    up_weight,
    down_weight,
    cotangent,
):
    tp = lax.axis_index("tp")
    small = jnp.concatenate(
        [
            query_weight,
            key_weight,
            value_weight,
            output_weight.T,
            router_weight,
            attn_gain[:, None],
            moe_gain[:, None],
            jnp.zeros((BLOCK, 128 - EXPERTS - 2), BF16),
        ],
        axis=1,
    )
    x_all, weights, gate_all = exchange(
        "exchange_inputs",
        1,
        [GatherTp(ROWS, D), GatherFsdp(1, 512), GatherFsdp(LOCAL, HIDDEN)],
        [inputs, small[None], gate_weight],
    )
    weights = weights[0]
    gain_one = weights[:, 416].astype(F32)[None, :]
    gain_two = weights[:, 417].astype(F32)[None, :]
    router_all = weights[:, 384:416]

    doc_index, offset = doc_layout(lengths[0])
    tables = rope_tables(offset)
    doc_column, doc_row = doc_index[:, None], doc_index[None, :]
    normed, query, pair, lse, mixed, attended = attention(
        x_all, weights, gain_one, tables, doc_column, doc_row
    )
    attended, up_all = exchange(
        "exchange_attended",
        2,
        [SumTp(ROWS, D), GatherFsdp(LOCAL, HIDDEN)],
        [attended, up_weight],
    )
    middle = inputs.astype(F32) + attended
    normed_two, unit_two, inverse_two = rms_parts(middle, gain_two)
    normed_two = normed_two.astype(BF16)
    tokens, down_all = exchange(
        "exchange_tokens",
        3,
        [GatherTp(ROWS, D), GatherFsdp(LOCAL, HIDDEN)],
        [normed_two, down_weight.transpose(0, 2, 1)],
    )

    expert_ids = jnp.arange(128, dtype=jnp.int32)
    chosen = jnp.any(routes[:, :, None] == expert_ids[None, None, :], axis=1)
    positions = jnp.arange(GROUP, dtype=jnp.int32)
    until = (positions[:, None] >= positions[None, :]).astype(BF16)
    running = jnp.dot(until, chosen.astype(BF16), preferred_element_type=F32).astype(jnp.int32)
    rank = jnp.where(chosen, running - 1, -1)
    rank = lax.dynamic_slice_in_dim(rank, tp * LOCAL, LOCAL, 1).T
    dy_all = lax.all_gather(cotangent, "tp", axis=0, tiled=True)
    router_wide = jnp.pad(router_all, ((0, 0), (0, 128 - EXPERTS)))
    combined, grads, gate_grad, up_grad, down_grad = experts(
        tp[None],
        tokens,
        dy_all,
        router_wide,
        chosen.astype(jnp.int32),
        rank[:, None, :],
        rank[:, :, None],
        gate_all,
        up_all,
        down_all,
    )
    grads, gate_grad = exchange(
        "exchange_expert_grads",
        4,
        [SumTp(ROWS, WIDE), SumFsdp(LOCAL, HIDDEN)],
        [grads, gate_grad],
    )
    chosen_own = lax.dynamic_slice_in_dim(chosen, tp * ROWS, ROWS, 0)
    logits = jnp.dot(normed_two, router_wide, preferred_element_type=F32)
    gates = jax.nn.softmax(jnp.where(chosen_own, logits, -1e30), axis=-1)
    dgates = grads[:, D:]
    dlogits = gates * (dgates - jnp.sum(gates * dgates, axis=-1, keepdims=True))
    dlogits = dlogits.astype(BF16)
    dnormed_two = grads[:, :D] + jnp.einsum(
        "te,de->td", dlogits, router_wide, preferred_element_type=F32
    )
    router_grad = jnp.einsum("td,te->de", normed_two, dlogits, preferred_element_type=F32)
    moe_gain_grad = jnp.sum(dnormed_two * unit_two, axis=0)
    dmiddle = cotangent.astype(F32) + rms_back(dnormed_two, unit_two, inverse_two, gain_two)
    datt, up_grad, moe_out = exchange(
        "exchange_attended_grads",
        5,
        [GatherTp(ROWS, D), SumFsdp(LOCAL, HIDDEN), SumTp(ROWS, D)],
        [dmiddle.astype(BF16), up_grad, combined],
    )
    outputs = (middle + moe_out).astype(BF16)
    dnormed, attention_grads, attn_gain_grad = attention_back(
        datt, x_all, normed, weights, query, pair, lse, mixed, tables, doc_column, doc_row
    )
    small_grads = jnp.where(
        expert_ids[None, :] == EXPERTS,
        moe_gain_grad[:, None],
        jnp.where(expert_ids[None, :] == EXPERTS + 1, attn_gain_grad[0][:, None], router_grad),
    )
    dnormed, down_grad, attention_grads, small_grads = exchange(
        "exchange_input_grads",
        6,
        [SumTp(ROWS, D), SumFsdp(LOCAL, HIDDEN), SumFsdp(1, 384), SumAll(128)],
        [dnormed, down_grad, attention_grads[None], small_grads[None]],
    )
    _, unit_one, inverse_one = rms_parts(inputs.astype(F32), gain_one)
    input_grad = dmiddle + rms_back(dnormed, unit_one, inverse_one, gain_one)
    attention_grads = attention_grads[0]
    return (
        outputs,
        input_grad,
        small_grads[:, EXPERTS + 1],
        attention_grads[:, 0:128],
        attention_grads[:, 128:192],
        attention_grads[:, 192:256],
        attention_grads[:, 256:384].T,
        small_grads[:, EXPERTS],
        small_grads[:, :EXPERTS],
        gate_grad,
        up_grad,
        down_grad.transpose(0, 2, 1),
    )


def solution(mesh):
    return jax.shard_map(
        per_device,
        mesh=mesh,
        in_specs=(
            P(("fsdp", "tp"), None),
            P("fsdp", None),
            P("fsdp", None),
            P("fsdp"),
            P("fsdp", "tp"),
            P("fsdp", "tp"),
            P("fsdp", "tp"),
            P("tp", "fsdp"),
            P("fsdp"),
            P("fsdp", None),
            P("tp", "fsdp", None),
            P("tp", "fsdp", None),
            P("tp", None, "fsdp"),
            P(("fsdp", "tp"), None),
        ),
        out_specs=(
            P(("fsdp", "tp"), None),
            P(("fsdp", "tp"), None),
            P(("fsdp", "tp")),
            P("fsdp", "tp"),
            P("fsdp", "tp"),
            P("fsdp", "tp"),
            P("tp", "fsdp"),
            P(("fsdp", "tp")),
            P(("fsdp", "tp"), None),
            P("tp", "fsdp", None),
            P("tp", "fsdp", None),
            P("tp", None, "fsdp"),
        ),
        check_vma=False,
    )
```

time: 1530 us -> 541 us (0.35)
  waiting for transfers between devices: 900 us -> 0.7 us
  Pallas kernels: 0 us -> 478 us
  blocking collectives: 215 us -> 0 us
  matrix products: 127 us -> 2.79 us
  local copies, waits for them, and re-layouts: 149 us -> 29.4 us
  other arithmetic: 98.2 us -> 15 us
    reduce_scatter x11 -> x0, waiting for transfers between devices: 703 us -> none  [the longest x1 88.2 us: per_device(): lax.psum_scatter(jnp.dot(mixed_low, output_all, preferred_element_type=jn...]
    pallas_call x0 -> x9, Pallas kernels: none -> 478 us  [the longest x6 405 us: exchange(): pl.pallas_call(body, name=name, out_shape=[task.out for task in tasks], i...]
    all_gather x7 -> x1, waiting for transfers between devices: 158 us -> 0.02 us  [per_device(): dy_all = lax.all_gather(cotangent, 'tp', axis=0, tiled=True)]
    dot_general x38 -> x4, matrix products: 127 us -> 2.79 us  [the longest x1 1.24 us: per_device(): logits = jnp.dot(normed_two, router_wide, preferred_element_type=F32)]
    all_gather x5 -> x0, blocking collectives: 110 us -> none  [the longest x1 24.9 us: per_device(): lax.all_gather(router_weight, 'fsdp', axis=0, tiled=True)]
    unnamed x2 -> x0, blocking collectives: 105 us -> none
    scatter x2 -> x0, local copies, waits for them, and re-layouts: 60.9 us -> none  [the longest x1 30.5 us: slot_tables(): jnp.full((EXPERTS * CAP,), GROUP, jnp.int32).at[where_to]]
    scatter-add x3 -> x0, other arithmetic: 46.5 us -> none  [the longest x1 17.7 us: per_device(): combined = jnp.zeros((GROUP + 1, D), jnp.float32).at[token_own].add(slot_...]
  transfers between devices with their start and end apart: 20 -> 1, of which waited for: 15 -> 0; matrix products, arithmetic and copies ran while one was open for 20% -> 4% of each run, Pallas kernels for 0% -> 41%
where the time goes in v1:
time: 541 us; the launch traced here: 540 us
  Pallas kernels  478 us (88%)
  local copies, waits for them, and re-layouts  29.4 us (5%)
  other arithmetic  15 us (3%)
  between operations  14.6 us (3%)
    pallas_call x6, Pallas kernels, exchange(): pl.pallas_call(body, name=name, out_shape=[task.out for task in tasks], i...  405 us
    pallas_call x1, Pallas kernels, experts(): pl.pallas_call(experts_body, name='experts', grid_spec=pltpu.PrefetchScal...  42.4 us
    unnamed x83, local copies, waits for them, and re-layouts  21.2 us
    pallas_call x1, Pallas kernels, attention_back(): pl.pallas_call(attention_back_body, name='attention_back', out_shape=[jax...  16.6 us
    pallas_call x1, Pallas kernels, attention(): pl.pallas_call(attention_body, name='attention', out_shape=[jax.ShapeDtyp...  13.7 us
  transfers between devices with their start and end apart: 1, of which 0 were waited for; matrix products, arithmetic and copies ran while one was open for 4% of the time, Pallas kernels for 41%

profile of v1, /device:TPU:0, one launch (start us, length us, event | category | flops | bytes accessed | tf_op | source)
XLA Modules:
  0.0 540.3 jit_solution(9249005341323981913)
XLA Ops:
  7.9 0.8 reduce-window.4
  11.4 0.9 concatenate.3
  12.3 0.9 copy-done.3
  13.2 0.9 copy-done.21
  14.2 99.8 %exchange_inputs.1 = (bf16[1024,1024]{1,0:T(8,128)(2,1)S(1)}, bf16[1,1024,512]{2,1,0:T(8,128)(2,1)S(1)}, bf16[4,1024,512]{2,1,0:T(8,128)(2,1)}) custom-call(bf16[128,1024]{1,0:T(8,128)(2,1)S(1)} %copy-done.3, bf16[1,64,512]{2,1,0:T(8,128)(2,1)S(1)} %bitcast.41, bf16[4,64,512]{2,1,0:T(8,128)(2,1)S(1)} %copy-done.21), custom_call_target="tpu_custom_call" | custom-call | tf_op jit(solution)/shard_map/exchange_inputs/pallas_call | solution.py:296
  114.0 1.3 copy-done
  115.4 1.0 copy.57
  116.4 5.8 %fusion = pred[1024,128]{1,0:T(8,128)(4,1)S(1)} fusion(s32[1024,8]{1,0:T(8,128)S(1)} %copy.57), kind=kLoop, calls=%fused_computation.2 | loop fusion | flops 1966080 | bytes 163840 | tf_op jit(solution)/shard_map/reduce_or | solution.py:695
  122.1 0.8 convert_element_type.85.chosen_ref
  124.1 1.9 copy.59.rank_column
  127.5 0.9 convert_reduce_fusion
  128.4 2.0 broadcast_select_fusion
  130.4 13.7 %attention.1 = (bf16[1024,1024]{1,0:T(8,128)(2,1)}, bf16[1024,128]{1,0:T(8,128)(2,1)S(1)}, bf16[1024,128]{1,0:T(8,128)(2,1)S(1)}, f32[2,1024]{1,0:T(2,128)S(1)},...) custom-call(bf16[1024,1024]{1,0:T(8,128)(2,1)} %copy-done, bf16[1024,512]{1,0:T(8,128)(2,1)S(1)} %bitcast.37, ...), custom_call_target="tpu_custom_call" | custom-call | tf_op jit(solution)/shard_map/attention/pallas_call | solution.py:388
  147.0 1.6 copy-done.10
  148.6 54.9 %exchange_attended.1 = (f32[128,1024]{1,0:T(8,128)S(1)}, bf16[4,1024,512]{2,1,0:T(8,128)(2,1)}) custom-call(bf16[1024,1024]{1,0:T(8,128)(2,1)S(1)} %copy-done.10, bf16[4,64,512]{2,1,0:T(8,128)(2,1)S(1)} %copy-done.14), custom_call_target="tpu_custom_call" | custom-call | tf_op jit(solution)/shard_map/exchange_attended/pallas_call | solution.py:296
  204.4 1.2 multiply_reduce_fusion.2
  205.6 0.8 multiply_convert_fusion.refs_0_
  206.5 1.0 copy-done.22
  207.5 53.0 %exchange_tokens.1 = (bf16[1024,1024]{1,0:T(8,128)(2,1)S(1)}, bf16[4,1024,512]{2,1,0:T(8,128)(2,1)}) custom-call(bf16[128,1024]{1,0:T(8,128)(2,1)S(1)} %multiply_convert_fusion.refs_0_, bf16[4,64,512]{2,1,0:T(8,128)(2,1)S(1)} %bitcast.42), custom_call_target="tpu_custom_call" | custom-call | tf_op jit(solution)/shard_map/exchange_tokens/pallas_call | solution.py:296
  260.6 1.3 copy-done.8
  262.5 1.2 fusion.27
  264.6 42.4 %experts.1 = (bf16[1024,1024]{1,0:T(8,128)(2,1)}, bf16[1024,1152]{1,0:T(8,128)(2,1)}, bf16[4,1024,512]{2,1,0:T(8,128)(2,1)}, bf16[4,1024,512]{2,1,0:T(8,128)(2,1)}, bf16[4,1024,512]{2,1,0:T(8,128)(2,1)}) custom-call(s32[1]{0:T(128)} %bitcast.11.tp_ref, bf16[1024,1024]{1,0:T(8,128)(2,1)} %copy-done.8, bf16[1024,1024]{1,0:T(8,128)(2,1)} %all-gather.2.cloned.1.call-done.dy_ref, ...), custom_call_target="tpu_custom_call" | custom-call | tf_op jit(solution)/shard_map/experts/pallas_call | solution.py:558
  307.1 1.7 copy-done.5
  308.7 57.2 %exchange_expert_grads.1 = (f32[128,1152]{1,0:T(8,128)S(1)}, f32[4,64,512]{2,1,0:T(8,128)S(1)}) custom-call(bf16[1024,1152]{1,0:T(8,128)(2,1)S(1)} %copy-done.5, bf16[4,1024,512]{2,1,0:T(8,128)(2,1)} %get-tuple-element.51.refs_1_), custom_call_target="tpu_custom_call" | custom-call | tf_op jit(solution)/shard_map/exchange_expert_grads/pallas_call | solution.py:296
  366.9 76.7 %exchange_attended_grads.1 = (bf16[1024,1024]{1,0:T(8,128)(2,1)S(1)}, f32[4,64,512]{2,1,0:T(8,128)S(1)}, f32[128,1024]{1,0:T(8,128)S(1)}) custom-call(bf16[128,1024]{1,0:T(8,128)(2,1)S(1)} %fusion.25.refs_0_, bf16[4,1024,512]{2,1,0:T(8,128)(2,1)} %get-tuple-element.53.refs_1_, bf16[1024,1024]{1,0:T(8,128)(2,1)S(1)} %copy-done.9), custom_call_target="tpu_custom_call" | custom-call | tf_op jit(solution)/shard_map/exchange_attended_grads/pallas_call | solution.py:296
  443.6 1.3 copy-done.12
  445.0 16.6 %attention_back.1 = (bf16[1024,1024]{1,0:T(8,128)(2,1)}, bf16[1024,384]{1,0:T(8,128)(2,1)S(1)}, f32[1,1024]{1,0:T(1,128)S(1)}) custom-call(bf16[1024,1024]{1,0:T(8,128)(2,1)} %copy-done.12, bf16[1024,1024]{1,0:T(8,128)(2,1)} %copy-done, bf16[1024,1024]{1,0:T(8,128)(2,1)} %get-tuple-element.57.normed_ref, bf16[1024,512]{1,0:T(8,128)(2,1)S(1)} %bitcast.38, ...), custom_call_target="tpu_custom_call" | custom-call | tf_op jit(solution)/shard_map/attention_back/pallas_call | solution.py:467
  462.1 1.6 copy-done.11
  463.7 63.4 %exchange_input_grads.1 = (f32[128,1024]{1,0:T(8,128)S(1)}, f32[4,64,512]{2,1,0:T(8,128)S(1)}, f32[1,64,384]{2,1,0:T(8,128)S(1)}, f32[8,128]{1,0:T(8,128)S(1)}) custom-call(bf16[1024,1024]{1,0:T(8,128)(2,1)S(1)} %copy-done.11, bf16[4,1024,512]{2,1,0:T(8,128)(2,1)} %get-tuple-element.63.refs_1_, bf16[1,1024,384]{2,1,0:T(8,128)(2,1)S(1)} %bitcast.39, ...), custom_call_target="tpu_custom_call" | custom-call | tf_op jit(solution)/shard_map/exchange_input_grads/pallas_call | solution.py:296
  529.4 1.1 fusion.9
  531.1 0.8 copy.69
  531.9 0.8 copy.70
  (104 shorter events, 16.1 us)
Async XLA Ops:
  7.2 257.4 %all-gather.2.cloned.1.call-start = ((), (), s32[]{:S(2)}) async-start(), calls=%async_computation | async-start | bytes 2359296 | tf_op jit(solution)/shard_map/all_gather | solution.py:701
  11.4 116.0 %copy-start.35 = (s32[1,3]{1,0:T(1,128)S(1)}, s32[1,3]{1,0:T(1,128)}, u32[]{:S(2)}) copy-start(s32[1,3]{1,0:T(1,128)} %param.15) | copy-start | bytes 40
  12.3 1.0 copy-start.3
  13.2 0.9 copy-start.21
  114.0 1.4 copy-start
  115.4 12.1 %copy-start.25 = (bf16[1024,32]{1,0:T(8,128)(2,1)}, bf16[1024,32]{1,0:T(8,128)(2,1)S(1)}, u32[]{:S(2)}) copy-start(bf16[1024,32]{1,0:T(8,128)(2,1)S(1)} %slice.50) | copy-start | bytes 196612
  127.5 19.5 %copy-start.14 = (bf16[4,64,512]{2,1,0:T(8,128)(2,1)S(1)}, bf16[4,64,512]{2,1,0:T(8,128)(2,1)}, u32[]{:S(2)}) copy-start(bf16[4,64,512]{2,1,0:T(8,128)(2,1)} %refs_1_.1) | copy-start | bytes 786436
  130.4 74.0 %copy-start.4 = (bf16[128,1024]{1,0:T(8,128)(2,1)S(1)}, bf16[128,1024]{1,0:T(8,128)(2,1)}, u32[]{:S(2)}) copy-start(bf16[128,1024]{1,0:T(8,128)(2,1)} %refs_0_.1) | copy-start | bytes 786436
  147.0 1.6 copy-start.10
  205.6 0.9 copy-start.23
  205.6 0.9 copy-start.33
  206.5 56.0 %copy-start.6 = (bf16[128,1024]{1,0:T(8,128)(2,1)}, bf16[128,1024]{1,0:T(8,128)(2,1)S(1)}, u32[]{:S(2)}) copy-start(bf16[128,1024]{1,0:T(8,128)(2,1)S(1)} %multiply_convert_fusion.refs_0_) | copy-start | bytes 786436
  206.5 1.0 copy-start.22
  260.6 1.4 copy-start.8
  264.6 101.4 %copy-start.29 = (f32[128,128]{1,0:T(8,128)S(1)}, f32[128,128]{1,0:T(8,128)}, u32[]{:S(2)}) copy-start(f32[128,128]{1,0:T(8,128)} %copy-done.28) | copy-start | bytes 196612
  264.6 101.6 %copy-start.24 = (f32[128,1024]{1,0:T(8,128)S(1)}, f32[128,1024]{1,0:T(8,128)}, u32[]{:S(2)}) copy-start(f32[128,1024]{1,0:T(8,128)} %copy-done.23) | copy-start | bytes 1572868
  264.6 101.6 %copy-start.30 = (f32[1024]{0:T(1024)S(1)}, f32[1024]{0:T(1024)}, u32[]{:S(2)}) copy-start(f32[1024]{0:T(1024)} %get-tuple-element.74) | copy-start | bytes 12292
  307.0 58.9 %copy-start.32 = (f32[128]{0:T(128)S(1)}, f32[128]{0:T(128)}, u32[]{:S(2)}) copy-start(f32[128]{0:T(128)} %copy-done.31) | copy-start | bytes 1540
  307.0 59.2 %copy-start.34 = (f32[128]{0:T(128)S(1)}, f32[128]{0:T(128)}, u32[]{:S(2)}) copy-start(f32[128]{0:T(128)} %copy-done.33) | copy-start | bytes 1540
  307.0 1.7 copy-start.5
  308.7 57.5 %copy-start.26 = (bf16[1024,32]{1,0:T(8,128)(2,1)S(1)}, bf16[1024,32]{1,0:T(8,128)(2,1)}, u32[]{:S(2)}) copy-start(bf16[1024,32]{1,0:T(8,128)(2,1)} %copy-done.25) | copy-start | bytes 196612
  308.7 58.0 %copy-start.27 = (bf16[128,1024]{1,0:T(8,128)(2,1)S(1)}, bf16[128,1024]{1,0:T(8,128)(2,1)}, u32[]{:S(2)}) copy-start(bf16[128,1024]{1,0:T(8,128)(2,1)} %param.27) | copy-start | bytes 786436
  308.7 58.2 %copy-start.9 = (bf16[1024,1024]{1,0:T(8,128)(2,1)S(1)}, bf16[1024,1024]{1,0:T(8,128)(2,1)}, u32[]{:S(2)}) copy-start(bf16[1024,1024]{1,0:T(8,128)(2,1)} %get-tuple-element.54.refs_2_) | copy-start | bytes 6291460
  366.6 78.3 %copy-start.2 = (f32[1024,128]{1,0:T(8,128)S(1)}, f32[1024,128]{1,0:T(8,128)}, u32[]{:S(2)}) copy-start(f32[1024,128]{1,0:T(8,128)} %copy-done.1) | copy-start | bytes 1572868
  366.6 78.3 %copy-start.16 = (bf16[1024,128]{1,0:T(8,128)(2,1)S(1)}, bf16[1024,128]{1,0:T(8,128)(2,1)}, u32[]{:S(2)}) copy-start(bf16[1024,128]{1,0:T(8,128)(2,1)} %copy-done.15) | copy-start | bytes 786436
  366.6 78.3 %copy-start.18 = (bf16[1024,128]{1,0:T(8,128)(2,1)S(1)}, bf16[1024,128]{1,0:T(8,128)(2,1)}, u32[]{:S(2)}) copy-start(bf16[1024,128]{1,0:T(8,128)(2,1)} %copy-done.17) | copy-start | bytes 786436
  366.7 78.3 %copy-start.20 = (bf16[128,1024]{1,0:T(8,128)(2,1)S(1)}, bf16[128,1024]{1,0:T(8,128)(2,1)}, u32[]{:S(2)}) copy-start(bf16[128,1024]{1,0:T(8,128)(2,1)} %copy-done.19) | copy-start | bytes 786436
  443.6 1.3 copy-start.12
  444.9 16.6 %copy-start.7 = (bf16[128,1024]{1,0:T(8,128)(2,1)S(1)}, bf16[128,1024]{1,0:T(8,128)(2,1)}, u32[]{:S(2)}) copy-start(bf16[128,1024]{1,0:T(8,128)(2,1)} %copy-done.6) | copy-start | bytes 786436
  444.9 16.6 %copy-start.36 = (pred[128]{0:T(512)(128)(4,1)S(1)}, pred[128]{0:T(512)(128)(4,1)}, u32[]{:S(2)}) copy-start(pred[128]{0:T(512)(128)(4,1)} %get-tuple-element.98) | copy-start | bytes 388
  445.0 16.6 %copy-start.37 = (pred[128]{0:T(512)(128)(4,1)S(1)}, pred[128]{0:T(512)(128)(4,1)}, u32[]{:S(2)}) copy-start(pred[128]{0:T(512)(128)(4,1)} %get-tuple-element.99) | copy-start | bytes 388
  462.1 1.6 copy-start.11
  (7 other events, 5.1 us)
Sparse Core Ops, SparseCore 0:
  9.7 93.2 all-gather.1

commit v2 on v1

--- a/solution.py
+++ b/solution.py
@@ -25,28 +25,22 @@
 score_scale = 1.0 / HEAD_DIM
 F32 = jnp.float32
 BF16 = jnp.bfloat16
-TP_STEPS = ((2, 0), (2, 1), (1, 1), (3, 1), (1, 0), (3, 0), (0, 1))
-CHIP_STEPS = ((1, 2), (0, 2), (1, 1), (1, 3), (0, 1), (0, 3), (1, 0))
-
-
-def tp_peer(step):
+
+
+def tp_at(along, across):
     tp = lax.axis_index("tp")
-    along_y, along_x = step
-    return lax.rem(tp // 2 + along_y, 4) * 2 + lax.rem(tp + along_x, 2)
-
-
-def chip_at(step):
-    chip = lax.axis_index("fsdp") // 2
-    along_x, along_z = step
-    return lax.rem(chip // 4 + along_x, 2) * 4 + lax.rem(chip + along_z, 4)
-
-
-def own_core():
-    return lax.rem(lax.axis_index("fsdp"), 2)
+    return lax.rem(tp // 2 + along, 4) * 2 + lax.rem(tp + across, 2)
+
+
+def fsdp_at(along, across):
+    fsdp = lax.axis_index("fsdp")
+    chip = lax.rem(fsdp // 8 + across, 2) * 4 + lax.rem(fsdp // 2 + along, 4)
+    return chip * 2 + lax.rem(fsdp, 2)
 
 
 def core_partner():
-    return (lax.axis_index("fsdp") // 2) * 2 + 1 - own_core()
+    fsdp = lax.axis_index("fsdp")
+    return fsdp // 2 * 2 + 1 - lax.rem(fsdp, 2)
 
 
 def send(src, dst, send_sem, recv_sem, device):
@@ -64,17 +58,38 @@
 
 def greet():
     barrier = pltpu.get_barrier_semaphore()
-    for step in TP_STEPS:
-        pl.semaphore_signal(barrier, inc=1, device_id={"tp": tp_peer(step)}, device_id_type=MESH)
-    for step in CHIP_STEPS:
-        pl.semaphore_signal(
-            barrier,
-            inc=1,
-            device_id={"fsdp": chip_at(step) * 2 + own_core()},
-            device_id_type=MESH,
-        )
+    for place in ((1, 0), (3, 0), (0, 1)):
+        for device in ({"tp": tp_at(*place)}, {"fsdp": fsdp_at(*place)}):
+            pl.semaphore_signal(barrier, inc=1, device_id=device, device_id_type=MESH)
     pl.semaphore_signal(barrier, inc=1, device_id={"fsdp": core_partner()}, device_id_type=MESH)
-    pl.semaphore_wait(barrier, 15)
+    pl.semaphore_wait(barrier, 7)
+
+
+def dma(count):
+    return pltpu.SemaphoreType.DMA((count,))
+
+
+GATHER = (
+    ((0, 0), (0, 1), None),
+    ((0, 0), (1, 0), None),
+    ((0, 0), (3, 0), None),
+    ((0, 1), (1, 0), 0),
+    ((0, 1), (3, 0), 0),
+    ((3, 0), (1, 0), 1),
+    ((1, 1), (3, 0), 4),
+)
+ARRIVES = ((0, 1), (3, 0), (1, 0), (3, 1), (1, 1), (2, 0), (2, 1))
+SUM = (
+    ((2, 0), (1, 0), ()),
+    ((2, 1), (3, 0), ()),
+    ((1, 1), (1, 0), ()),
+    ((3, 0), (3, 0), ()),
+    ((1, 0), (1, 0), (0,)),
+    ((3, 1), (3, 0), (1,)),
+    ((0, 1), (0, 1), (2, 5)),
+)
+LAST = (3, 4, 6)
+CORE_ORDER = tuple(block for block, _, _ in SUM) + ((0, 0),)
 
 
 class GatherTp:
@@ -82,24 +97,35 @@
         self.rows = rows
         self.out = jax.ShapeDtypeStruct((8 * rows, columns), BF16)
         self.out_space = pltpu.VMEM
-        self.scratch = [pltpu.SemaphoreType.DMA((7,)), pltpu.SemaphoreType.DMA((7,)), pltpu.SemaphoreType.DMA(())]
-
-    def start(self, src, out, send_sem, recv_sem, own_sem):
-        here = out.at[pl.ds(pl.multiple_of(lax.axis_index("tp") * self.rows, self.rows), self.rows)]
-        self.copies = [
-            send(src, here, send_sem.at[k], recv_sem.at[k], {"tp": tp_peer(step)})
-            for k, step in enumerate(TP_STEPS)
-        ]
-        self.own = pltpu.make_async_copy(src, here, own_sem)
-        self.own.start()
-
-    def progress(self, k):
-        pass
-
-    def finish(self):
-        for copy in self.copies:
-            copy.wait()
-        self.own.wait()
+        self.scratch = [dma(7), dma(7), pltpu.SemaphoreType.DMA(())]
+
+    def run(self, src, out, send_sem, recv_sem, own_sem):
+        def block(place):
+            return out.at[pl.ds(pl.multiple_of(tp_at(*place) * self.rows, self.rows), self.rows)]
+
+        own = pltpu.make_async_copy(src, block((0, 0)), own_sem)
+        own.start()
+        copies, arrived = [], set()
+        for k, (place, target, after) in enumerate(GATHER):
+            if after is not None and after not in arrived:
+                yield
+                copies[after].wait_recv()
+                arrived.add(after)
+            copies.append(
+                send(
+                    src if place == (0, 0) else block(place),
+                    block(place),
+                    send_sem.at[k],
+                    recv_sem.at[k],
+                    {"tp": tp_at(*target)},
+                )
+            )
+        yield
+        for k, copy in enumerate(copies):
+            if k not in arrived:
+                copy.wait_recv()
+            copy.wait_send()
+        own.wait()
 
 
 class SumTp:
@@ -107,73 +133,92 @@
         self.rows = rows
         self.out = jax.ShapeDtypeStruct((rows, columns), F32)
         self.out_space = pltpu.VMEM
-        self.scratch = [
-            pltpu.SemaphoreType.DMA((7,)),
-            pltpu.SemaphoreType.DMA((7,)),
-            pltpu.VMEM((7, rows, columns), BF16),
-        ]
-
-    def start(self, src, out, send_sem, recv_sem, landed):
-        self.src, self.out_ref, self.landed = src, out, landed
-        self.copies = []
-        for k, step in enumerate(TP_STEPS):
-            peer = tp_peer(step)
-            part = src.at[pl.ds(pl.multiple_of(peer * self.rows, self.rows), self.rows)]
-            self.copies.append(send(part, landed.at[k], send_sem.at[k], recv_sem.at[k], {"tp": peer}))
-
-    def progress(self, k):
-        pass
-
-    def finish(self):
-        for copy in self.copies:
-            copy.wait()
-        first = lax.axis_index("tp") * self.rows
-
-        @pl.loop(0, self.rows // 16)
-        def _(i):
-            at = pl.multiple_of(i * 16, 16)
-            total = self.src[pl.ds(pl.multiple_of(first + at, 16), 16), :].astype(F32)
-            for k in range(7):
-                total = total + self.landed[k, pl.ds(at, 16), :].astype(F32)
-            self.out_ref[pl.ds(at, 16), :] = total
+        self.scratch = [dma(7), dma(7), pltpu.VMEM((7, rows, columns), BF16)]
+
+    def run(self, src, out, send_sem, recv_sem, landed):
+        def first(place):
+            return pl.multiple_of(tp_at(*place) * self.rows, self.rows)
+
+        def total(place, others, dst):
+            start = first(place)
+
+            @pl.loop(0, self.rows // 16)
+            def _(i):
+                at = pl.multiple_of(i * 16, 16)
+                value = src[pl.ds(pl.multiple_of(start + at, 16), 16), :].astype(F32)
+                for k in others:
+                    value = value + landed[k, pl.ds(at, 16), :].astype(F32)
+                dst[pl.ds(at, 16), :] = value.astype(dst.dtype)
+
+        copies, arrived = [], set()
+        for k, (place, target, others) in enumerate(SUM):
+            if others:
+                yield
+                for other in others:
+                    copies[other].wait_recv()
+                    arrived.add(other)
+                part = landed.at[others[0]]
+                total(place, others, part)
+            else:
+                part = src.at[pl.ds(first(place), self.rows)]
+            copies.append(
+                send(part, landed.at[k], send_sem.at[k], recv_sem.at[k], {"tp": tp_at(*target)})
+            )
+        yield
+        for k in LAST:
+            copies[k].wait_recv()
+        total((0, 0), LAST, out)
+        for copy in copies:
+            copy.wait_send()
 
 
 class GatherFsdp:
     def __init__(self, experts, columns):
         self.out = jax.ShapeDtypeStruct((experts, D, columns), BF16)
         self.out_space = pl.ANY
-        self.scratch = [pltpu.SemaphoreType.DMA((7,)), pltpu.SemaphoreType.DMA((7,)), pltpu.SemaphoreType.DMA((8,)), pltpu.SemaphoreType.DMA((8,)), pltpu.SemaphoreType.DMA(())]
-
-    def block(self, fsdp):
-        return self.out_ref.at[:, pl.ds(pl.multiple_of(fsdp * BLOCK, BLOCK), BLOCK)]
-
-    def start(self, src, out, send_sem, recv_sem, core_send, core_recv, own_sem):
-        self.out_ref, self.core_send, self.core_recv = out, core_send, core_recv
-        here = self.block(lax.axis_index("fsdp"))
-        self.copies = [
-            send(src, here, send_sem.at[k], recv_sem.at[k], {"fsdp": chip_at(step) * 2 + own_core()})
-            for k, step in enumerate(CHIP_STEPS)
-        ]
-        self.across = [send(src, here, core_send.at[7], core_recv.at[7], {"fsdp": core_partner()})]
-        self.own = pltpu.make_async_copy(src, here, own_sem)
-        self.own.start()
-
-    def progress(self, k):
-        if k == 7:
-            return
-        along_x, along_z = CHIP_STEPS[k]
-        self.copies[k].wait_recv()
-        block = self.block(chip_at((along_x, (4 - along_z) % 4)) * 2 + own_core())
-        self.across.append(
-            send(block, block, self.core_send.at[k], self.core_recv.at[k], {"fsdp": core_partner()})
+        self.scratch = [dma(7), dma(7), dma(8), dma(8), pltpu.SemaphoreType.DMA(())]
+
+    def run(self, src, out, send_sem, recv_sem, core_send, core_recv, own_sem):
+        def block(place):
+            return out.at[:, pl.ds(pl.multiple_of(fsdp_at(*place) * BLOCK, BLOCK), BLOCK)]
+
+        own = pltpu.make_async_copy(src, block((0, 0)), own_sem)
+        own.start()
+        copies, arrived, crossed = [], set(), []
+
+        def arrive(k):
+            copies[k].wait_recv()
+            arrived.add(k)
+            here = block(ARRIVES[k])
+            crossed.append(
+                send(here, here, core_send.at[k], core_recv.at[k], {"fsdp": core_partner()})
+            )
+
+        for k, (place, target, after) in enumerate(GATHER):
+            if after is not None and after not in arrived:
+                yield
+                arrive(after)
+            copies.append(
+                send(
+                    src if place == (0, 0) else block(place),
+                    block(place),
+                    send_sem.at[k],
+                    recv_sem.at[k],
+                    {"fsdp": fsdp_at(*target)},
+                )
+            )
+        crossed.append(
+            send(src, block((0, 0)), core_send.at[7], core_recv.at[7], {"fsdp": core_partner()})
         )
-
-    def finish(self):
-        for copy in self.copies:
+        yield
+        for k in range(7):
+            if k not in arrived:
+                arrive(k)
+        for copy in copies:
             copy.wait_send()
-        for copy in self.across:
+        for copy in crossed:
             copy.wait()
-        self.own.wait()
+        own.wait()
 
 
 class SumFsdp:
@@ -182,57 +227,66 @@
         self.out = jax.ShapeDtypeStruct((experts, BLOCK, columns), F32)
         self.out_space = pltpu.VMEM
         self.scratch = [
-            pltpu.SemaphoreType.DMA((7,)),
-            pltpu.SemaphoreType.DMA((7,)),
-            pltpu.SemaphoreType.DMA((8,)),
-            pltpu.SemaphoreType.DMA((8,)),
+            dma(7),
+            dma(7),
+            dma(8),
+            dma(8),
             pltpu.VMEM((8, experts, BLOCK, columns), dtype),
             pltpu.VMEM((7, experts, BLOCK, columns), dtype),
         ]
 
-    def start(self, src, out, send_sem, recv_sem, core_send, core_recv, pair, landed):
-        self.src, self.out_ref, self.pair, self.landed = src, out, pair, landed
-        self.send_sem, self.recv_sem = send_sem, recv_sem
-        self.across, self.copies = [], []
-        for k, step in enumerate(CHIP_STEPS + ((0, 0),)):
-            first = (chip_at(step) * 2 + 1 - own_core()) * BLOCK
-            part = src.at[:, pl.ds(pl.multiple_of(first, BLOCK), BLOCK)]
-            self.across.append(
-                send(part, pair.at[k], core_send.at[k], core_recv.at[k], {"fsdp": core_partner()})
+    def run(self, src, out, send_sem, recv_sem, core_send, core_recv, pair, landed):
+        def over_rows(body):
+            @pl.loop(0, self.experts * (BLOCK // 16))
+            def _(i):
+                body(i // (BLOCK // 16), pl.multiple_of(lax.rem(i, BLOCK // 16) * 16, 16))
+
+        crossed, copies, arrived = [], [], set()
+        mine = lax.rem(lax.axis_index("fsdp"), 2)
+        for k, place in enumerate(CORE_ORDER):
+            start = pl.multiple_of((fsdp_at(*place) + 1 - 2 * mine) * BLOCK, BLOCK)
+            crossed.append(
+                send(
+                    src.at[:, pl.ds(start, BLOCK)],
+                    pair.at[k],
+                    core_send.at[k],
+                    core_recv.at[k],
+                    {"fsdp": core_partner()},
+                )
             )
-
-    def progress(self, k):
-        self.across[k].wait_recv()
-        step = (CHIP_STEPS + ((0, 0),))[k]
-        owner = chip_at(step) * 2 + own_core()
-
-        @pl.loop(0, self.experts * (BLOCK // 16))
-        def _(i):
-            expert = i // (BLOCK // 16)
-            at = pl.multiple_of(lax.rem(i, BLOCK // 16) * 16, 16)
-            mine = self.src[expert, pl.ds(pl.multiple_of(owner * BLOCK + at, 16), 16), :].astype(F32)
-            total = mine + self.pair[k, expert, pl.ds(at, 16), :].astype(F32)
-            self.pair[k, expert, pl.ds(at, 16), :] = total.astype(self.pair.dtype)
-
-        if k < 7:
-            self.copies.append(
-                send(self.pair.at[k], self.landed.at[k], self.send_sem.at[k], self.recv_sem.at[k], {"fsdp": owner})
-            )
-
-    def finish(self):
-        for copy in self.across:
-            copy.wait_send()
-        for copy in self.copies:
-            copy.wait()
-
-        @pl.loop(0, self.experts * (BLOCK // 16))
-        def _(i):
-            expert = i // (BLOCK // 16)
-            at = pl.multiple_of(lax.rem(i, BLOCK // 16) * 16, 16)
-            total = self.pair[7, expert, pl.ds(at, 16), :].astype(F32)
-            for k in range(7):
-                total = total + self.landed[k, expert, pl.ds(at, 16), :].astype(F32)
-            self.out_ref[expert, pl.ds(at, 16), :] = total
+        for k, place in enumerate(CORE_ORDER):
+            if k in (0, 4, 5, 6):
+                yield
+            others = SUM[k][2] if k < 7 else LAST
+            crossed[k].wait_recv()
+            for other in others:
+                if other not in arrived:
+                    copies[other].wait_recv()
+                    arrived.add(other)
+            start = fsdp_at(*place) * BLOCK
+            if k == 7:
+                for copy in copies + crossed:
+                    copy.wait_send()
+            dst = out if k == 7 else pair.at[k]
+
+            def add(expert, at):
+                rows = pl.ds(pl.multiple_of(start + at, 16), 16)
+                value = src[expert, rows, :].astype(F32) + pair[k, expert, pl.ds(at, 16), :].astype(F32)
+                for other in others:
+                    value = value + landed[other, expert, pl.ds(at, 16), :].astype(F32)
+                dst[expert, pl.ds(at, 16), :] = value.astype(dst.dtype)
+
+            over_rows(add)
+            if k < 7:
+                copies.append(
+                    send(
+                        pair.at[k],
+                        landed.at[k],
+                        send_sem.at[k],
+                        recv_sem.at[k],
+                        {"fsdp": fsdp_at(*SUM[k][1])},
+                    )
+                )
 
 
 class SumAll:
@@ -242,56 +296,68 @@
         self.out_space = pltpu.VMEM
         self.scratch = self.over_fsdp.scratch + [
             pltpu.VMEM((1, BLOCK, columns), F32),
-            pltpu.SemaphoreType.DMA((7,)),
-            pltpu.SemaphoreType.DMA((7,)),
+            dma(7),
+            dma(7),
             pltpu.VMEM((7, 8, columns), F32),
         ]
 
-    def start(self, src, out, *scratch):
-        self.out_ref = out
-        self.total, self.send_sem, self.recv_sem, self.landed = scratch[-4:]
-        self.over_fsdp.start(src, self.total, *scratch[:-4])
-
-    def progress(self, k):
-        self.over_fsdp.progress(k)
-
-    def middle(self):
-        self.over_fsdp.finish()
-        self.copies = []
-        for k, step in enumerate(TP_STEPS):
-            peer = tp_peer(step)
-            part = self.total.at[0, pl.ds(pl.multiple_of(peer * 8, 8), 8)]
-            self.copies.append(
-                send(part, self.landed.at[k], self.send_sem.at[k], self.recv_sem.at[k], {"tp": peer})
+    def run(self, src, out, *scratch):
+        total, send_sem, recv_sem, landed = scratch[-4:]
+        yield from self.over_fsdp.run(src, total, *scratch[:-4])
+
+        def own(place):
+            return total[0, pl.ds(pl.multiple_of(tp_at(*place) * 8, 8), 8), :]
+
+        copies = []
+        for k, (place, target, others) in enumerate(SUM):
+            if others:
+                yield
+                value = own(place)
+                for other in others:
+                    copies[other].wait_recv()
+                    value = value + landed[other]
+                landed[others[0]] = value
+                part = landed.at[others[0]]
+            else:
+                part = total.at[0, pl.ds(pl.multiple_of(tp_at(*place) * 8, 8), 8)]
+            copies.append(
+                send(part, landed.at[k], send_sem.at[k], recv_sem.at[k], {"tp": tp_at(*target)})
             )
-
-    def finish(self):
-        for copy in self.copies:
-            copy.wait()
-        total = self.total[0, pl.ds(pl.multiple_of(lax.axis_index("tp") * 8, 8), 8), :]
-        for k in range(7):
-            total = total + self.landed[k]
-        self.out_ref[...] = total
+        yield
+        value = own((0, 0))
+        for other in LAST:
+            copies[other].wait_recv()
+            value = value + landed[other]
+        out[...] = value
+        for copy in copies:
+            copy.wait_send()
+
+
+def together(runs):
+    runs = list(runs)
+    while runs:
+        still = []
+        for run in runs:
+            try:
+                next(run)
+                still.append(run)
+            except StopIteration:
+                pass
+        runs = still
 
 
 def exchange(name, number, tasks, arrays):
     n = len(tasks)
-    counts = [len(task.scratch) for task in tasks]
 
     def body(*refs):
         sources, outs, scratch = refs[:n], refs[n : 2 * n], list(refs[2 * n :])
         greet()
-        for task, source, out, count in zip(tasks, sources, outs, counts):
-            task.start(source, out, *scratch[:count])
+        runs = []
+        for task, source, out in zip(tasks, sources, outs):
+            count = len(task.scratch)
+            runs.append(task.run(source, out, *scratch[:count]))
             scratch = scratch[count:]
-        for k in range(8):
-            for task in tasks:
-                task.progress(k)
-        for task in tasks:
-            if isinstance(task, SumAll):
-                task.middle()
-        for task in tasks:
-            task.finish()
+        together(runs)
 
     return pl.pallas_call(
         body,

time: 541 us -> 399 us (0.74)
  Pallas kernels: 478 us -> 336 us
    pallas_call x6, Pallas kernels: 405 us -> 264 us  [exchange(): pl.pallas_call(body, name=name, out_shape=[task.out for task in tasks], i...]
  transfers between devices with their start and end apart: 1 -> 1, of which waited for: 0 -> 0; matrix products, arithmetic and copies ran while one was open for 4% -> 6% of each run, Pallas kernels for 41% -> 32%
where the time goes in v2:
time: 399 us
  Pallas kernels  336 us (84%)
  local copies, waits for them, and re-layouts  29.4 us (7%)
  other arithmetic  15 us (4%)
  between operations  14.6 us (4%)
    pallas_call x6, Pallas kernels, exchange(): pl.pallas_call(body, name=name, out_shape=[task.out for task in tasks], i...  264 us
    pallas_call x1, Pallas kernels, experts(): pl.pallas_call(experts_body, name='experts', grid_spec=pltpu.PrefetchScal...  42.4 us
    unnamed x83, local copies, waits for them, and re-layouts  21.2 us
    pallas_call x1, Pallas kernels, attention_back(): pl.pallas_call(attention_back_body, name='attention_back', out_shape=[jax...  16.6 us
    pallas_call x1, Pallas kernels, attention(): pl.pallas_call(attention_body, name='attention', out_shape=[jax.ShapeDtyp...  13.7 us
  transfers between devices with their start and end apart: 1, of which 0 were waited for; matrix products, arithmetic and copies ran while one was open for 6% of the time, Pallas kernels for 32%

profile of v2, /device:TPU:0, one launch (start us, length us, event | category | flops | bytes accessed | tf_op | source)
XLA Modules:
  0.0 398.8 jit_solution(14885186906996069130)
XLA Ops:
  7.9 0.8 reduce-window.4
  11.4 0.9 concatenate.3
  12.3 0.9 copy-done.3
  13.2 0.9 copy-done.21
  14.2 48.2 %exchange_inputs.1 = (bf16[1024,1024]{1,0:T(8,128)(2,1)S(1)}, bf16[1,1024,512]{2,1,0:T(8,128)(2,1)S(1)}, bf16[4,1024,512]{2,1,0:T(8,128)(2,1)}) custom-call(bf16[128,1024]{1,0:T(8,128)(2,1)S(1)} %copy-done.3, bf16[1,64,512]{2,1,0:T(8,128)(2,1)S(1)} %bitcast.41, bf16[4,64,512]{2,1,0:T(8,128)(2,1)S(1)} %copy-done.21), custom_call_target="tpu_custom_call" | custom-call | tf_op jit(solution)/shard_map/exchange_inputs/pallas_call | solution.py:362
  62.4 1.3 copy-done
  63.8 1.0 copy.57
  64.8 5.8 %fusion = pred[1024,128]{1,0:T(8,128)(4,1)S(1)} fusion(s32[1024,8]{1,0:T(8,128)S(1)} %copy.57), kind=kLoop, calls=%fused_computation.2 | loop fusion | flops 1966080 | bytes 163840 | tf_op jit(solution)/shard_map/reduce_or | solution.py:761
  70.6 0.8 convert_element_type.85.chosen_ref
  72.5 1.9 copy.59.rank_column
  76.0 0.9 convert_reduce_fusion
  76.9 2.0 broadcast_select_fusion
  78.9 13.7 %attention.1 = (bf16[1024,1024]{1,0:T(8,128)(2,1)}, bf16[1024,128]{1,0:T(8,128)(2,1)S(1)}, bf16[1024,128]{1,0:T(8,128)(2,1)S(1)}, f32[2,1024]{1,0:T(2,128)S(1)},...) custom-call(bf16[1024,1024]{1,0:T(8,128)(2,1)} %copy-done, bf16[1024,512]{1,0:T(8,128)(2,1)S(1)} %bitcast.37, ...), custom_call_target="tpu_custom_call" | custom-call | tf_op jit(solution)/shard_map/attention/pallas_call | solution.py:454
  95.5 1.6 copy-done.10
  97.1 30.6 %exchange_attended.1 = (f32[128,1024]{1,0:T(8,128)S(1)}, bf16[4,1024,512]{2,1,0:T(8,128)(2,1)}) custom-call(bf16[1024,1024]{1,0:T(8,128)(2,1)S(1)} %copy-done.10, bf16[4,64,512]{2,1,0:T(8,128)(2,1)S(1)} %copy-done.14), custom_call_target="tpu_custom_call" | custom-call | tf_op jit(solution)/shard_map/exchange_attended/pallas_call | solution.py:362
  128.5 1.2 multiply_reduce_fusion.2
  129.8 0.8 multiply_convert_fusion.refs_0_
  130.7 1.0 copy-done.22
  131.7 33.9 %exchange_tokens.1 = (bf16[1024,1024]{1,0:T(8,128)(2,1)S(1)}, bf16[4,1024,512]{2,1,0:T(8,128)(2,1)}) custom-call(bf16[128,1024]{1,0:T(8,128)(2,1)S(1)} %multiply_convert_fusion.refs_0_, bf16[4,64,512]{2,1,0:T(8,128)(2,1)S(1)} %bitcast.42), custom_call_target="tpu_custom_call" | custom-call | tf_op jit(solution)/shard_map/exchange_tokens/pallas_call | solution.py:362
  165.7 1.3 copy-done.8
  167.6 1.2 fusion.27
  169.7 42.4 %experts.1 = (bf16[1024,1024]{1,0:T(8,128)(2,1)}, bf16[1024,1152]{1,0:T(8,128)(2,1)}, bf16[4,1024,512]{2,1,0:T(8,128)(2,1)}, bf16[4,1024,512]{2,1,0:T(8,128)(2,1)}, bf16[4,1024,512]{2,1,0:T(8,128)(2,1)}) custom-call(s32[1]{0:T(128)} %bitcast.11.tp_ref, bf16[1024,1024]{1,0:T(8,128)(2,1)} %copy-done.8, bf16[1024,1024]{1,0:T(8,128)(2,1)} %all-gather.2.cloned.1.call-done.dy_ref, ...), custom_call_target="tpu_custom_call" | custom-call | tf_op jit(solution)/shard_map/experts/pallas_call | solution.py:624
  212.1 1.7 copy-done.5
  213.8 41.7 %exchange_expert_grads.1 = (f32[128,1152]{1,0:T(8,128)S(1)}, f32[4,64,512]{2,1,0:T(8,128)S(1)}) custom-call(bf16[1024,1152]{1,0:T(8,128)(2,1)S(1)} %copy-done.5, bf16[4,1024,512]{2,1,0:T(8,128)(2,1)} %get-tuple-element.51.refs_1_), custom_call_target="tpu_custom_call" | custom-call | tf_op jit(solution)/shard_map/exchange_expert_grads/pallas_call | solution.py:362
  256.4 47.5 %exchange_attended_grads.1 = (bf16[1024,1024]{1,0:T(8,128)(2,1)S(1)}, f32[4,64,512]{2,1,0:T(8,128)S(1)}, f32[128,1024]{1,0:T(8,128)S(1)}) custom-call(bf16[128,1024]{1,0:T(8,128)(2,1)S(1)} %fusion.25.refs_0_, bf16[4,1024,512]{2,1,0:T(8,128)(2,1)} %get-tuple-element.53.refs_1_, bf16[1024,1024]{1,0:T(8,128)(2,1)S(1)} %copy-done.9), custom_call_target="tpu_custom_call" | custom-call | tf_op jit(solution)/shard_map/exchange_attended_grads/pallas_call | solution.py:362
  304.0 1.3 copy-done.12
  305.3 16.6 %attention_back.1 = (bf16[1024,1024]{1,0:T(8,128)(2,1)}, bf16[1024,384]{1,0:T(8,128)(2,1)S(1)}, f32[1,1024]{1,0:T(1,128)S(1)}) custom-call(bf16[1024,1024]{1,0:T(8,128)(2,1)} %copy-done.12, bf16[1024,1024]{1,0:T(8,128)(2,1)} %copy-done, bf16[1024,1024]{1,0:T(8,128)(2,1)} %get-tuple-element.57.normed_ref, bf16[1024,512]{1,0:T(8,128)(2,1)S(1)} %bitcast.38, ...), custom_call_target="tpu_custom_call" | custom-call | tf_op jit(solution)/shard_map/attention_back/pallas_call | solution.py:533
  322.5 1.6 copy-done.11
  324.0 61.5 %exchange_input_grads.1 = (f32[128,1024]{1,0:T(8,128)S(1)}, f32[4,64,512]{2,1,0:T(8,128)S(1)}, f32[1,64,384]{2,1,0:T(8,128)S(1)}, f32[8,128]{1,0:T(8,128)S(1)}) custom-call(bf16[1024,1024]{1,0:T(8,128)(2,1)S(1)} %copy-done.11, bf16[4,1024,512]{2,1,0:T(8,128)(2,1)} %get-tuple-element.63.refs_1_, bf16[1,1024,384]{2,1,0:T(8,128)(2,1)S(1)} %bitcast.39, ...), custom_call_target="tpu_custom_call" | custom-call | tf_op jit(solution)/shard_map/exchange_input_grads/pallas_call | solution.py:362
  387.8 1.1 fusion.9
  389.5 0.8 copy.69
  391.1 0.8 copy.71
  (104 shorter events, 16.1 us)
Async XLA Ops:
  7.2 162.5 %all-gather.2.cloned.1.call-start = ((), (), s32[]{:S(2)}) async-start(), calls=%async_computation | async-start | bytes 2359296 | tf_op jit(solution)/shard_map/all_gather | solution.py:767
  11.4 64.5 %copy-start.35 = (s32[1,3]{1,0:T(1,128)S(1)}, s32[1,3]{1,0:T(1,128)}, u32[]{:S(2)}) copy-start(s32[1,3]{1,0:T(1,128)} %param.15) | copy-start | bytes 40
  12.3 1.0 copy-start.3
  13.2 0.9 copy-start.21
  62.4 1.4 copy-start
  63.8 12.1 %copy-start.25 = (bf16[1024,32]{1,0:T(8,128)(2,1)}, bf16[1024,32]{1,0:T(8,128)(2,1)S(1)}, u32[]{:S(2)}) copy-start(bf16[1024,32]{1,0:T(8,128)(2,1)S(1)} %slice.50) | copy-start | bytes 196612
  76.0 19.5 %copy-start.14 = (bf16[4,64,512]{2,1,0:T(8,128)(2,1)S(1)}, bf16[4,64,512]{2,1,0:T(8,128)(2,1)}, u32[]{:S(2)}) copy-start(bf16[4,64,512]{2,1,0:T(8,128)(2,1)} %refs_1_.1) | copy-start | bytes 786436
  78.8 49.7 %copy-start.4 = (bf16[128,1024]{1,0:T(8,128)(2,1)S(1)}, bf16[128,1024]{1,0:T(8,128)(2,1)}, u32[]{:S(2)}) copy-start(bf16[128,1024]{1,0:T(8,128)(2,1)} %refs_0_.1) | copy-start | bytes 786436
  95.5 1.6 copy-start.10
  129.8 0.9 copy-start.23
  129.8 0.9 copy-start.33
  130.7 36.9 %copy-start.6 = (bf16[128,1024]{1,0:T(8,128)(2,1)}, bf16[128,1024]{1,0:T(8,128)(2,1)S(1)}, u32[]{:S(2)}) copy-start(bf16[128,1024]{1,0:T(8,128)(2,1)S(1)} %multiply_convert_fusion.refs_0_) | copy-start | bytes 786436
  130.7 1.0 copy-start.22
  165.7 1.4 copy-start.8
  169.7 85.8 %copy-start.29 = (f32[128,128]{1,0:T(8,128)S(1)}, f32[128,128]{1,0:T(8,128)}, u32[]{:S(2)}) copy-start(f32[128,128]{1,0:T(8,128)} %copy-done.28) | copy-start | bytes 196612
  169.7 86.0 %copy-start.24 = (f32[128,1024]{1,0:T(8,128)S(1)}, f32[128,1024]{1,0:T(8,128)}, u32[]{:S(2)}) copy-start(f32[128,1024]{1,0:T(8,128)} %copy-done.23) | copy-start | bytes 1572868
  169.7 86.0 %copy-start.30 = (f32[1024]{0:T(1024)S(1)}, f32[1024]{0:T(1024)}, u32[]{:S(2)}) copy-start(f32[1024]{0:T(1024)} %get-tuple-element.74) | copy-start | bytes 12292
  212.1 43.4 %copy-start.32 = (f32[128]{0:T(128)S(1)}, f32[128]{0:T(128)}, u32[]{:S(2)}) copy-start(f32[128]{0:T(128)} %copy-done.31) | copy-start | bytes 1540
  212.1 43.6 %copy-start.34 = (f32[128]{0:T(128)S(1)}, f32[128]{0:T(128)}, u32[]{:S(2)}) copy-start(f32[128]{0:T(128)} %copy-done.33) | copy-start | bytes 1540
  212.1 1.7 copy-start.5
  213.8 41.9 %copy-start.26 = (bf16[1024,32]{1,0:T(8,128)(2,1)S(1)}, bf16[1024,32]{1,0:T(8,128)(2,1)}, u32[]{:S(2)}) copy-start(bf16[1024,32]{1,0:T(8,128)(2,1)} %copy-done.25) | copy-start | bytes 196612
  213.8 42.4 %copy-start.27 = (bf16[128,1024]{1,0:T(8,128)(2,1)S(1)}, bf16[128,1024]{1,0:T(8,128)(2,1)}, u32[]{:S(2)}) copy-start(bf16[128,1024]{1,0:T(8,128)(2,1)} %param.27) | copy-start | bytes 786436
  213.8 42.6 %copy-start.9 = (bf16[1024,1024]{1,0:T(8,128)(2,1)S(1)}, bf16[1024,1024]{1,0:T(8,128)(2,1)}, u32[]{:S(2)}) copy-start(bf16[1024,1024]{1,0:T(8,128)(2,1)} %get-tuple-element.54.refs_2_) | copy-start | bytes 6291460
  256.1 49.2 %copy-start.2 = (f32[1024,128]{1,0:T(8,128)S(1)}, f32[1024,128]{1,0:T(8,128)}, u32[]{:S(2)}) copy-start(f32[1024,128]{1,0:T(8,128)} %copy-done.1) | copy-start | bytes 1572868
  256.2 49.1 %copy-start.16 = (bf16[1024,128]{1,0:T(8,128)(2,1)S(1)}, bf16[1024,128]{1,0:T(8,128)(2,1)}, u32[]{:S(2)}) copy-start(bf16[1024,128]{1,0:T(8,128)(2,1)} %copy-done.15) | copy-start | bytes 786436
  256.2 49.1 %copy-start.18 = (bf16[1024,128]{1,0:T(8,128)(2,1)S(1)}, bf16[1024,128]{1,0:T(8,128)(2,1)}, u32[]{:S(2)}) copy-start(bf16[1024,128]{1,0:T(8,128)(2,1)} %copy-done.17) | copy-start | bytes 786436
  256.2 49.1 %copy-start.20 = (bf16[128,1024]{1,0:T(8,128)(2,1)S(1)}, bf16[128,1024]{1,0:T(8,128)(2,1)}, u32[]{:S(2)}) copy-start(bf16[128,1024]{1,0:T(8,128)(2,1)} %copy-done.19) | copy-start | bytes 786436
  304.0 1.3 copy-start.12
  305.3 16.6 %copy-start.7 = (bf16[128,1024]{1,0:T(8,128)(2,1)S(1)}, bf16[128,1024]{1,0:T(8,128)(2,1)}, u32[]{:S(2)}) copy-start(bf16[128,1024]{1,0:T(8,128)(2,1)} %copy-done.6) | copy-start | bytes 786436
  305.3 16.6 %copy-start.36 = (pred[128]{0:T(512)(128)(4,1)S(1)}, pred[128]{0:T(512)(128)(4,1)}, u32[]{:S(2)}) copy-start(pred[128]{0:T(512)(128)(4,1)} %get-tuple-element.98) | copy-start | bytes 388
  305.3 16.6 %copy-start.37 = (pred[128]{0:T(512)(128)(4,1)S(1)}, pred[128]{0:T(512)(128)(4,1)}, u32[]{:S(2)}) copy-start(pred[128]{0:T(512)(128)(4,1)} %get-tuple-element.99) | copy-start | bytes 388
  322.4 1.6 copy-start.11
  (7 other events, 5.1 us)
Sparse Core Ops, SparseCore 0:
  9.7 64.8 all-gather.1

commit v3 on v2

v3 whole, which is shorter than its diff:
```python
import jax
import jax.numpy as jnp
from jax import lax
from jax.experimental import pallas as pl
from jax.experimental.pallas import tpu as pltpu
from jax.sharding import PartitionSpec as P

MESH = pl.DeviceIdType.MESH
D = 1024
HEAD_DIM = 64
EXPERTS = 32
HIDDEN = 512
GROUP = 1024
ROWS = 128
SLOTS = 352
LOCAL = 4
BLOCK = 64
WIDE = D + 128

eps_norm = 1e-06
rope_base = 10000.0
score_scale = 1.0 / HEAD_DIM
F32 = jnp.float32
BF16 = jnp.bfloat16


def tp_at(along, across):
    tp = lax.axis_index("tp")
    return lax.rem(tp // 2 + along, 4) * 2 + lax.rem(tp + across, 2)


def fsdp_at(along, across):
    fsdp = lax.axis_index("fsdp")
    chip = lax.rem(fsdp // 8 + across, 2) * 4 + lax.rem(fsdp // 2 + along, 4)
    return chip * 2 + lax.rem(fsdp, 2)


def core_partner():
    fsdp = lax.axis_index("fsdp")
    return fsdp // 2 * 2 + 1 - lax.rem(fsdp, 2)


def send(src, dst, send_sem, recv_sem, device):
    copy = pltpu.make_async_remote_copy(
        src_ref=src,
        dst_ref=dst,
        send_sem=send_sem,
        recv_sem=recv_sem,
        device_id=device,
        device_id_type=MESH,
    )
    copy.start()
    return copy


def greet():
    barrier = pltpu.get_barrier_semaphore()
    for place in ((1, 0), (3, 0), (0, 1)):
        for device in ({"tp": tp_at(*place)}, {"fsdp": fsdp_at(*place)}):
            pl.semaphore_signal(barrier, inc=1, device_id=device, device_id_type=MESH)
    pl.semaphore_signal(barrier, inc=1, device_id={"fsdp": core_partner()}, device_id_type=MESH)
    pl.semaphore_wait(barrier, 7)


def dma(count):
    return pltpu.SemaphoreType.DMA((count,))


GATHER = (
    ((0, 0), (0, 1), None),
    ((0, 0), (1, 0), None),
    ((0, 0), (3, 0), None),
    ((0, 1), (1, 0), 0),
    ((0, 1), (3, 0), 0),
    ((3, 0), (1, 0), 1),
    ((1, 1), (3, 0), 4),
)
ARRIVES = ((0, 1), (3, 0), (1, 0), (3, 1), (1, 1), (2, 0), (2, 1))
SUM = (
    ((2, 0), (1, 0), ()),
    ((2, 1), (3, 0), ()),
    ((1, 1), (1, 0), ()),
    ((3, 0), (3, 0), ()),
    ((1, 0), (1, 0), (0,)),
    ((3, 1), (3, 0), (1,)),
    ((0, 1), (0, 1), (2, 5)),
)
LAST = (3, 4, 6)
CORE_ORDER = tuple(block for block, _, _ in SUM) + ((0, 0),)


class GatherTp:
    def __init__(self, rows, columns):
        self.rows = rows
        self.scratch = [dma(7), dma(7), pltpu.SemaphoreType.DMA(())]

    def run(self, src, out, send_sem, recv_sem, own_sem):
        def block(place):
            return out.at[pl.ds(pl.multiple_of(tp_at(*place) * self.rows, self.rows), self.rows)]

        own = pltpu.make_async_copy(src, block((0, 0)), own_sem)
        own.start()
        copies, arrived = [], set()
        for k, (place, target, after) in enumerate(GATHER):
            if after is not None and after not in arrived:
                yield
                copies[after].wait_recv()
                arrived.add(after)
            copies.append(
                send(
                    src if place == (0, 0) else block(place),
                    block(place),
                    send_sem.at[k],
                    recv_sem.at[k],
                    {"tp": tp_at(*target)},
                )
            )
        yield
        for k, copy in enumerate(copies):
            if k not in arrived:
                copy.wait_recv()
            copy.wait_send()
        own.wait()


class SumTp:
    def __init__(self, rows, columns):
        self.rows = rows
        self.scratch = [dma(7), dma(7), pltpu.VMEM((7, rows, columns), BF16)]

    def run(self, src, out, send_sem, recv_sem, landed):
        def first(place):
            return pl.multiple_of(tp_at(*place) * self.rows, self.rows)

        def total(place, others, dst):
            start = first(place)

            @pl.loop(0, self.rows // 16)
            def _(i):
                at = pl.multiple_of(i * 16, 16)
                value = src[pl.ds(pl.multiple_of(start + at, 16), 16), :].astype(F32)
                for k in others:
                    value = value + landed[k, pl.ds(at, 16), :].astype(F32)
                dst[pl.ds(at, 16), :] = value.astype(dst.dtype)

        copies, arrived = [], set()
        for k, (place, target, others) in enumerate(SUM):
            if others:
                yield
                for other in others:
                    copies[other].wait_recv()
                    arrived.add(other)
                part = landed.at[others[0]]
                total(place, others, part)
            else:
                part = src.at[pl.ds(first(place), self.rows)]
            copies.append(
                send(part, landed.at[k], send_sem.at[k], recv_sem.at[k], {"tp": tp_at(*target)})
            )
        yield
        for k in LAST:
            copies[k].wait_recv()
        total((0, 0), LAST, out)
        for copy in copies:
            copy.wait_send()


class GatherFsdp:
    def __init__(self, experts, columns):
        self.scratch = [dma(7), dma(7), dma(8), dma(8), pltpu.SemaphoreType.DMA(())]

    def run(self, src, out, send_sem, recv_sem, core_send, core_recv, own_sem):
        def block(place):
            return out.at[:, pl.ds(pl.multiple_of(fsdp_at(*place) * BLOCK, BLOCK), BLOCK)]

        own = pltpu.make_async_copy(src, block((0, 0)), own_sem)
        own.start()
        copies, arrived, crossed = [], set(), []

        def arrive(k):
            copies[k].wait_recv()
            arrived.add(k)
            here = block(ARRIVES[k])
            crossed.append(
                send(here, here, core_send.at[k], core_recv.at[k], {"fsdp": core_partner()})
            )

        for k, (place, target, after) in enumerate(GATHER):
            if after is not None and after not in arrived:
                yield
                arrive(after)
            copies.append(
                send(
                    src if place == (0, 0) else block(place),
                    block(place),
                    send_sem.at[k],
                    recv_sem.at[k],
                    {"fsdp": fsdp_at(*target)},
                )
            )
        crossed.append(
            send(src, block((0, 0)), core_send.at[7], core_recv.at[7], {"fsdp": core_partner()})
        )
        for k in range(7):
            if k not in arrived:
                yield
                arrive(k)
        yield
        for copy in copies:
            copy.wait_send()
        for copy in crossed:
            copy.wait()
        own.wait()


class SumFsdp:
    def __init__(self, experts, columns, dtype=BF16):
        self.experts = experts
        self.scratch = [
            dma(7),
            dma(7),
            dma(8),
            dma(8),
            dma(8),
            pltpu.VMEM((8, experts, BLOCK, columns), dtype),
            pltpu.VMEM((8, experts, BLOCK, columns), dtype),
            pltpu.VMEM((7, experts, BLOCK, columns), dtype),
        ]

    def run(self, src, out, send_sem, recv_sem, core_send, core_recv, own_sem, own, pair, landed):
        def over_rows(body):
            @pl.loop(0, self.experts * (BLOCK // 16))
            def _(i):
                body(i // (BLOCK // 16), pl.multiple_of(lax.rem(i, BLOCK // 16) * 16, 16))

        crossed, copies, arrived, kept = [], [], set(), []
        mine = lax.rem(lax.axis_index("fsdp"), 2)
        for k, place in enumerate(CORE_ORDER):
            start = pl.multiple_of((fsdp_at(*place) + 1 - 2 * mine) * BLOCK, BLOCK)
            crossed.append(
                send(
                    src.at[:, pl.ds(start, BLOCK)],
                    pair.at[k],
                    core_send.at[k],
                    core_recv.at[k],
                    {"fsdp": core_partner()},
                )
            )
            start = pl.multiple_of(fsdp_at(*place) * BLOCK, BLOCK)
            kept.append(
                pltpu.make_async_copy(src.at[:, pl.ds(start, BLOCK)], own.at[k], own_sem.at[k])
            )
            kept[k].start()
        for k, place in enumerate(CORE_ORDER):
            yield
            others = SUM[k][2] if k < 7 else LAST
            crossed[k].wait_recv()
            for other in others:
                if other not in arrived:
                    copies[other].wait_recv()
                    arrived.add(other)
            kept[k].wait()
            dst = out if k == 7 else pair.at[k]

            def add(expert, at):
                rows = pl.ds(at, 16)
                value = own[k, expert, rows, :].astype(F32) + pair[k, expert, rows, :].astype(F32)
                for other in others:
                    value = value + landed[other, expert, pl.ds(at, 16), :].astype(F32)
                dst[expert, pl.ds(at, 16), :] = value.astype(dst.dtype)

            over_rows(add)
            if k < 7:
                copies.append(
                    send(
                        pair.at[k],
                        landed.at[k],
                        send_sem.at[k],
                        recv_sem.at[k],
                        {"fsdp": fsdp_at(*SUM[k][1])},
                    )
                )
        for copy in copies + crossed:
            copy.wait_send()


class SumAll:
    def __init__(self, columns):
        self.over_fsdp = SumFsdp(1, columns, F32)
        self.scratch = self.over_fsdp.scratch + [
            pltpu.VMEM((1, BLOCK, columns), F32),
            dma(7),
            dma(7),
            pltpu.VMEM((7, 8, columns), F32),
        ]

    def run(self, src, out, *scratch):
        total, send_sem, recv_sem, landed = scratch[-4:]
        yield from self.over_fsdp.run(src, total, *scratch[:-4])

        def own(place):
            return total[0, pl.ds(pl.multiple_of(tp_at(*place) * 8, 8), 8), :]

        copies = []
        for k, (place, target, others) in enumerate(SUM):
            if others:
                yield
                value = own(place)
                for other in others:
                    copies[other].wait_recv()
                    value = value + landed[other]
                landed[others[0]] = value
                part = landed.at[others[0]]
            else:
                part = total.at[0, pl.ds(pl.multiple_of(tp_at(*place) * 8, 8), 8)]
            copies.append(
                send(part, landed.at[k], send_sem.at[k], recv_sem.at[k], {"tp": tp_at(*target)})
            )
        yield
        value = own((0, 0))
        for other in LAST:
            copies[other].wait_recv()
            value = value + landed[other]
        out[...] = value
        for copy in copies:
            copy.wait_send()


def pump(runs):
    for run in list(runs):
        if next(run, "done") == "done":
            runs.remove(run)
    return bool(runs)


def drain(run, behind=(), steps=1):
    for _ in run:
        for _ in range(steps):
            pump(behind)


def run_task(task, scratch, src, out):
    count = len(task.scratch)
    mine, scratch[:] = scratch[:count], scratch[count:]
    return task.run(src, out, *mine)


def dot(a, b, dims=((1,), (0,))):
    return lax.dot_general(a, b, (dims, ((), ())), preferred_element_type=F32)


def lanes(rows):
    return lax.broadcasted_iota(jnp.int32, (rows, 128), 1)


def turn(values):
    low_half = lax.rem(lanes(values.shape[0]), HEAD_DIM) < HEAD_DIM // 2
    return jnp.where(low_half, pltpu.roll(values, 96, 1), pltpu.roll(values, 32, 1))


def both_halves(pair):
    low = lanes(pair.shape[0]) < HEAD_DIM
    other = pltpu.roll(pair, HEAD_DIM, 1)
    return jnp.where(low, pair, other), jnp.where(low, other, pair)


def head_lanes(values, head):
    return jnp.where(lanes(values.shape[0]) // HEAD_DIM == head, values, 0.0)


def doc_of(position, lengths):
    first = lengths[0, 0]
    return jnp.where(position >= first, 1, 0) + jnp.where(position >= first + lengths[0, 1], 1, 0)


def allowed(keys, first, lengths):
    key_at = lax.broadcasted_iota(jnp.int32, (keys, 1), 0)
    query_at = first + lax.broadcasted_iota(jnp.int32, (1, QUERIES), 1)
    return (key_at <= query_at) & (doc_of(key_at, lengths) == doc_of(query_at, lengths))


def inverse_root(values):
    return lax.rsqrt(jnp.mean(values * values, axis=-1, keepdims=True) + eps_norm)


def rms_back(grad_out, unit, inverse, gain):
    grad_unit = grad_out * gain
    return inverse * (grad_unit - unit * jnp.mean(grad_unit * unit, axis=-1, keepdims=True))


def key_tables(cosine, sine):
    key = lanes(cosine.shape[0]) < HEAD_DIM
    return jnp.where(key, cosine, 1.0), jnp.where(key, sine, 0.0)


QUERIES = 256


def attend(x_ref, w_ref, gain_ref, cos_ref, sin_ref, lengths, normed_ref, query_ref, pair_ref, lse_ref, mixed_ref, mixed_t, attended_ref, between):
    @pl.loop(0, GROUP // 128)
    def _(i):
        rows = pl.ds(pl.multiple_of(i * 128, 128), 128)
        x = x_ref[rows, :].astype(F32)
        normed = (x * inverse_root(x) * gain_ref[0:1, :]).astype(BF16)
        normed_ref[rows, :] = normed
        raw = dot(normed, w_ref[0, :, 0:256])
        query, pair = raw[:, 0:128], raw[:, 128:256]
        cosine, sine = cos_ref[rows, :], sin_ref[rows, :]
        query_ref[rows, :] = (query * cosine + turn(query) * sine).astype(BF16)
        cosine, sine = key_tables(cosine, sine)
        pair_ref[rows, :] = (pair * cosine + turn(pair) * sine).astype(BF16)

    between()
    keys, values = both_halves(pair_ref[...].astype(F32))
    keys, values_t = keys.astype(BF16), values.T.astype(BF16)

    for first in range(0, GROUP, QUERIES):
        count = first + QUERIES
        mask = allowed(count, first, lengths)
        for head in range(2):
            query = head_lanes(query_ref[first : first + QUERIES, :].astype(F32), head).astype(BF16)
            scores = dot(keys[:count], query, ((1,), (1,))) * score_scale
            scores = jnp.where(mask, scores, -1e30)
            top = jnp.max(scores, axis=0, keepdims=True)
            raised = jnp.exp(scores - top)
            total = jnp.sum(raised, axis=0, keepdims=True)
            lse_ref[head : head + 1, first : first + QUERIES] = top + jnp.log(total)
            weights = (raised * (1.0 / total)).astype(BF16)
            mixed_t[HEAD_DIM * head : HEAD_DIM * (head + 1), first : first + QUERIES] = dot(
                values_t[HEAD_DIM * head : HEAD_DIM * (head + 1), :count], weights
            )
        between()
    mixed_ref[...] = mixed_t[...].astype(BF16)

    @pl.loop(0, GROUP // 128)
    def _(i):
        at = pl.multiple_of(i * 128, 128)
        mixed = mixed_t[:, pl.ds(at, 128)].T.astype(BF16)
        attended_ref[pl.ds(at, 128), :] = dot(mixed, w_ref[0, :, 256:384], ((1,), (1,))).astype(BF16)


def attend_back(datt_ref, x_ref, w_ref, query_ref, pair_ref, lse_ref, cos_ref, sin_ref, lengths, grad_ref, gain_grad, dmixed_ref, dquery_t, dpair_ref, raw_ref, raw_t, between):
    @pl.loop(0, GROUP // 128)
    def _(i):
        rows = pl.ds(pl.multiple_of(i * 128, 128), 128)
        dmixed_ref[rows, :] = dot(datt_ref[rows, :], w_ref[0, :, 256:384]).astype(BF16)

    keys, values = both_halves(pair_ref[...].astype(F32))
    keys_t = keys.T.astype(BF16)
    keys, values = keys.astype(BF16), values.astype(BF16)
    dpair_ref[...] = jnp.zeros_like(dpair_ref)

    for first in range(0, GROUP, QUERIES):
        count = first + QUERIES
        mask = allowed(count, first, lengths)
        for head in range(2):
            query = head_lanes(query_ref[first : first + QUERIES, :].astype(F32), head).astype(BF16)
            dmixed = head_lanes(dmixed_ref[first : first + QUERIES, :].astype(F32), head).astype(BF16)
            scores = dot(keys[:count], query, ((1,), (1,))) * score_scale
            scores = jnp.where(mask, scores, -1e30)
            weights = jnp.exp(scores - lse_ref[head : head + 1, first : first + QUERIES])
            dweights = dot(values[:count], dmixed, ((1,), (1,)))
            inner = jnp.sum(weights * dweights, axis=0, keepdims=True)
            dscores = (weights * (dweights - inner)).astype(BF16)
            dquery_t[HEAD_DIM * head : HEAD_DIM * (head + 1), first : first + QUERIES] = (
                dot(keys_t[HEAD_DIM * head : HEAD_DIM * (head + 1), :count], dscores) * score_scale
            )
            dpair_ref[0, :count, :] += dot(dscores, query) * score_scale
            dpair_ref[1, :count, :] += dot(weights.astype(BF16), dmixed)
        between()

    gain_grad[...] = jnp.zeros_like(gain_grad)

    @pl.loop(0, GROUP // 128)
    def _(i):
        at = pl.multiple_of(i * 128, 128)
        rows = pl.ds(at, 128)
        dquery = dquery_t[:, rows].T
        dkey, dvalue = dpair_ref[0, rows, :], dpair_ref[1, rows, :]
        dkey = dkey + pltpu.roll(dkey, HEAD_DIM, 1)
        dvalue = dvalue + pltpu.roll(dvalue, HEAD_DIM, 1)
        dpair = jnp.where(lanes(128) < HEAD_DIM, dkey, dvalue)
        cosine, sine = cos_ref[rows, :], sin_ref[rows, :]
        dquery = dquery * cosine + turn(dquery * sine)
        cosine, sine = key_tables(cosine, sine)
        dpair = dpair * cosine + turn(dpair * sine)
        raw_ref[rows, 0:128] = dquery.astype(BF16)
        raw_ref[rows, 128:256] = dpair.astype(BF16)
        raw_t[0:128, rows] = dquery.T.astype(BF16)
        raw_t[128:256, rows] = dpair.T.astype(BF16)
        dnormed = dot(raw_ref[rows, :], w_ref[0, :, 0:256], ((1,), (1,)))
        grad_ref[rows, :] = dnormed.astype(BF16)
        x = x_ref[rows, :].astype(F32)
        gain_grad[...] += jnp.sum(dnormed * (x * inverse_root(x)), axis=0, keepdims=True)


HEAD_TASKS = (
    GatherTp(ROWS, D),
    GatherFsdp(1, 512),
    GatherFsdp(LOCAL, HIDDEN),
    GatherFsdp(LOCAL, HIDDEN),
    GatherFsdp(LOCAL, HIDDEN),
    GatherTp(ROWS, D),
    SumTp(ROWS, D),
    GatherTp(ROWS, D),
)


def head_body(
    lengths, x_ref, small_ref, gate_ref, up_ref, down_ref, dy_ref, routes_ref, cos_ref, sin_ref,
    x_all, w_all, gate_all, up_all, down_all, dy_all, tokens,
    normed_ref, query_ref, pair_ref, lse_ref, mixed_ref, middle_ref, own_ref, chosen_ref, rank_ref, rank_t, gains_ref,
    mixed_t, attended_ref, summed, *scratch,
):
    scratch = list(scratch)
    greet()
    pairs = (
        (x_ref, x_all), (small_ref, w_all), (gate_ref, gate_all), (up_ref, up_all), (down_ref, down_all),
        (dy_ref, dy_all), (attended_ref, summed), (own_ref, tokens),
    )
    x_run, w_run, gate_run, up_run, down_run, dy_run, sum_run, token_run = [
        run_task(task, scratch, *pair) for task, pair in zip(HEAD_TASKS, pairs)
    ]
    front = [x_run, w_run]
    pump(front)

    lane = lanes(GROUP)
    chosen = lane == routes_ref[:, 0:1]
    for k in range(1, 8):
        chosen = chosen | (lane == routes_ref[:, k : k + 1])
    chosen = jnp.where(chosen, 1.0, 0.0)
    chosen_ref[...] = chosen
    pump(front)
    chosen = chosen.astype(BF16)
    for i in range(4):
        rows = slice(256 * i, 256 * (i + 1))
        later = 256 * i + lax.broadcasted_iota(jnp.int32, (256, GROUP), 0)
        until = jnp.where(later >= lax.broadcasted_iota(jnp.int32, (256, GROUP), 1), 1.0, 0.0)
        running = dot(until.astype(BF16), chosen)
        rank = jnp.where(chosen_ref[rows, :] > 0.0, running - 1.0, -1.0)
        rank_ref[rows, :] = rank
        rank_t[:, rows] = rank.T
    drain(w_run)
    behind = [gate_run, up_run, down_run]
    pump(behind)
    gains_ref[...] = w_all[0, :, 384:512].astype(F32).T[32:40, :]
    drain(x_run)
    pump(behind)
    far = [dy_run]
    pump(far)
    calls = [0]

    def between():
        calls[0] += 1
        if calls[0] in (3, 4, 5):
            pump(far)
        if calls[0] in (2, 5):
            pump(behind)

    attend(
        x_all, w_all, gains_ref, cos_ref, sin_ref, lengths,
        normed_ref, query_ref, pair_ref, lse_ref, mixed_ref, mixed_t, attended_ref, between,
    )
    next(sum_run)
    while pump(far):
        pass
    drain(sum_run, behind)
    middle = x_ref[...].astype(F32) + summed[...]
    middle_ref[...] = middle
    own_ref[...] = (middle * inverse_root(middle) * gains_ref[1:2, :]).astype(BF16)
    drain(token_run, behind, 2)
    while pump(behind):
        pass


def head(lengths, x, small, gate, up, down, dy, routes, cosine, sine):
    def shape(*dims, dtype=BF16):
        return jax.ShapeDtypeStruct(dims, dtype)

    vmem = pl.BlockSpec(memory_space=pltpu.VMEM)
    far = pl.BlockSpec(memory_space=pl.ANY)
    weight = shape(LOCAL, D, HIDDEN)
    return pl.pallas_call(
        head_body,
        name="head",
        out_shape=[
            shape(GROUP, D),
            shape(1, D, 512),
            weight,
            weight,
            weight,
            shape(GROUP, D),
            shape(GROUP, D),
            shape(GROUP, D),
            shape(GROUP, 128),
            shape(GROUP, 128),
            shape(2, GROUP, dtype=F32),
            shape(128, GROUP),
            shape(ROWS, D, dtype=F32),
            shape(ROWS, D),
            shape(GROUP, 128, dtype=F32),
            shape(GROUP, 128, dtype=F32),
            shape(128, GROUP, dtype=F32),
            shape(8, D, dtype=F32),
        ],
        in_specs=[pl.BlockSpec(memory_space=pltpu.SMEM)] + [vmem] * 9,
        out_specs=[vmem] * 2 + [far] * 3 + [vmem] * 13,
        scratch_shapes=[
            pltpu.VMEM((128, GROUP), F32),
            pltpu.VMEM((GROUP, D), BF16),
            pltpu.VMEM((ROWS, D), F32),
        ]
        + [buffer for task in HEAD_TASKS for buffer in task.scratch],
        compiler_params=pltpu.CompilerParams(
            collective_id=1, has_side_effects=True, vmem_limit_bytes=56 * 2**20
        ),
    )(lengths, x, small, gate, up, down, dy, routes, cosine, sine)


TAIL_TASKS = (
    SumTp(ROWS, WIDE),
    SumFsdp(LOCAL, HIDDEN),
    SumFsdp(LOCAL, HIDDEN),
    SumFsdp(LOCAL, HIDDEN),
    GatherTp(ROWS, D),
    SumTp(ROWS, D),
    SumTp(ROWS, D),
    SumFsdp(1, 384),
    SumAll(128),
)


def tail_body(
    lengths, grads_ref, combined_ref, gate_part, up_part, down_part,
    x_ref, dy_ref, middle_ref, own_ref, chosen_ref, gains_ref,
    x_all, w_all, normed_ref, query_ref, pair_ref, lse_ref, mixed_ref, cos_ref, sin_ref,
    outputs_ref, input_grad, small_grad, attention_grad, gate_grad, up_grad, down_grad,
    grads_sum, moe_sum, datt_own, datt_all, dmiddle_ref, dnormed_part, dnormed_sum, weights_part, small_part, gain_grads,
    gain_row, dmixed_ref, dquery_t, dpair_ref, raw_ref, raw_t, *scratch,
):
    scratch = list(scratch)
    greet()
    pairs = (
        (grads_ref, grads_sum), (gate_part, gate_grad), (up_part, up_grad), (down_part, down_grad),
        (datt_own, datt_all), (combined_ref, moe_sum), (dnormed_part, dnormed_sum),
        (weights_part, attention_grad), (small_part, small_grad),
    )
    grads_run, gate_run, up_run, down_run, datt_run, moe_run, dnormed_run, weights_run, small_run = [
        run_task(task, scratch, *pair) for task, pair in zip(TAIL_TASKS, pairs)
    ]
    behind = [gate_run, up_run, down_run]
    next(grads_run)
    pump(behind)
    drain(grads_run, behind, 2)

    middle = middle_ref[...]
    inverse = inverse_root(middle)
    unit = middle * inverse
    router = w_all[0, :, 384:512]
    own_rows = pl.ds(pl.multiple_of(lax.axis_index("tp") * ROWS, ROWS), ROWS)
    logits = jnp.where(chosen_ref[own_rows, :] > 0.0, dot(own_ref[...], router), -1e30)
    raised = jnp.exp(logits - jnp.max(logits, axis=-1, keepdims=True))
    gates = raised / jnp.sum(raised, axis=-1, keepdims=True)
    dgates = grads_sum[:, D:WIDE]
    dlogits = gates * (dgates - jnp.sum(gates * dgates, axis=-1, keepdims=True))
    dlogits = dlogits.astype(BF16)
    dtokens = grads_sum[:, 0:D] + dot(dlogits, router, ((1,), (1,)))
    dmiddle = dy_ref[...].astype(F32) + rms_back(dtokens, unit, inverse, gains_ref[1:2, :])
    dmiddle_ref[...] = dmiddle
    datt_own[...] = dmiddle.astype(BF16)
    next(datt_run)
    small_part[0] = dot(own_ref[...], dlogits, ((0,), (0,)))
    gain_grads[...] = jnp.zeros_like(gain_grads)
    gain_grads[EXPERTS : EXPERTS + 1, :] = jnp.sum(dtokens * unit, axis=0, keepdims=True)
    drain(datt_run, behind)

    far = [moe_run]
    pump(far)
    calls = [0]

    def between():
        calls[0] += 1
        if calls[0] in (2, 4):
            pump(far)
        if calls[0] in (1, 3):
            pump(behind)

    attend_back(
        datt_all, x_all, w_all, query_ref, pair_ref, lse_ref, cos_ref, sin_ref, lengths,
        dnormed_part, gain_row, dmixed_ref, dquery_t, dpair_ref, raw_ref, raw_t, between,
    )
    next(dnormed_run)
    gain_grads[EXPERTS + 1 : EXPERTS + 2, :] = gain_row[...]
    small_part[0] += gain_grads[...].T
    next(small_run)

    @pl.loop(0, D // 256)
    def _(i):
        at = pl.ds(pl.multiple_of(i * 256, 256), 256)
        weights_part[0, at, 0:256] = dot(raw_t[...], normed_ref[:, at]).T.astype(BF16)
        weights_part[0, at, 256:384] = dot(mixed_ref[...], datt_all[:, at]).T.astype(BF16)

    last = [dnormed_run, weights_run, small_run] + far + behind
    while pump(last):
        pass
    outputs_ref[...] = (middle_ref[...] + moe_sum[...]).astype(BF16)
    x = x_ref[...].astype(F32)
    inverse = inverse_root(x)
    input_grad[...] = dmiddle_ref[...] + rms_back(dnormed_sum[...], x * inverse, inverse, gains_ref[0:1, :])


def tail(*arrays):
    def shape(*dims, dtype=F32):
        return jax.ShapeDtypeStruct(dims, dtype)

    vmem = pl.BlockSpec(memory_space=pltpu.VMEM)
    far = pl.BlockSpec(memory_space=pl.ANY)
    weight = shape(LOCAL, BLOCK, HIDDEN)
    return pl.pallas_call(
        tail_body,
        name="tail",
        out_shape=[
            shape(ROWS, D, dtype=BF16),
            shape(ROWS, D),
            shape(8, 128),
            shape(1, BLOCK, 384),
            weight,
            weight,
            weight,
        ],
        in_specs=[pl.BlockSpec(memory_space=pltpu.SMEM)] + [vmem] * 2 + [far] * 3 + [vmem] * 15,
        out_specs=[vmem] * 7,
        scratch_shapes=[
            pltpu.VMEM((ROWS, WIDE), F32),
            pltpu.VMEM((ROWS, D), F32),
            pltpu.VMEM((ROWS, D), BF16),
            pltpu.VMEM((GROUP, D), BF16),
            pltpu.VMEM((ROWS, D), F32),
            pltpu.VMEM((GROUP, D), BF16),
            pltpu.VMEM((ROWS, D), F32),
            pltpu.VMEM((1, D, 384), BF16),
            pltpu.VMEM((1, D, 128), F32),
            pltpu.VMEM((128, D), F32),
            pltpu.VMEM((1, D), F32),
            pltpu.VMEM((GROUP, 128), BF16),
            pltpu.VMEM((128, GROUP), F32),
            pltpu.VMEM((2, GROUP, 128), F32),
            pltpu.VMEM((GROUP, 256), BF16),
            pltpu.VMEM((256, GROUP), BF16),
        ]
        + [buffer for task in TAIL_TASKS for buffer in task.scratch],
        compiler_params=pltpu.CompilerParams(
            collective_id=2, has_side_effects=True, vmem_limit_bytes=62 * 2**20
        ),
    )(*arrays)


def experts_body(
    tp_ref, tokens_ref, dy_ref, router_ref, chosen_ref, rank_ref, rank_t,
    gate_ref, up_ref, down_ref,
    combined_ref, grad_ref, gate_grad, up_grad, down_grad, combined_sum, grad_sum, gate_sum, gates_ref,
):
    step = pl.program_id(0)
    lane = lax.broadcasted_iota(jnp.int32, (1, 128), 1)

    @pl.when(step == 0)
    def _():
        combined_sum[...] = jnp.zeros_like(combined_sum)
        grad_sum[...] = jnp.zeros_like(grad_sum)
        gate_sum[...] = jnp.zeros_like(gate_sum)
        logits = jnp.where(chosen_ref[...] > 0.0, dot(tokens_ref[...], router_ref[0]), -1e30)
        raised = jnp.exp(logits - jnp.max(logits, axis=-1, keepdims=True))
        gates = raised / jnp.sum(raised, axis=-1, keepdims=True)
        high = gates.astype(BF16)
        gates_ref[:, 0:128] = high
        gates_ref[:, 128:256] = (gates - high.astype(F32)).astype(BF16)

    expert = tp_ref[0] * LOCAL + step
    expert_lane = lane == expert
    slot = lax.broadcasted_iota(jnp.int32, (SLOTS, GROUP), 0)
    rank_row = rank_t[pl.ds(expert, 1), :].astype(jnp.int32)
    rank_column = jnp.sum(jnp.where(expert_lane, rank_ref[...], 0.0), axis=1, keepdims=True)
    take = jnp.where(slot == rank_row, 1.0, 0.0).astype(BF16)
    slot_gates = dot(take, gates_ref[...])
    slot_gates = slot_gates[:, 0:128] + slot_gates[:, 128:256]
    slot_gate = jnp.sum(jnp.where(expert_lane, slot_gates, 0.0), axis=1, keepdims=True)
    picked = dot(take, tokens_ref[...]).astype(BF16)
    dy = dot(take, dy_ref[...]).astype(BF16)

    gate_part = dot(picked, gate_ref[0])
    up_part = dot(picked, up_ref[0])
    sigmoid = 1.0 / (1.0 + jnp.exp(-gate_part))
    silu = gate_part * sigmoid
    hidden = silu * up_part
    dhidden = dot(dy, down_ref[0])
    dgate = jnp.sum(hidden * dhidden, axis=1, keepdims=True)
    weighted = (hidden * slot_gate).astype(BF16)
    dhidden = dhidden * slot_gate
    dgate_part = (dhidden * up_part * (sigmoid * (1.0 + gate_part * (1.0 - sigmoid)))).astype(BF16)
    dup_part = (dhidden * silu).astype(BF16)

    down_grad[0] = dot(dy, weighted, ((0,), (0,))).astype(BF16)
    gate_grad[0] = dot(picked, dgate_part, ((0,), (0,))).astype(BF16)
    up_grad[0] = dot(picked, dup_part, ((0,), (0,))).astype(BF16)

    out = dot(weighted, down_ref[0], ((1,), (1,))).astype(BF16)
    dpicked = dot(dgate_part, gate_ref[0], ((1,), (1,)))
    dpicked = (dpicked + dot(dup_part, up_ref[0], ((1,), (1,)))).astype(BF16)
    dgate = jnp.where(expert_lane, dgate, 0.0).astype(BF16)

    give = jnp.where(
        lax.broadcasted_iota(jnp.int32, (GROUP, SLOTS), 1) == rank_column.astype(jnp.int32), 1.0, 0.0
    ).astype(BF16)
    combined_sum[...] += dot(give, out)
    grad_sum[...] += dot(give, dpicked)
    gate_sum[...] += dot(give, dgate)

    @pl.when(step == LOCAL - 1)
    def _():
        combined_ref[...] = combined_sum[...].astype(BF16)
        grad_ref[:, 0:D] = grad_sum[...].astype(BF16)
        grad_ref[:, D:WIDE] = gate_sum[...].astype(BF16)


def experts(tp, tokens, dy, router, chosen, rank, rank_t, gate, up, down):
    def whole(*shape):
        return pl.BlockSpec(shape, lambda i, tp: (0,) * len(shape))

    def own(*shape):
        return pl.BlockSpec((1,) + shape, lambda i, tp: (i,) + (0,) * len(shape))

    weight = jax.ShapeDtypeStruct((LOCAL, D, HIDDEN), BF16)
    return pl.pallas_call(
        experts_body,
        name="experts",
        grid_spec=pltpu.PrefetchScalarGridSpec(
            num_scalar_prefetch=1,
            grid=(LOCAL,),
            in_specs=[
                whole(GROUP, D),
                whole(GROUP, D),
                pl.BlockSpec((1, D, 128), lambda i, tp: (0, 0, 3)),
                whole(GROUP, 128),
                whole(GROUP, 128),
                whole(128, GROUP),
                own(D, HIDDEN),
                own(D, HIDDEN),
                own(D, HIDDEN),
            ],
            out_specs=[
                whole(GROUP, D),
                whole(GROUP, WIDE),
                own(D, HIDDEN),
                own(D, HIDDEN),
                own(D, HIDDEN),
            ],
            scratch_shapes=[
                pltpu.VMEM((GROUP, D), F32),
                pltpu.VMEM((GROUP, D), F32),
                pltpu.VMEM((GROUP, 128), F32),
                pltpu.VMEM((GROUP, 256), BF16),
            ],
        ),
        out_shape=[
            jax.ShapeDtypeStruct((GROUP, D), BF16),
            jax.ShapeDtypeStruct((GROUP, WIDE), BF16),
            weight,
            weight,
            weight,
        ],
        compiler_params=pltpu.CompilerParams(vmem_limit_bytes=60 * 2**20),
    )(tp, tokens, dy, router, chosen, rank, rank_t, gate, up, down)


def rope_tables(lengths):
    ends = jnp.cumsum(lengths)
    positions = jnp.arange(GROUP, dtype=jnp.int32)
    starts = jnp.where(positions >= ends[1], ends[1], jnp.where(positions >= ends[0], ends[0], 0))
    lane = jnp.arange(128, dtype=jnp.int32)
    frequency = rope_base ** (-(lane % 32).astype(F32) * 2.0 / HEAD_DIM)
    angles = (positions - starts).astype(F32)[:, None] * frequency[None, :]
    sine = jnp.sin(angles)
    return jnp.cos(angles), jnp.where(lane % 64 < 32, -sine, sine)


def per_device(
    inputs,
    lengths,
    routes,
    attn_gain,
    query_weight,
    key_weight,
    value_weight,
    output_weight,
    moe_gain,
    router_weight,
    gate_weight,
    up_weight,
    down_weight,
    cotangent,
):
    tp = lax.axis_index("tp")
    small = jnp.concatenate(
        [
            query_weight,
            key_weight,
            value_weight,
            output_weight.T,
            router_weight,
            attn_gain[:, None],
            moe_gain[:, None],
            jnp.zeros((BLOCK, 128 - EXPERTS - 2), BF16),
        ],
        axis=1,
    )
    cosine, sine = rope_tables(lengths[0])
    (
        x_all, w_all, gate_all, up_all, down_all, dy_all, tokens,
        normed, query, pair, lse, mixed, middle, own, chosen, rank, rank_t, gains,
    ) = head(
        lengths, inputs, small[None], gate_weight, up_weight, down_weight.transpose(0, 2, 1),
        cotangent, routes, cosine, sine,
    )
    combined, grads, gate_part, up_part, down_part = experts(
        tp[None], tokens, dy_all, w_all, chosen, rank, rank_t, gate_all, up_all, down_all
    )
    outputs, input_grad, small_grad, attention_grad, gate_grad, up_grad, down_grad = tail(
        lengths, grads, combined, gate_part, up_part, down_part,
        inputs, cotangent, middle, own, chosen, gains,
        x_all, w_all, normed, query, pair, lse, mixed, cosine, sine,
    )
    attention_grad = attention_grad[0]
    return (
        outputs,
        input_grad,
        small_grad[:, EXPERTS + 1],
        attention_grad[:, 0:128],
        attention_grad[:, 128:192],
        attention_grad[:, 192:256],
        attention_grad[:, 256:384].T,
        small_grad[:, EXPERTS],
        small_grad[:, :EXPERTS],
        gate_grad,
        up_grad,
        down_grad.transpose(0, 2, 1),
    )


def solution(mesh):
    return jax.shard_map(
        per_device,
        mesh=mesh,
        in_specs=(
            P(("fsdp", "tp"), None),
            P("fsdp", None),
            P("fsdp", None),
            P("fsdp"),
            P("fsdp", "tp"),
            P("fsdp", "tp"),
            P("fsdp", "tp"),
            P("tp", "fsdp"),
            P("fsdp"),
            P("fsdp", None),
            P("tp", "fsdp", None),
            P("tp", "fsdp", None),
            P("tp", None, "fsdp"),
            P(("fsdp", "tp"), None),
        ),
        out_specs=(
            P(("fsdp", "tp"), None),
            P(("fsdp", "tp"), None),
            P(("fsdp", "tp")),
            P("fsdp", "tp"),
            P("fsdp", "tp"),
            P("fsdp", "tp"),
            P("tp", "fsdp"),
            P(("fsdp", "tp")),
            P(("fsdp", "tp"), None),
            P("tp", "fsdp", None),
            P("tp", "fsdp", None),
            P("tp", None, "fsdp"),
        ),
        check_vma=False,
    )
```

time: 399 us -> 327 us (0.82)
  Pallas kernels: 336 us -> 298 us
  between operations: 14.6 us -> 0.69 us
  other arithmetic: 15 us -> 5.19 us
  local copies, waits for them, and re-layouts: 29.4 us -> 19.9 us
    pallas_call x8 -> x2, Pallas kernels: 294 us -> 256 us  [the longest x1 143 us: tail(): pl.pallas_call(tail_body, name='tail', out_shape=[shape(ROWS, D, dtype=BF...]
    unnamed x83 -> x10, local copies, waits for them, and re-layouts: 21.2 us -> 11.9 us
    reduce_or x1 -> x0, other arithmetic: 5.79 us -> none  [per_device(): chosen = jnp.any(routes[:, :, None] == expert_ids[None, None, :], axis=1)]
  transfers between devices with their start and end apart: 1 -> 0, of which waited for: 0 -> 0; matrix products, arithmetic and copies ran while one was open for 6% -> 0% of each run, Pallas kernels for 32% -> 0%
where the time goes in v3:
time: 327 us; the launch traced here: 324 us
  Pallas kernels  298 us (91%)
  local copies, waits for them, and re-layouts  19.9 us (6%)
  other arithmetic  5.19 us (2%)
    pallas_call x1, Pallas kernels, tail(): pl.pallas_call(tail_body, name='tail', out_shape=[shape(ROWS, D, dtype=BF...  143 us
    pallas_call x1, Pallas kernels, head(): pl.pallas_call(head_body, name='head', out_shape=[shape(GROUP, D), shape(...  113 us
    pallas_call x1, Pallas kernels, experts(): pl.pallas_call(experts_body, name='experts', grid_spec=pltpu.PrefetchScal...  42.2 us
    unnamed x10, local copies, waits for them, and re-layouts  11.9 us

profile of v3, /device:TPU:0, one launch (start us, length us, event | category | flops | bytes accessed | tf_op | source)
XLA Modules:
  0.0 324.3 jit_solution(14558241278122925468)
XLA Ops:
  0.6 0.8 reduce-window.4
  1.5 0.6 fusion.6
  2.1 1.3 subtract_convert_fusion
  3.4 0.8 copy.31
  4.1 0.8 copy.32
  4.9 0.8 copy.30
  5.7 1.5 concatenate.3
  7.2 1.8 copy.33.routes_ref
  9.0 3.1 negate_select_fusion
  12.0 113.4 %head.1 = (bf16[1024,1024]{1,0:T(8,128)(2,1)}, bf16[1,1024,512]{2,1,0:T(8,128)(2,1)}, bf16[4,1024,512]{2,1,0:T(8,128)(2,1)}, bf16[4,1024,512]{2,1,0:T(8,128)(2,1...) custom-call(s32[1,3]{1,0:T(1,128)} %lengths.3, ...), custom_call_target="tpu_custom_call" | custom-call | tf_op jit(solution)/shard_map/head/pallas_call | solution.py:583
  125.4 42.2 %experts.1 = (bf16[1024,1024]{1,0:T(8,128)(2,1)}, bf16[1024,1152]{1,0:T(8,128)(2,1)}, bf16[4,1024,512]{2,1,0:T(8,128)(2,1)}, bf16[4,1024,512]{2,1,0:T(8,128)(2,1)}, bf16[4,1024,512]{2,1,0:T(8,128)(2,1)}) custom-call(s32[1]{0:T(128)} %bitcast.tp_ref, bf16[1024,1024]{1,0:T(8,128)(2,1)} %get-tuple-element.42.tokens_ref, ...), custom_call_target="tpu_custom_call" | custom-call | tf_op jit(solution)/shard_map/experts/pallas_call | solution.py:833
  167.7 142.8 %tail.1 = (bf16[128,1024]{1,0:T(8,128)(2,1)}, f32[128,1024]{1,0:T(8,128)}, f32[8,128]{1,0:T(8,128)}, f32[1,64,384]{2,1,0:T(8,128)}, f32[4,64,512]{2,1,0:T(8,128)...) custom-call(s32[1,3]{1,0:T(1,128)} %lengths.3, bf16[1024,1152]{1,0:T(8,128)(2,1)} %get-tuple-element.51.grads_ref, ...), custom_call_target="tpu_custom_call" | custom-call | tf_op jit(solution)/shard_map/tail/pallas_call | solution.py:719
  310.5 0.0 copy-start
  310.5 1.5 slice_reduce_fusion
  312.0 1.4 slice_bitcast_fusion
  313.4 1.5 fusion.5
  314.9 1.7 copy.40
  316.6 1.9 copy.41
  318.5 1.3 copy.42
  319.7 1.9 copy.43
  321.6 1.9 copy.44
  323.5 0.0 copy-done
  323.5 0.8 copy.45
  (3 shorter events, 0.0 us)
Async XLA Ops:
  310.5 13.0 %copy-start = (f32[4,64,512]{2,1,0:T(8,128)S(1)}, f32[4,64,512]{2,1,0:T(8,128)}, u32[]{:S(2)}) copy-start(f32[4,64,512]{2,1,0:T(8,128)} %get-tuple-element.71) | copy-start | bytes 1572868

commit v4 on v3

--- a/solution.py
+++ b/solution.py
@@ -1,3 +1,5 @@
+import math
+
 import jax
 import jax.numpy as jnp
 from jax import lax
@@ -284,6 +286,58 @@
             copy.wait_send()
 
 
+class SumChips:
+    def __init__(self, kind):
+        self.kind = kind
+        self.scratch = [
+            dma(7),
+            dma(7),
+            dma(4),
+            pltpu.VMEM((4, LOCAL, BLOCK, HIDDEN), BF16),
+            pltpu.VMEM((7, LOCAL, BLOCK, HIDDEN), BF16),
+        ]
+
+    def run(self, src, out, send_sem, recv_sem, own_sem, own, landed):
+        def block(place):
+            return src.at[:, self.kind, fsdp_at(*place) // 2]
+
+        def total(k, others, dst):
+            @pl.loop(0, LOCAL * (BLOCK // 16))
+            def _(i):
+                expert, at = i // (BLOCK // 16), pl.multiple_of(lax.rem(i, BLOCK // 16) * 16, 16)
+                value = own[k, expert, pl.ds(at, 16), :].astype(F32)
+                for other in others:
+                    value = value + landed[other, expert, pl.ds(at, 16), :].astype(F32)
+                dst[expert, pl.ds(at, 16), :] = value.astype(dst.dtype)
+
+        copies, arrived, kept = [], set(), []
+        for k, (place, target, others) in enumerate(SUM):
+            if others:
+                yield
+                for other in others:
+                    copies[other].wait_recv()
+                kept[k - 4].wait()
+                part = landed.at[others[0]]
+                total(k - 4, others, part)
+            else:
+                part = block(place)
+            copies.append(
+                send(part, landed.at[k], send_sem.at[k], recv_sem.at[k], {"fsdp": fsdp_at(*target)})
+            )
+            if k == 3:
+                for place in [place for place, _, _ in SUM[4:]] + [(0, 0)]:
+                    j = len(kept)
+                    kept.append(pltpu.make_async_copy(block(place), own.at[j], own_sem.at[j]))
+                    kept[j].start()
+        yield
+        for k in LAST:
+            copies[k].wait_recv()
+        kept[3].wait()
+        total(3, LAST, out)
+        for copy in copies:
+            copy.wait_send()
+
+
 class SumAll:
     def __init__(self, columns):
         self.over_fsdp = SumFsdp(1, columns, F32)
@@ -507,9 +561,9 @@
 
 
 def head_body(
-    lengths, x_ref, small_ref, gate_ref, up_ref, down_ref, dy_ref, routes_ref, cos_ref, sin_ref,
+    lengths, x_ref, small_ref, gate_ref, up_ref, down_ref, dy_ref, routes_ref,
     x_all, w_all, gate_all, up_all, down_all, dy_all, tokens,
-    normed_ref, query_ref, pair_ref, lse_ref, mixed_ref, middle_ref, own_ref, chosen_ref, rank_ref, rank_t, gains_ref,
+    normed_ref, query_ref, pair_ref, lse_ref, mixed_ref, middle_ref, own_ref, chosen_ref, rank_ref, rank_t, gains_ref, cos_ref, sin_ref,
     mixed_t, attended_ref, summed, *scratch,
 ):
     scratch = list(scratch)
@@ -525,9 +579,10 @@
     pump(front)
 
     lane = lanes(GROUP)
-    chosen = lane == routes_ref[:, 0:1]
+    routes = routes_ref[...].astype(F32).T.astype(jnp.int32)
+    chosen = lane == routes[:, 0:1]
     for k in range(1, 8):
-        chosen = chosen | (lane == routes_ref[:, k : k + 1])
+        chosen = chosen | (lane == routes[:, k : k + 1])
     chosen = jnp.where(chosen, 1.0, 0.0)
     chosen_ref[...] = chosen
     pump(front)
@@ -540,6 +595,16 @@
         rank = jnp.where(chosen_ref[rows, :] > 0.0, running - 1.0, -1.0)
         rank_ref[rows, :] = rank
         rank_t[:, rows] = rank.T
+    pump(front)
+    position = lax.broadcasted_iota(jnp.int32, (GROUP, 1), 0)
+    ends = (lengths[0, 0], lengths[0, 0] + lengths[0, 1])
+    start = jnp.where(position >= ends[1], ends[1], jnp.where(position >= ends[0], ends[0], 0))
+    half = lax.rem(lane[0:1], HEAD_DIM // 2).astype(F32)
+    frequency = jnp.exp(half * (-2.0 / HEAD_DIM * math.log(rope_base)))
+    angles = (position - start).astype(F32) * frequency
+    cos_ref[...] = jnp.cos(angles)
+    sine = jnp.sin(angles)
+    sin_ref[...] = jnp.where(lax.rem(lane, HEAD_DIM) < HEAD_DIM // 2, -sine, sine)
     drain(w_run)
     behind = [gate_run, up_run, down_run]
     pump(behind)
@@ -564,7 +629,9 @@
     next(sum_run)
     while pump(far):
         pass
-    drain(sum_run, behind)
+    drain(sum_run)
+    pump(behind)
+    pump(behind)
     middle = x_ref[...].astype(F32) + summed[...]
     middle_ref[...] = middle
     own_ref[...] = (middle * inverse_root(middle) * gains_ref[1:2, :]).astype(BF16)
@@ -573,7 +640,7 @@
         pass
 
 
-def head(lengths, x, small, gate, up, down, dy, routes, cosine, sine):
+def head(lengths, x, small, gate, up, down, dy, routes):
     def shape(*dims, dtype=BF16):
         return jax.ShapeDtypeStruct(dims, dtype)
 
@@ -602,9 +669,11 @@
             shape(GROUP, 128, dtype=F32),
             shape(128, GROUP, dtype=F32),
             shape(8, D, dtype=F32),
+            shape(GROUP, 128, dtype=F32),
+            shape(GROUP, 128, dtype=F32),
         ],
-        in_specs=[pl.BlockSpec(memory_space=pltpu.SMEM)] + [vmem] * 9,
-        out_specs=[vmem] * 2 + [far] * 3 + [vmem] * 13,
+        in_specs=[pl.BlockSpec(memory_space=pltpu.SMEM)] + [vmem] * 7,
+        out_specs=[vmem] * 2 + [far] * 3 + [vmem] * 15,
         scratch_shapes=[
             pltpu.VMEM((128, GROUP), F32),
             pltpu.VMEM((GROUP, D), BF16),
@@ -614,14 +683,14 @@
         compiler_params=pltpu.CompilerParams(
             collective_id=1, has_side_effects=True, vmem_limit_bytes=56 * 2**20
         ),
-    )(lengths, x, small, gate, up, down, dy, routes, cosine, sine)
+    )(lengths, x, small, gate, up, down, dy, routes)
 
 
 TAIL_TASKS = (
     SumTp(ROWS, WIDE),
-    SumFsdp(LOCAL, HIDDEN),
-    SumFsdp(LOCAL, HIDDEN),
-    SumFsdp(LOCAL, HIDDEN),
+    SumChips(0),
+    SumChips(1),
+    SumChips(2),
     GatherTp(ROWS, D),
     SumTp(ROWS, D),
     SumTp(ROWS, D),
@@ -631,7 +700,7 @@
 
 
 def tail_body(
-    lengths, grads_ref, combined_ref, gate_part, up_part, down_part,
+    lengths, grads_ref, combined_ref, pairs_ref,
     x_ref, dy_ref, middle_ref, own_ref, chosen_ref, gains_ref,
     x_all, w_all, normed_ref, query_ref, pair_ref, lse_ref, mixed_ref, cos_ref, sin_ref,
     outputs_ref, input_grad, small_grad, attention_grad, gate_grad, up_grad, down_grad,
@@ -641,7 +710,7 @@
     scratch = list(scratch)
     greet()
     pairs = (
-        (grads_ref, grads_sum), (gate_part, gate_grad), (up_part, up_grad), (down_part, down_grad),
+        (grads_ref, grads_sum), (pairs_ref, gate_grad), (pairs_ref, up_grad), (pairs_ref, down_grad),
         (datt_own, datt_all), (combined_ref, moe_sum), (dnormed_part, dnormed_sum),
         (weights_part, attention_grad), (small_part, small_grad),
     )
@@ -651,7 +720,7 @@
     behind = [gate_run, up_run, down_run]
     next(grads_run)
     pump(behind)
-    drain(grads_run, behind, 2)
+    drain(grads_run)
 
     middle = middle_ref[...]
     inverse = inverse_root(middle)
@@ -669,10 +738,12 @@
     dmiddle_ref[...] = dmiddle
     datt_own[...] = dmiddle.astype(BF16)
     next(datt_run)
+    pump(behind)
+    pump(behind)
     small_part[0] = dot(own_ref[...], dlogits, ((0,), (0,)))
     gain_grads[...] = jnp.zeros_like(gain_grads)
     gain_grads[EXPERTS : EXPERTS + 1, :] = jnp.sum(dtokens * unit, axis=0, keepdims=True)
-    drain(datt_run, behind)
+    drain(datt_run)
 
     far = [moe_run]
     pump(far)
@@ -682,7 +753,7 @@
         calls[0] += 1
         if calls[0] in (2, 4):
             pump(far)
-        if calls[0] in (1, 3):
+        if calls[0] == 2:
             pump(behind)
 
     attend_back(
@@ -728,7 +799,7 @@
             weight,
             weight,
         ],
-        in_specs=[pl.BlockSpec(memory_space=pltpu.SMEM)] + [vmem] * 2 + [far] * 3 + [vmem] * 15,
+        in_specs=[pl.BlockSpec(memory_space=pltpu.SMEM)] + [vmem] * 2 + [far] + [vmem] * 15,
         out_specs=[vmem] * 7,
         scratch_shapes=[
             pltpu.VMEM((ROWS, WIDE), F32),
@@ -756,15 +827,31 @@
 
 
 def experts_body(
-    tp_ref, tokens_ref, dy_ref, router_ref, chosen_ref, rank_ref, rank_t,
+    tokens_ref, dy_ref, router_ref, chosen_ref, rank_ref, rank_t,
     gate_ref, up_ref, down_ref,
-    combined_ref, grad_ref, gate_grad, up_grad, down_grad, combined_sum, grad_sum, gate_sum, gates_ref,
+    combined_ref, grad_ref, pair_ref,
+    combined_sum, grad_sum, gate_sum, gates_ref, parts, got, send_sem, recv_sem,
 ):
     step = pl.program_id(0)
     lane = lax.broadcasted_iota(jnp.int32, (1, 128), 1)
+    core = lax.rem(lax.axis_index("fsdp"), 2)
+
+    def across(expert):
+        slot = lax.rem(expert, 2)
+        return pltpu.make_async_remote_copy(
+            src_ref=parts.at[slot, :, :, 1 - core],
+            dst_ref=got.at[expert],
+            send_sem=send_sem.at[slot],
+            recv_sem=recv_sem.at[expert],
+            device_id={"fsdp": core_partner()},
+            device_id_type=MESH,
+        )
 
     @pl.when(step == 0)
     def _():
+        barrier = pltpu.get_barrier_semaphore()
+        pl.semaphore_signal(barrier, inc=1, device_id={"fsdp": core_partner()}, device_id_type=MESH)
+        pl.semaphore_wait(barrier, 1)
         combined_sum[...] = jnp.zeros_like(combined_sum)
         grad_sum[...] = jnp.zeros_like(grad_sum)
         gate_sum[...] = jnp.zeros_like(gate_sum)
@@ -775,112 +862,167 @@
         gates_ref[:, 0:128] = high
         gates_ref[:, 128:256] = (gates - high.astype(F32)).astype(BF16)
 
-    expert = tp_ref[0] * LOCAL + step
-    expert_lane = lane == expert
-    slot = lax.broadcasted_iota(jnp.int32, (SLOTS, GROUP), 0)
-    rank_row = rank_t[pl.ds(expert, 1), :].astype(jnp.int32)
-    rank_column = jnp.sum(jnp.where(expert_lane, rank_ref[...], 0.0), axis=1, keepdims=True)
-    take = jnp.where(slot == rank_row, 1.0, 0.0).astype(BF16)
-    slot_gates = dot(take, gates_ref[...])
-    slot_gates = slot_gates[:, 0:128] + slot_gates[:, 128:256]
-    slot_gate = jnp.sum(jnp.where(expert_lane, slot_gates, 0.0), axis=1, keepdims=True)
-    picked = dot(take, tokens_ref[...]).astype(BF16)
-    dy = dot(take, dy_ref[...]).astype(BF16)
-
-    gate_part = dot(picked, gate_ref[0])
-    up_part = dot(picked, up_ref[0])
-    sigmoid = 1.0 / (1.0 + jnp.exp(-gate_part))
-    silu = gate_part * sigmoid
-    hidden = silu * up_part
-    dhidden = dot(dy, down_ref[0])
-    dgate = jnp.sum(hidden * dhidden, axis=1, keepdims=True)
-    weighted = (hidden * slot_gate).astype(BF16)
-    dhidden = dhidden * slot_gate
-    dgate_part = (dhidden * up_part * (sigmoid * (1.0 + gate_part * (1.0 - sigmoid)))).astype(BF16)
-    dup_part = (dhidden * silu).astype(BF16)
-
-    down_grad[0] = dot(dy, weighted, ((0,), (0,))).astype(BF16)
-    gate_grad[0] = dot(picked, dgate_part, ((0,), (0,))).astype(BF16)
-    up_grad[0] = dot(picked, dup_part, ((0,), (0,))).astype(BF16)
-
-    out = dot(weighted, down_ref[0], ((1,), (1,))).astype(BF16)
-    dpicked = dot(dgate_part, gate_ref[0], ((1,), (1,)))
-    dpicked = (dpicked + dot(dup_part, up_ref[0], ((1,), (1,)))).astype(BF16)
-    dgate = jnp.where(expert_lane, dgate, 0.0).astype(BF16)
-
-    give = jnp.where(
-        lax.broadcasted_iota(jnp.int32, (GROUP, SLOTS), 1) == rank_column.astype(jnp.int32), 1.0, 0.0
-    ).astype(BF16)
-    combined_sum[...] += dot(give, out)
-    grad_sum[...] += dot(give, dpicked)
-    gate_sum[...] += dot(give, dgate)
-
-    @pl.when(step == LOCAL - 1)
+    @pl.when(step < LOCAL)
+    def _():
+        expert = lax.axis_index("tp") * LOCAL + step
+        expert_lane = lane == expert
+        slot = lax.broadcasted_iota(jnp.int32, (SLOTS, GROUP), 0)
+        rank_row = rank_t[pl.ds(expert, 1), :].astype(jnp.int32)
+        rank_column = jnp.sum(jnp.where(expert_lane, rank_ref[...], 0.0), axis=1, keepdims=True)
+        take = jnp.where(slot == rank_row, 1.0, 0.0).astype(BF16)
+        slot_gates = dot(take, gates_ref[...])
+        slot_gates = slot_gates[:, 0:128] + slot_gates[:, 128:256]
+        slot_gate = jnp.sum(jnp.where(expert_lane, slot_gates, 0.0), axis=1, keepdims=True)
+        picked = dot(take, tokens_ref[...]).astype(BF16)
+        dy = dot(take, dy_ref[...]).astype(BF16)
+
+        gate_part = dot(picked, gate_ref[0])
+        up_part = dot(picked, up_ref[0])
+        sigmoid = 1.0 / (1.0 + jnp.exp(-gate_part))
+        silu = gate_part * sigmoid
+        hidden = silu * up_part
+        dhidden = dot(dy, down_ref[0])
+        dgate = jnp.sum(hidden * dhidden, axis=1, keepdims=True)
+        weighted = (hidden * slot_gate).astype(BF16)
+        dhidden = dhidden * slot_gate
+        dgate_part = (dhidden * up_part * (sigmoid * (1.0 + gate_part * (1.0 - sigmoid)))).astype(BF16)
+        dup_part = (dhidden * silu).astype(BF16)
+
+        @pl.when(step >= 2)
+        def _():
+            across(step - 2).wait_send()
+
+        slot_now = lax.rem(step, 2)
+        for k, (left, right) in enumerate(((picked, dgate_part), (picked, dup_part), (dy, weighted))):
+            grad = dot(left, right, ((0,), (0,))).astype(BF16)
+            parts[slot_now, k] = grad.reshape(8, 2, BLOCK, HIDDEN)
+        across(step).start()
+
+        out = dot(weighted, down_ref[0], ((1,), (1,))).astype(BF16)
+        dpicked = dot(dgate_part, gate_ref[0], ((1,), (1,)))
+        dpicked = (dpicked + dot(dup_part, up_ref[0], ((1,), (1,)))).astype(BF16)
+        dgate = jnp.where(expert_lane, dgate, 0.0).astype(BF16)
+
+        give = jnp.where(
+            lax.broadcasted_iota(jnp.int32, (GROUP, SLOTS), 1) == rank_column.astype(jnp.int32), 1.0, 0.0
+        ).astype(BF16)
+        combined_sum[...] += dot(give, out)
+        grad_sum[...] += dot(give, dpicked)
+        gate_sum[...] += dot(give, dgate)
+
+    @pl.when(step == LOCAL)
     def _():
         combined_ref[...] = combined_sum[...].astype(BF16)
         grad_ref[:, 0:D] = grad_sum[...].astype(BF16)
         grad_ref[:, D:WIDE] = gate_sum[...].astype(BF16)
 
-
-def experts(tp, tokens, dy, router, chosen, rank, rank_t, gate, up, down):
+    @pl.when(step >= 1)
+    def _():
+        across(step - 1).wait_recv()
+        slot_before = lax.rem(step - 1, 2)
+
+        @pl.loop(0, 24)
+        def _(i):
+            kind, chip = i // 8, lax.rem(i, 8)
+            total = parts[slot_before, kind, chip, core].astype(F32) + got[step - 1, kind, chip].astype(F32)
+            pair_ref[0, kind, chip] = total.astype(BF16)
+
+    @pl.when(step == LOCAL)
+    def _():
+        for expert in (LOCAL - 2, LOCAL - 1):
+            across(expert).wait_send()
+
+
+def experts(tokens, dy, router, chosen, rank, rank_t, gate, up, down):
     def whole(*shape):
-        return pl.BlockSpec(shape, lambda i, tp: (0,) * len(shape))
+        return pl.BlockSpec(shape, lambda i: (0,) * len(shape))
 
     def own(*shape):
-        return pl.BlockSpec((1,) + shape, lambda i, tp: (i,) + (0,) * len(shape))
-
-    weight = jax.ShapeDtypeStruct((LOCAL, D, HIDDEN), BF16)
+        return pl.BlockSpec((1,) + shape, lambda i: (jnp.minimum(i, LOCAL - 1),) + (0,) * len(shape))
+
     return pl.pallas_call(
         experts_body,
         name="experts",
-        grid_spec=pltpu.PrefetchScalarGridSpec(
-            num_scalar_prefetch=1,
-            grid=(LOCAL,),
-            in_specs=[
-                whole(GROUP, D),
-                whole(GROUP, D),
-                pl.BlockSpec((1, D, 128), lambda i, tp: (0, 0, 3)),
-                whole(GROUP, 128),
-                whole(GROUP, 128),
-                whole(128, GROUP),
-                own(D, HIDDEN),
-                own(D, HIDDEN),
-                own(D, HIDDEN),
-            ],
-            out_specs=[
-                whole(GROUP, D),
-                whole(GROUP, WIDE),
-                own(D, HIDDEN),
-                own(D, HIDDEN),
-                own(D, HIDDEN),
-            ],
-            scratch_shapes=[
-                pltpu.VMEM((GROUP, D), F32),
-                pltpu.VMEM((GROUP, D), F32),
-                pltpu.VMEM((GROUP, 128), F32),
-                pltpu.VMEM((GROUP, 256), BF16),
-            ],
-        ),
+        grid=(LOCAL + 1,),
+        in_specs=[
+            whole(GROUP, D),
+            whole(GROUP, D),
+            pl.BlockSpec((1, D, 128), lambda i: (0, 0, 3)),
+            whole(GROUP, 128),
+            whole(GROUP, 128),
+            whole(128, GROUP),
+            own(D, HIDDEN),
+            own(D, HIDDEN),
+            own(D, HIDDEN),
+        ],
+        out_specs=[
+            whole(GROUP, D),
+            whole(GROUP, WIDE),
+            pl.BlockSpec((1, 3, 8, BLOCK, HIDDEN), lambda i: (jnp.maximum(i - 1, 0), 0, 0, 0, 0)),
+        ],
+        scratch_shapes=[
+            pltpu.VMEM((GROUP, D), F32),
+            pltpu.VMEM((GROUP, D), F32),
+            pltpu.VMEM((GROUP, 128), F32),
+            pltpu.VMEM((GROUP, 256), BF16),
+            pltpu.VMEM((2, 3, 8, 2, BLOCK, HIDDEN), BF16),
+            pltpu.VMEM((LOCAL, 3, 8, BLOCK, HIDDEN), BF16),
+            dma(2),
+            dma(LOCAL),
+        ],
         out_shape=[
             jax.ShapeDtypeStruct((GROUP, D), BF16),
             jax.ShapeDtypeStruct((GROUP, WIDE), BF16),
-            weight,
-            weight,
-            weight,
+            jax.ShapeDtypeStruct((LOCAL, 3, 8, BLOCK, HIDDEN), BF16),
         ],
-        compiler_params=pltpu.CompilerParams(vmem_limit_bytes=60 * 2**20),
-    )(tp, tokens, dy, router, chosen, rank, rank_t, gate, up, down)
-
-
-def rope_tables(lengths):
-    ends = jnp.cumsum(lengths)
-    positions = jnp.arange(GROUP, dtype=jnp.int32)
-    starts = jnp.where(positions >= ends[1], ends[1], jnp.where(positions >= ends[0], ends[0], 0))
-    lane = jnp.arange(128, dtype=jnp.int32)
-    frequency = rope_base ** (-(lane % 32).astype(F32) * 2.0 / HEAD_DIM)
-    angles = (positions - starts).astype(F32)[:, None] * frequency[None, :]
-    sine = jnp.sin(angles)
-    return jnp.cos(angles), jnp.where(lane % 64 < 32, -sine, sine)
+        compiler_params=pltpu.CompilerParams(
+            collective_id=3, has_side_effects=True, vmem_limit_bytes=60 * 2**20
+        ),
+    )(tokens, dy, router, chosen, rank, rank_t, gate, up, down)
+
+
+def finish_body(*refs):
+    outputs, input_grad, small, attention, gate, up, down = refs[:7]
+    outs = refs[7:]
+    outs[0][...] = outputs[...]
+    outs[1][...] = input_grad[...]
+    outs[2][...] = attention[0, :, 0:128]
+    outs[3][...] = attention[0, :, 128:192]
+    outs[4][...] = attention[0, :, 192:256]
+    outs[5][...] = attention[0, :, 256:384].T
+    outs[6][...] = small[:, 0:EXPERTS]
+    columns = small[...].T
+    outs[7][...] = columns[EXPERTS + 1 : EXPERTS + 2, :]
+    outs[8][...] = columns[EXPERTS : EXPERTS + 1, :]
+    outs[9][...] = gate[...]
+    outs[10][...] = up[...]
+    outs[11][...] = down[...]
+
+
+def finish(*arrays):
+    def shape(*dims, dtype=F32):
+        return jax.ShapeDtypeStruct(dims, dtype)
+
+    vmem = pl.BlockSpec(memory_space=pltpu.VMEM)
+    return pl.pallas_call(
+        finish_body,
+        name="finish",
+        out_shape=[
+            shape(ROWS, D, dtype=BF16),
+            shape(ROWS, D),
+            shape(BLOCK, 128),
+            shape(BLOCK, BLOCK),
+            shape(BLOCK, BLOCK),
+            shape(128, BLOCK),
+            shape(8, EXPERTS),
+            shape(1, 8),
+            shape(1, 8),
+        ]
+        + [shape(LOCAL, BLOCK, HIDDEN)] * 3,
+        in_specs=[vmem] * 7,
+        out_specs=[vmem] * 12,
+        compiler_params=pltpu.CompilerParams(vmem_limit_bytes=32 * 2**20),
+    )(*arrays)
 
 
 def per_device(
@@ -899,7 +1041,6 @@
     down_weight,
     cotangent,
 ):
-    tp = lax.axis_index("tp")
     small = jnp.concatenate(
         [
             query_weight,
@@ -913,33 +1054,35 @@
         ],
         axis=1,
     )
-    cosine, sine = rope_tables(lengths[0])
     (
         x_all, w_all, gate_all, up_all, down_all, dy_all, tokens,
-        normed, query, pair, lse, mixed, middle, own, chosen, rank, rank_t, gains,
+        normed, query, pair, lse, mixed, middle, own, chosen, rank, rank_t, gains, cosine, sine,
     ) = head(
         lengths, inputs, small[None], gate_weight, up_weight, down_weight.transpose(0, 2, 1),
-        cotangent, routes, cosine, sine,
+        cotangent, routes.T,
     )
-    combined, grads, gate_part, up_part, down_part = experts(
-        tp[None], tokens, dy_all, w_all, chosen, rank, rank_t, gate_all, up_all, down_all
+    combined, grads, pairs = experts(
+        tokens, dy_all, w_all, chosen, rank, rank_t, gate_all, up_all, down_all
     )
-    outputs, input_grad, small_grad, attention_grad, gate_grad, up_grad, down_grad = tail(
-        lengths, grads, combined, gate_part, up_part, down_part,
+    results = tail(
+        lengths, grads, combined, pairs,
         inputs, cotangent, middle, own, chosen, gains,
         x_all, w_all, normed, query, pair, lse, mixed, cosine, sine,
     )
-    attention_grad = attention_grad[0]
+    (
+        outputs, input_grad, query_grad, key_grad, value_grad, output_grad, router_grad, attn_gain_grad, moe_gain_grad,
+        gate_grad, up_grad, down_grad,
+    ) = finish(*results)
     return (
         outputs,
         input_grad,
-        small_grad[:, EXPERTS + 1],
-        attention_grad[:, 0:128],
-        attention_grad[:, 128:192],
-        attention_grad[:, 192:256],
-        attention_grad[:, 256:384].T,
-        small_grad[:, EXPERTS],
-        small_grad[:, :EXPERTS],
+        attn_gain_grad.reshape(8),
+        query_grad,
+        key_grad,
+        value_grad,
+        output_grad,
+        moe_gain_grad.reshape(8),
+        router_grad,
         gate_grad,
         up_grad,
         down_grad.transpose(0, 2, 1),

time: 327 us -> 293 us (0.90)
  Pallas kernels: 298 us -> 279 us
  local copies, waits for them, and re-layouts: 19.9 us -> 11.2 us
  other arithmetic: 5.19 us -> 0 us
    pallas_call x1, Pallas kernels: 143 us -> 117 us  [tail(): pl.pallas_call(tail_body, name='tail', out_shape=[shape(ROWS, D, dtype=BF...]
    pallas_call x1 -> x2, Pallas kernels: 42.2 us -> 49.5 us  [the longest x1 48 us: experts(): pl.pallas_call(experts_body, name='experts', grid=(LOCAL + 1,), in_specs=...]
    unnamed x10 -> x16, local copies, waits for them, and re-layouts: 11.9 us -> 8.16 us
    slice x3 -> x0, local copies, waits for them, and re-layouts: 3.6 us -> none  [the longest x1 1.53 us: per_device(): attention_grad[:, 192:256]]
where the time goes in v4:
time: 293 us; the launch traced here: 291 us
  Pallas kernels  279 us (95%)
  local copies, waits for them, and re-layouts  11.2 us (4%)
    pallas_call x1, Pallas kernels, tail(): pl.pallas_call(tail_body, name='tail', out_shape=[shape(ROWS, D, dtype=BF...  117 us
    pallas_call x1, Pallas kernels, head(): pl.pallas_call(head_body, name='head', out_shape=[shape(GROUP, D), shape(...  113 us
    pallas_call x1, Pallas kernels, experts(): pl.pallas_call(experts_body, name='experts', grid=(LOCAL + 1,), in_specs=...  48 us
    unnamed x16, local copies, waits for them, and re-layouts  8.16 us

profile of v4, /device:TPU:0, one launch (start us, length us, event | category | flops | bytes accessed | tf_op | source)
XLA Modules:
  0.0 291.3 jit_solution(16408568638308042834)
XLA Ops:
  0.6 0.8 copy.27
  1.4 0.8 copy.28
  2.2 0.8 copy.26
  3.0 1.5 concatenate.3
  4.5 112.9 %head.1 = (bf16[1024,1024]{1,0:T(8,128)(2,1)}, bf16[1,1024,512]{2,1,0:T(8,128)(2,1)}, bf16[4,1024,512]{2,1,0:T(8,128)(2,1)}, bf16[4,1024,512]{2,1,0:T(8,128)(2,1...) custom-call(s32[1,3]{1,0:T(1,128)} %lengths.3, ...), custom_call_target="tpu_custom_call" | custom-call | tf_op jit(solution)/shard_map/head/pallas_call | solution.py:650
  117.4 48.0 %experts.1 = (bf16[1024,1024]{1,0:T(8,128)(2,1)}, bf16[1024,1152]{1,0:T(8,128)(2,1)}, bf16[4,3,8,64,512]{4,3,2,1,0:T(8,128)(2,1)}) custom-call(bf16[1024,1024]{1,0:T(8,128)(2,1)} %get-tuple-element.54.tokens_ref, bf16[1024,1024]{1,0:T(8,128)(2,1)} %get-tuple-element.55.dy_ref, bf16[1,1024,512]{2,1,0:T(8,128)(2,1)} %get-tuple-element.56.router_ref.w_all, ...), custom_call_target="tpu_custom_call" | custom-call | tf_op jit(solution)/shard_map/experts/pallas_call | solution.py:943
  165.4 117.0 %tail.1 = (bf16[128,1024]{1,0:T(8,128)(2,1)}, f32[128,1024]{1,0:T(8,128)}, f32[8,128]{1,0:T(8,128)}, f32[1,64,384]{2,1,0:T(8,128)}, f32[4,64,512]{2,1,0:T(8,128)...) custom-call(s32[1,3]{1,0:T(1,128)} %lengths.3, bf16[1024,1152]{1,0:T(8,128)(2,1)} %get-tuple-element.63.grads_ref, ...), custom_call_target="tpu_custom_call" | custom-call | tf_op jit(solution)/shard_map/tail/pallas_call | solution.py:790
  282.4 0.0 copy-start
  282.4 1.0 copy-done
  283.5 0.0 copy-start.1
  283.5 1.0 copy-done.1
  284.5 0.0 copy-start.2
  284.5 1.0 copy-done.2
  285.5 0.0 copy-start.3
  285.5 1.0 copy-done.3
  286.6 0.0 copy-start.4
  286.6 0.9 copy-done.4
  287.5 0.0 copy-start.5
  287.5 0.9 copy-done.5
  288.4 0.0 copy-start.6
  288.4 0.7 copy-done.6
  289.1 1.5 finish.1
  290.6 0.7 copy.29
  (1 shorter events, 0.0 us)
Async XLA Ops:
  282.4 1.0 copy-start
  283.5 1.0 copy-start.1
  284.5 1.0 copy-start.2
  285.5 1.0 copy-start.3
  286.6 0.9 copy-start.4
  287.5 0.9 copy-start.5
  288.4 0.7 copy-start.6

commit v5 on v4

--- a/solution.py
+++ b/solution.py
@@ -1,3 +1,4 @@
+import functools
 import math
 
 import jax
@@ -15,6 +16,7 @@
 GROUP = 1024
 ROWS = 128
 SLOTS = 352
+PLACES = 384
 LOCAL = 4
 BLOCK = 64
 WIDE = D + 128
@@ -57,17 +59,18 @@
 
 def greet():
     barrier = pltpu.get_barrier_semaphore()
-    for place in ((1, 0), (3, 0), (0, 1)):
+    for place in EVERY:
         for device in ({"tp": tp_at(*place)}, {"fsdp": fsdp_at(*place)}):
             pl.semaphore_signal(barrier, inc=1, device_id=device, device_id_type=MESH)
     pl.semaphore_signal(barrier, inc=1, device_id={"fsdp": core_partner()}, device_id_type=MESH)
-    pl.semaphore_wait(barrier, 7)
+    pl.semaphore_wait(barrier, 15)
 
 
 def dma(count):
     return pltpu.SemaphoreType.DMA((count,))
 
 
+EVERY = ((2, 0), (2, 1), (1, 1), (3, 1), (1, 0), (3, 0), (0, 1))
 GATHER = (
     ((0, 0), (0, 1), None),
     ((0, 0), (1, 0), None),
@@ -88,7 +91,6 @@
     ((0, 1), (0, 1), (2, 5)),
 )
 LAST = (3, 4, 6)
-CORE_ORDER = tuple(block for block, _, _ in SUM) + ((0, 0),)
 
 
 class GatherTp:
@@ -165,6 +167,24 @@
         total((0, 0), LAST, out)
         for copy in copies:
             copy.wait_send()
+
+
+class ExchangeTp:
+    def __init__(self):
+        self.scratch = [dma(7), dma(7), pltpu.SemaphoreType.DMA(())]
+
+    def run(self, block, place, send_sem, recv_sem, own_sem):
+        here = lax.axis_index("tp")
+        copies = [
+            send(block(peer), place(here), send_sem.at[k], recv_sem.at[k], {"tp": peer})
+            for k, peer in enumerate(tp_at(*step) for step in EVERY)
+        ]
+        own = pltpu.make_async_copy(block(here), place(here), own_sem)
+        own.start()
+        yield
+        for copy in copies:
+            copy.wait()
+        own.wait()
 
 
 class GatherFsdp:
@@ -216,73 +236,36 @@
 
 
 class SumFsdp:
-    def __init__(self, experts, columns, dtype=BF16):
-        self.experts = experts
-        self.scratch = [
-            dma(7),
-            dma(7),
-            dma(8),
-            dma(8),
-            dma(8),
-            pltpu.VMEM((8, experts, BLOCK, columns), dtype),
-            pltpu.VMEM((8, experts, BLOCK, columns), dtype),
-            pltpu.VMEM((7, experts, BLOCK, columns), dtype),
-        ]
-
-    def run(self, src, out, send_sem, recv_sem, core_send, core_recv, own_sem, own, pair, landed):
-        def over_rows(body):
-            @pl.loop(0, self.experts * (BLOCK // 16))
-            def _(i):
-                body(i // (BLOCK // 16), pl.multiple_of(lax.rem(i, BLOCK // 16) * 16, 16))
-
-        crossed, copies, arrived, kept = [], [], set(), []
-        mine = lax.rem(lax.axis_index("fsdp"), 2)
-        for k, place in enumerate(CORE_ORDER):
-            start = pl.multiple_of((fsdp_at(*place) + 1 - 2 * mine) * BLOCK, BLOCK)
-            crossed.append(
-                send(
-                    src.at[:, pl.ds(start, BLOCK)],
-                    pair.at[k],
-                    core_send.at[k],
-                    core_recv.at[k],
-                    {"fsdp": core_partner()},
-                )
+    def __init__(self, columns, dtype):
+        blocks = pltpu.VMEM((8, BLOCK, columns), dtype)
+        self.scratch = [dma(7), dma(7), dma(2), blocks, blocks]
+
+    def run(self, src, out, send_sem, recv_sem, core_sem, pair, landed):
+        core = lax.rem(lax.axis_index("fsdp"), 2)
+        across = send(
+            src.at[:, 1 - core], pair, core_sem.at[0], core_sem.at[1], {"fsdp": core_partner()}
+        )
+        yield
+        across.wait_recv()
+
+        @pl.loop(0, 8)
+        def _(chip):
+            pair[chip] = (src[chip, core].astype(F32) + pair[chip].astype(F32)).astype(pair.dtype)
+
+        copies = []
+        for k, place in enumerate(EVERY):
+            device = fsdp_at(*place)
+            copies.append(
+                send(pair.at[device // 2], landed.at[k], send_sem.at[k], recv_sem.at[k], {"fsdp": device})
             )
-            start = pl.multiple_of(fsdp_at(*place) * BLOCK, BLOCK)
-            kept.append(
-                pltpu.make_async_copy(src.at[:, pl.ds(start, BLOCK)], own.at[k], own_sem.at[k])
-            )
-            kept[k].start()
-        for k, place in enumerate(CORE_ORDER):
-            yield
-            others = SUM[k][2] if k < 7 else LAST
-            crossed[k].wait_recv()
-            for other in others:
-                if other not in arrived:
-                    copies[other].wait_recv()
-                    arrived.add(other)
-            kept[k].wait()
-            dst = out if k == 7 else pair.at[k]
-
-            def add(expert, at):
-                rows = pl.ds(at, 16)
-                value = own[k, expert, rows, :].astype(F32) + pair[k, expert, rows, :].astype(F32)
-                for other in others:
-                    value = value + landed[other, expert, pl.ds(at, 16), :].astype(F32)
-                dst[expert, pl.ds(at, 16), :] = value.astype(dst.dtype)
-
-            over_rows(add)
-            if k < 7:
-                copies.append(
-                    send(
-                        pair.at[k],
-                        landed.at[k],
-                        send_sem.at[k],
-                        recv_sem.at[k],
-                        {"fsdp": fsdp_at(*SUM[k][1])},
-                    )
-                )
-        for copy in copies + crossed:
+        yield
+        value = pair[lax.axis_index("fsdp") // 2].astype(F32)
+        for k, copy in enumerate(copies):
+            copy.wait_recv()
+            value = value + landed[k].astype(F32)
+        out[...] = value
+        across.wait_send()
+        for copy in copies:
             copy.wait_send()
 
 
@@ -340,9 +323,9 @@
 
 class SumAll:
     def __init__(self, columns):
-        self.over_fsdp = SumFsdp(1, columns, F32)
+        self.over_fsdp = SumFsdp(columns, F32)
         self.scratch = self.over_fsdp.scratch + [
-            pltpu.VMEM((1, BLOCK, columns), F32),
+            pltpu.VMEM((BLOCK, columns), F32),
             dma(7),
             dma(7),
             pltpu.VMEM((7, 8, columns), F32),
@@ -352,32 +335,21 @@
         total, send_sem, recv_sem, landed = scratch[-4:]
         yield from self.over_fsdp.run(src, total, *scratch[:-4])
 
-        def own(place):
-            return total[0, pl.ds(pl.multiple_of(tp_at(*place) * 8, 8), 8), :]
+        def rows(tp):
+            return pl.ds(pl.multiple_of(tp * 8, 8), 8)
 
         copies = []
-        for k, (place, target, others) in enumerate(SUM):
-            if others:
-                yield
-                value = own(place)
-                for other in others:
-                    copies[other].wait_recv()
-                    value = value + landed[other]
-                landed[others[0]] = value
-                part = landed.at[others[0]]
-            else:
-                part = total.at[0, pl.ds(pl.multiple_of(tp_at(*place) * 8, 8), 8)]
+        for k, place in enumerate(EVERY):
+            peer = tp_at(*place)
             copies.append(
-                send(part, landed.at[k], send_sem.at[k], recv_sem.at[k], {"tp": tp_at(*target)})
+                send(total.at[rows(peer)], landed.at[k], send_sem.at[k], recv_sem.at[k], {"tp": peer})
             )
         yield
-        value = own((0, 0))
-        for other in LAST:
-            copies[other].wait_recv()
-            value = value + landed[other]
+        value = total[rows(lax.axis_index("tp")), :]
+        for k, copy in enumerate(copies):
+            copy.wait()
+            value = value + landed[k]
         out[...] = value
-        for copy in copies:
-            copy.wait_send()
 
 
 def pump(runs):
@@ -393,6 +365,10 @@
             pump(behind)
 
 
+def part(ref, index):
+    return ref.at[pl.ds(pl.multiple_of(index * ROWS, ROWS), ROWS)]
+
+
 def run_task(task, scratch, src, out):
     count = len(task.scratch)
     mine, scratch[:] = scratch[:count], scratch[count:]
@@ -450,7 +426,7 @@
 QUERIES = 256
 
 
-def attend(x_ref, w_ref, gain_ref, cos_ref, sin_ref, lengths, normed_ref, query_ref, pair_ref, lse_ref, mixed_ref, mixed_t, attended_ref, between):
+def attend(x_ref, w_ref, gain_ref, cos_ref, sin_ref, lengths, normed_ref, query_ref, pair_ref, lse_ref, mixed_ref, mixed_t, mixed_rows, between):
     @pl.loop(0, GROUP // 128)
     def _(i):
         rows = pl.ds(pl.multiple_of(i * 128, 128), 128)
@@ -485,20 +461,10 @@
             )
         between()
     mixed_ref[...] = mixed_t[...].astype(BF16)
-
-    @pl.loop(0, GROUP // 128)
-    def _(i):
-        at = pl.multiple_of(i * 128, 128)
-        mixed = mixed_t[:, pl.ds(at, 128)].T.astype(BF16)
-        attended_ref[pl.ds(at, 128), :] = dot(mixed, w_ref[0, :, 256:384], ((1,), (1,))).astype(BF16)
-
-
-def attend_back(datt_ref, x_ref, w_ref, query_ref, pair_ref, lse_ref, cos_ref, sin_ref, lengths, grad_ref, gain_grad, dmixed_ref, dquery_t, dpair_ref, raw_ref, raw_t, between):
-    @pl.loop(0, GROUP // 128)
-    def _(i):
-        rows = pl.ds(pl.multiple_of(i * 128, 128), 128)
-        dmixed_ref[rows, :] = dot(datt_ref[rows, :], w_ref[0, :, 256:384]).astype(BF16)
-
+    mixed_rows[...] = mixed_t[...].T.astype(BF16)
+
+
+def attend_back(x_ref, w_ref, query_ref, pair_ref, lse_ref, cos_ref, sin_ref, lengths, grad_ref, gain_grad, dmixed_ref, dquery_t, dpair_ref, raw_ref, raw_t, between):
     keys, values = both_halves(pair_ref[...].astype(F32))
     keys_t = keys.T.astype(BF16)
     keys, values = keys.astype(BF16), values.astype(BF16)
@@ -555,24 +521,33 @@
     GatherFsdp(LOCAL, HIDDEN),
     GatherFsdp(LOCAL, HIDDEN),
     GatherTp(ROWS, D),
-    SumTp(ROWS, D),
+    GatherTp(D, ROWS),
+    ExchangeTp(),
     GatherTp(ROWS, D),
 )
 
 
 def head_body(
     lengths, x_ref, small_ref, gate_ref, up_ref, down_ref, dy_ref, routes_ref,
-    x_all, w_all, gate_all, up_all, down_all, dy_all, tokens,
-    normed_ref, query_ref, pair_ref, lse_ref, mixed_ref, middle_ref, own_ref, chosen_ref, rank_ref, rank_t, gains_ref, cos_ref, sin_ref,
-    mixed_t, attended_ref, summed, *scratch,
+    x_out, w_out, gate_all, up_all, down_all, dy_out, tokens,
+    normed_out, query_out, pair_out, lse_ref, mixed_ref, middle_ref, own_ref, chosen_out, rank_out, rank_t_out, gains_ref, cos_out, sin_out, output_out,
+    x_all, w_all, dy_all, normed_ref, query_ref, pair_ref, chosen_ref, rank_ref, rank_t, cos_ref, sin_ref, store_sem,
+    mixed_t, mixed_rows, mixed_own, output_all, *scratch,
 ):
     scratch = list(scratch)
+    stores = []
+
+    def store(src, dst):
+        stores.append(pltpu.make_async_copy(src, dst, store_sem.at[len(stores)]))
+        stores[-1].start()
+
     greet()
     pairs = (
         (x_ref, x_all), (small_ref, w_all), (gate_ref, gate_all), (up_ref, up_all), (down_ref, down_all),
-        (dy_ref, dy_all), (attended_ref, summed), (own_ref, tokens),
+        (dy_ref, dy_all), (w_all.at[0, :, 256:384], output_all),
+        (functools.partial(part, mixed_rows), lambda tp: mixed_own.at[tp]), (own_ref, tokens),
     )
-    x_run, w_run, gate_run, up_run, down_run, dy_run, sum_run, token_run = [
+    x_run, w_run, gate_run, up_run, down_run, dy_run, output_run, mixed_run, token_run = [
         run_task(task, scratch, *pair) for task, pair in zip(HEAD_TASKS, pairs)
     ]
     front = [x_run, w_run]
@@ -605,39 +580,57 @@
     cos_ref[...] = jnp.cos(angles)
     sine = jnp.sin(angles)
     sin_ref[...] = jnp.where(lax.rem(lane, HEAD_DIM) < HEAD_DIM // 2, -sine, sine)
+    for pair in ((chosen_ref, chosen_out), (rank_ref, rank_out), (rank_t, rank_t_out), (cos_ref, cos_out), (sin_ref, sin_out)):
+        store(*pair)
     drain(w_run)
     behind = [gate_run, up_run, down_run]
     pump(behind)
+    store(w_all, w_out)
     gains_ref[...] = w_all[0, :, 384:512].astype(F32).T[32:40, :]
     drain(x_run)
     pump(behind)
-    far = [dy_run]
+    store(x_all, x_out)
+    far = [output_run, dy_run]
     pump(far)
     calls = [0]
 
     def between():
         calls[0] += 1
         if calls[0] in (3, 4, 5):
-            pump(far)
+            pump(far[:1])
         if calls[0] in (2, 5):
             pump(behind)
 
     attend(
         x_all, w_all, gains_ref, cos_ref, sin_ref, lengths,
-        normed_ref, query_ref, pair_ref, lse_ref, mixed_ref, mixed_t, attended_ref, between,
+        normed_ref, query_ref, pair_ref, lse_ref, mixed_ref, mixed_t, mixed_rows, between,
     )
-    next(sum_run)
+    next(mixed_run)
+    store(normed_ref, normed_out)
+    store(query_ref, query_out)
+    store(pair_ref, pair_out)
+    drain(output_run)
+    store(output_all, output_out)
+    drain(mixed_run)
+    middle = x_ref[...].astype(F32)
+    for tp in range(8):
+        middle = middle + dot(mixed_own[tp], output_all[tp * D : (tp + 1) * D, :], ((1,), (1,)))
+    middle_ref[...] = middle
+    own_ref[...] = (middle * inverse_root(middle) * gains_ref[1:2, :]).astype(BF16)
+    next(token_run)
+    far = [dy_run]
+    pump(behind)
+    pump(far)
+    pump(behind)
+    pump(far)
+    drain(token_run, far + behind)
     while pump(far):
         pass
-    drain(sum_run)
-    pump(behind)
-    pump(behind)
-    middle = x_ref[...].astype(F32) + summed[...]
-    middle_ref[...] = middle
-    own_ref[...] = (middle * inverse_root(middle) * gains_ref[1:2, :]).astype(BF16)
-    drain(token_run, behind, 2)
+    store(dy_all, dy_out)
     while pump(behind):
         pass
+    for copy in stores:
+        copy.wait()
 
 
 def head(lengths, x, small, gate, up, down, dy, routes):
@@ -671,13 +664,27 @@
             shape(8, D, dtype=F32),
             shape(GROUP, 128, dtype=F32),
             shape(GROUP, 128, dtype=F32),
+            shape(8 * D, ROWS),
         ],
         in_specs=[pl.BlockSpec(memory_space=pltpu.SMEM)] + [vmem] * 7,
-        out_specs=[vmem] * 2 + [far] * 3 + [vmem] * 15,
+        out_specs=[far] * 6 + [vmem] + [far] * 3 + [vmem] * 4 + [far] * 3 + [vmem] + [far] * 3,
         scratch_shapes=[
+            pltpu.VMEM((GROUP, D), BF16),
+            pltpu.VMEM((1, D, 512), BF16),
+            pltpu.VMEM((GROUP, D), BF16),
+            pltpu.VMEM((GROUP, D), BF16),
+            pltpu.VMEM((GROUP, 128), BF16),
+            pltpu.VMEM((GROUP, 128), BF16),
+            pltpu.VMEM((GROUP, 128), F32),
+            pltpu.VMEM((GROUP, 128), F32),
             pltpu.VMEM((128, GROUP), F32),
-            pltpu.VMEM((GROUP, D), BF16),
-            pltpu.VMEM((ROWS, D), F32),
+            pltpu.VMEM((GROUP, 128), F32),
+            pltpu.VMEM((GROUP, 128), F32),
+            dma(12),
+            pltpu.VMEM((128, GROUP), F32),
+            pltpu.VMEM((GROUP, 128), BF16),
+            pltpu.VMEM((8, ROWS, 128), BF16),
+            pltpu.VMEM((8 * D, ROWS), BF16),
         ]
         + [buffer for task in HEAD_TASKS for buffer in task.scratch],
         compiler_params=pltpu.CompilerParams(
@@ -691,19 +698,21 @@
     SumChips(0),
     SumChips(1),
     SumChips(2),
+    ExchangeTp(),
     GatherTp(ROWS, D),
     SumTp(ROWS, D),
     SumTp(ROWS, D),
-    SumFsdp(1, 384),
+    SumFsdp(384, BF16),
     SumAll(128),
 )
 
 
 def tail_body(
-    lengths, grads_ref, combined_ref, pairs_ref,
-    x_ref, dy_ref, middle_ref, own_ref, chosen_ref, gains_ref,
-    x_all, w_all, normed_ref, query_ref, pair_ref, lse_ref, mixed_ref, cos_ref, sin_ref,
+    lengths, grads_ref, combined_in, pairs_ref,
+    x_ref, dy_ref, middle_ref, own_ref, chosen_ref, gains_ref, lse_ref, mixed_ref,
+    x_in, w_in, normed_in, query_in, pair_in, cos_in, sin_in, output_in,
     outputs_ref, input_grad, small_grad, attention_grad, gate_grad, up_grad, down_grad,
+    x_all, w_all, normed_ref, query_ref, pair_ref, cos_ref, sin_ref, output_all, combined_ref, dmixed_own, load_sem,
     grads_sum, moe_sum, datt_own, datt_all, dmiddle_ref, dnormed_part, dnormed_sum, weights_part, small_part, gain_grads,
     gain_row, dmixed_ref, dquery_t, dpair_ref, raw_ref, raw_t, *scratch,
 ):
@@ -711,17 +720,30 @@
     greet()
     pairs = (
         (grads_ref, grads_sum), (pairs_ref, gate_grad), (pairs_ref, up_grad), (pairs_ref, down_grad),
+        (lambda tp: dmixed_own.at[tp], functools.partial(part, dmixed_ref)),
         (datt_own, datt_all), (combined_ref, moe_sum), (dnormed_part, dnormed_sum),
         (weights_part, attention_grad), (small_part, small_grad),
     )
-    grads_run, gate_run, up_run, down_run, datt_run, moe_run, dnormed_run, weights_run, small_run = [
+    grads_run, gate_run, up_run, down_run, dmixed_run, datt_run, moe_run, dnormed_run, weights_run, small_run = [
         run_task(task, scratch, *pair) for task, pair in zip(TAIL_TASKS, pairs)
     ]
     behind = [gate_run, up_run, down_run]
     next(grads_run)
     pump(behind)
+    loads = []
+    for k, (src, dst) in enumerate(
+        (
+            (w_in, w_all), (x_in, x_all), (normed_in, normed_ref), (query_in, query_ref),
+            (pair_in, pair_ref), (cos_in, cos_ref), (sin_in, sin_ref), (output_in, output_all),
+            (combined_in, combined_ref),
+        )
+    ):
+        loads.append(pltpu.make_async_copy(src, dst, load_sem.at[k]))
+        loads[k].start()
     drain(grads_run)
 
+    for copy in loads:
+        copy.wait()
     middle = middle_ref[...]
     inverse = inverse_root(middle)
     unit = middle * inverse
@@ -737,41 +759,47 @@
     dmiddle = dy_ref[...].astype(F32) + rms_back(dtokens, unit, inverse, gains_ref[1:2, :])
     dmiddle_ref[...] = dmiddle
     datt_own[...] = dmiddle.astype(BF16)
+    for tp in range(8):
+        dmixed_own[tp] = dot(datt_own[...], output_all[tp * D : (tp + 1) * D, :]).astype(BF16)
+    next(dmixed_run)
     next(datt_run)
     pump(behind)
     pump(behind)
-    small_part[0] = dot(own_ref[...], dlogits, ((0,), (0,)))
+    small_part[...] = dot(own_ref[...], dlogits, ((0,), (0,))).reshape(small_part.shape)
     gain_grads[...] = jnp.zeros_like(gain_grads)
     gain_grads[EXPERTS : EXPERTS + 1, :] = jnp.sum(dtokens * unit, axis=0, keepdims=True)
-    drain(datt_run)
-
-    far = [moe_run]
+    drain(dmixed_run)
+    far = [datt_run, moe_run]
     pump(far)
     calls = [0]
 
     def between():
         calls[0] += 1
-        if calls[0] in (2, 4):
-            pump(far)
+        if calls[0] in (2, 3, 4):
+            pump(far[:1])
         if calls[0] == 2:
             pump(behind)
 
     attend_back(
-        datt_all, x_all, w_all, query_ref, pair_ref, lse_ref, cos_ref, sin_ref, lengths,
+        x_all, w_all, query_ref, pair_ref, lse_ref, cos_ref, sin_ref, lengths,
         dnormed_part, gain_row, dmixed_ref, dquery_t, dpair_ref, raw_ref, raw_t, between,
     )
     next(dnormed_run)
     gain_grads[EXPERTS + 1 : EXPERTS + 2, :] = gain_row[...]
-    small_part[0] += gain_grads[...].T
+    small_part[...] += gain_grads[...].T.reshape(small_part.shape)
     next(small_run)
-
-    @pl.loop(0, D // 256)
+    drain(datt_run)
+
+    @pl.loop(0, 4)
     def _(i):
         at = pl.ds(pl.multiple_of(i * 256, 256), 256)
-        weights_part[0, at, 0:256] = dot(raw_t[...], normed_ref[:, at]).T.astype(BF16)
-        weights_part[0, at, 256:384] = dot(mixed_ref[...], datt_all[:, at]).T.astype(BF16)
-
-    last = [dnormed_run, weights_run, small_run] + far + behind
+        chips = pl.ds(i * 2, 2)
+        into_qkv = dot(raw_t[...], normed_ref[:, at]).T.astype(BF16)
+        weights_part[chips, :, :, 0:256] = into_qkv.reshape(2, 2, BLOCK, 256)
+        into_output = dot(mixed_ref[...], datt_all[:, at]).T.astype(BF16)
+        weights_part[chips, :, :, 256:384] = into_output.reshape(2, 2, BLOCK, 128)
+
+    last = [dnormed_run, weights_run, small_run, moe_run] + behind
     while pump(last):
         pass
     outputs_ref[...] = (middle_ref[...] + moe_sum[...]).astype(BF16)
@@ -794,14 +822,25 @@
             shape(ROWS, D, dtype=BF16),
             shape(ROWS, D),
             shape(8, 128),
-            shape(1, BLOCK, 384),
+            shape(BLOCK, 384),
             weight,
             weight,
             weight,
         ],
-        in_specs=[pl.BlockSpec(memory_space=pltpu.SMEM)] + [vmem] * 2 + [far] + [vmem] * 15,
+        in_specs=[pl.BlockSpec(memory_space=pltpu.SMEM)] + [vmem] + [far] * 2 + [vmem] * 8 + [far] * 8,
         out_specs=[vmem] * 7,
         scratch_shapes=[
+            pltpu.VMEM((GROUP, D), BF16),
+            pltpu.VMEM((1, D, 512), BF16),
+            pltpu.VMEM((GROUP, D), BF16),
+            pltpu.VMEM((GROUP, 128), BF16),
+            pltpu.VMEM((GROUP, 128), BF16),
+            pltpu.VMEM((GROUP, 128), F32),
+            pltpu.VMEM((GROUP, 128), F32),
+            pltpu.VMEM((8 * D, ROWS), BF16),
+            pltpu.VMEM((GROUP, D), BF16),
+            pltpu.VMEM((8, ROWS, 128), BF16),
+            dma(9),
             pltpu.VMEM((ROWS, WIDE), F32),
             pltpu.VMEM((ROWS, D), F32),
             pltpu.VMEM((ROWS, D), BF16),
@@ -809,8 +848,8 @@
             pltpu.VMEM((ROWS, D), F32),
             pltpu.VMEM((GROUP, D), BF16),
             pltpu.VMEM((ROWS, D), F32),
-            pltpu.VMEM((1, D, 384), BF16),
-            pltpu.VMEM((1, D, 128), F32),
+            pltpu.VMEM((8, 2, BLOCK, 384), BF16),
+            pltpu.VMEM((8, 2, BLOCK, 128), F32),
             pltpu.VMEM((128, D), F32),
             pltpu.VMEM((1, D), F32),
             pltpu.VMEM((GROUP, 128), BF16),
@@ -830,7 +869,7 @@
     tokens_ref, dy_ref, router_ref, chosen_ref, rank_ref, rank_t,
     gate_ref, up_ref, down_ref,
     combined_ref, grad_ref, pair_ref,
-    combined_sum, grad_sum, gate_sum, gates_ref, parts, got, send_sem, recv_sem,
+    give_all, out_all, dpicked_all, dgate_all, gates_ref, parts, got, send_sem, recv_sem,
 ):
     step = pl.program_id(0)
     lane = lax.broadcasted_iota(jnp.int32, (1, 128), 1)
@@ -852,9 +891,9 @@
         barrier = pltpu.get_barrier_semaphore()
         pl.semaphore_signal(barrier, inc=1, device_id={"fsdp": core_partner()}, device_id_type=MESH)
         pl.semaphore_wait(barrier, 1)
-        combined_sum[...] = jnp.zeros_like(combined_sum)
-        grad_sum[...] = jnp.zeros_like(grad_sum)
-        gate_sum[...] = jnp.zeros_like(gate_sum)
+        out_all[...] = jnp.zeros_like(out_all)
+        dpicked_all[...] = jnp.zeros_like(dpicked_all)
+        dgate_all[...] = jnp.zeros_like(dgate_all)
         logits = jnp.where(chosen_ref[...] > 0.0, dot(tokens_ref[...], router_ref[0]), -1e30)
         raised = jnp.exp(logits - jnp.max(logits, axis=-1, keepdims=True))
         gates = raised / jnp.sum(raised, axis=-1, keepdims=True)
@@ -893,28 +932,29 @@
             across(step - 2).wait_send()
 
         slot_now = lax.rem(step, 2)
-        for k, (left, right) in enumerate(((picked, dgate_part), (picked, dup_part), (dy, weighted))):
-            grad = dot(left, right, ((0,), (0,))).astype(BF16)
-            parts[slot_now, k] = grad.reshape(8, 2, BLOCK, HIDDEN)
+        picked_t, dy_t = picked.T, dy.T
+        for k, (left, right) in enumerate(
+            ((picked_t, dgate_part), (picked_t, dup_part), (dy_t, weighted))
+        ):
+            parts[slot_now, k] = dot(left, right).astype(BF16).reshape(8, 2, BLOCK, HIDDEN)
         across(step).start()
 
-        out = dot(weighted, down_ref[0], ((1,), (1,))).astype(BF16)
+        rows = pl.ds(pl.multiple_of(step * PLACES, PLACES), SLOTS)
+        out_all[rows, :] = dot(weighted, down_ref[0], ((1,), (1,))).astype(BF16)
         dpicked = dot(dgate_part, gate_ref[0], ((1,), (1,)))
-        dpicked = (dpicked + dot(dup_part, up_ref[0], ((1,), (1,)))).astype(BF16)
-        dgate = jnp.where(expert_lane, dgate, 0.0).astype(BF16)
-
-        give = jnp.where(
-            lax.broadcasted_iota(jnp.int32, (GROUP, SLOTS), 1) == rank_column.astype(jnp.int32), 1.0, 0.0
-        ).astype(BF16)
-        combined_sum[...] += dot(give, out)
-        grad_sum[...] += dot(give, dpicked)
-        gate_sum[...] += dot(give, dgate)
+        dpicked_all[rows, :] = (dpicked + dot(dup_part, up_ref[0], ((1,), (1,)))).astype(BF16)
+        dgate_all[rows, :] = jnp.where(expert_lane, dgate, 0.0).astype(BF16)
+        place = lax.broadcasted_iota(jnp.int32, (GROUP, PLACES), 1)
+        give = jnp.where(place == rank_column.astype(jnp.int32), 1.0, 0.0)
+        give_all[:, pl.ds(pl.multiple_of(step * PLACES, PLACES), PLACES)] = give.astype(BF16)
 
     @pl.when(step == LOCAL)
     def _():
-        combined_ref[...] = combined_sum[...].astype(BF16)
-        grad_ref[:, 0:D] = grad_sum[...].astype(BF16)
-        grad_ref[:, D:WIDE] = gate_sum[...].astype(BF16)
+        for i in range(4):
+            columns = slice(256 * i, 256 * (i + 1))
+            combined_ref[:, columns] = dot(give_all[...], out_all[:, columns]).astype(BF16)
+            grad_ref[:, columns] = dot(give_all[...], dpicked_all[:, columns]).astype(BF16)
+        grad_ref[:, D:WIDE] = dot(give_all[...], dgate_all[...]).astype(BF16)
 
     @pl.when(step >= 1)
     def _():
@@ -961,9 +1001,10 @@
             pl.BlockSpec((1, 3, 8, BLOCK, HIDDEN), lambda i: (jnp.maximum(i - 1, 0), 0, 0, 0, 0)),
         ],
         scratch_shapes=[
-            pltpu.VMEM((GROUP, D), F32),
-            pltpu.VMEM((GROUP, D), F32),
-            pltpu.VMEM((GROUP, 128), F32),
+            pltpu.VMEM((GROUP, LOCAL * PLACES), BF16),
+            pltpu.VMEM((LOCAL * PLACES, D), BF16),
+            pltpu.VMEM((LOCAL * PLACES, D), BF16),
+            pltpu.VMEM((LOCAL * PLACES, 128), BF16),
             pltpu.VMEM((GROUP, 256), BF16),
             pltpu.VMEM((2, 3, 8, 2, BLOCK, HIDDEN), BF16),
             pltpu.VMEM((LOCAL, 3, 8, BLOCK, HIDDEN), BF16),
@@ -982,21 +1023,24 @@
 
 
 def finish_body(*refs):
-    outputs, input_grad, small, attention, gate, up, down = refs[:7]
-    outs = refs[7:]
-    outs[0][...] = outputs[...]
-    outs[1][...] = input_grad[...]
-    outs[2][...] = attention[0, :, 0:128]
-    outs[3][...] = attention[0, :, 128:192]
-    outs[4][...] = attention[0, :, 192:256]
-    outs[5][...] = attention[0, :, 256:384].T
+    sources, outs = refs[:7], refs[7:19]
+    small, attention, sems = refs[19:]
+    copies = []
+    for k, (source, target) in enumerate(
+        zip(sources, (outs[0], outs[1], small, attention, outs[9], outs[10], outs[11]))
+    ):
+        copies.append(pltpu.make_async_copy(source, target, sems.at[k]))
+        copies[k].start()
+    for copy in copies:
+        copy.wait()
+    outs[2][...] = attention[:, 0:128]
+    outs[3][...] = attention[:, 128:192]
+    outs[4][...] = attention[:, 192:256]
+    outs[5][...] = attention[:, 256:384].T
     outs[6][...] = small[:, 0:EXPERTS]
     columns = small[...].T
     outs[7][...] = columns[EXPERTS + 1 : EXPERTS + 2, :]
     outs[8][...] = columns[EXPERTS : EXPERTS + 1, :]
-    outs[9][...] = gate[...]
-    outs[10][...] = up[...]
-    outs[11][...] = down[...]
 
 
 def finish(*arrays):
@@ -1004,6 +1048,7 @@
         return jax.ShapeDtypeStruct(dims, dtype)
 
     vmem = pl.BlockSpec(memory_space=pltpu.VMEM)
+    far = pl.BlockSpec(memory_space=pl.ANY)
     return pl.pallas_call(
         finish_body,
         name="finish",
@@ -1019,9 +1064,10 @@
             shape(1, 8),
         ]
         + [shape(LOCAL, BLOCK, HIDDEN)] * 3,
-        in_specs=[vmem] * 7,
+        in_specs=[far] * 7,
         out_specs=[vmem] * 12,
-        compiler_params=pltpu.CompilerParams(vmem_limit_bytes=32 * 2**20),
+        scratch_shapes=[pltpu.VMEM((8, 128), F32), pltpu.VMEM((BLOCK, 384), F32), dma(7)],
+        compiler_params=pltpu.CompilerParams(vmem_limit_bytes=60 * 2**20),
     )(*arrays)
 
 
@@ -1056,7 +1102,7 @@
     )
     (
         x_all, w_all, gate_all, up_all, down_all, dy_all, tokens,
-        normed, query, pair, lse, mixed, middle, own, chosen, rank, rank_t, gains, cosine, sine,
+        normed, query, pair, lse, mixed, middle, own, chosen, rank, rank_t, gains, cosine, sine, output_all,
     ) = head(
         lengths, inputs, small[None], gate_weight, up_weight, down_weight.transpose(0, 2, 1),
         cotangent, routes.T,
@@ -1066,8 +1112,8 @@
     )
     results = tail(
         lengths, grads, combined, pairs,
-        inputs, cotangent, middle, own, chosen, gains,
-        x_all, w_all, normed, query, pair, lse, mixed, cosine, sine,
+        inputs, cotangent, middle, own, chosen, gains, lse, mixed,
+        x_all, w_all, normed, query, pair, cosine, sine, output_all,
     )
     (
         outputs, input_grad, query_grad, key_grad, value_grad, output_grad, router_grad, attn_gain_grad, moe_gain_grad,

time: 293 us -> 273 us (0.932)
  Pallas kernels: 279 us -> 266 us
  local copies, waits for them, and re-layouts: 11.2 us -> 5.36 us
    pallas_call x1, Pallas kernels: 117 us -> 108 us  [tail(): pl.pallas_call(tail_body, name='tail', out_shape=[shape(ROWS, D, dtype=BF...]
    unnamed x16 -> x2, local copies, waits for them, and re-layouts: 8.16 us -> 2.32 us
    pallas_call x1, Pallas kernels: 113 us -> 109 us  [head(): pl.pallas_call(head_body, name='head', out_shape=[shape(GROUP, D), shape(...]
where the time goes in v5:
time: 273 us; the launch traced here: 272 us
  Pallas kernels  266 us (97%)
  local copies, waits for them, and re-layouts  5.36 us (2%)
    pallas_call x1, Pallas kernels, head(): pl.pallas_call(head_body, name='head', out_shape=[shape(GROUP, D), shape(...  109 us
    pallas_call x1, Pallas kernels, tail(): pl.pallas_call(tail_body, name='tail', out_shape=[shape(ROWS, D, dtype=BF...  108 us
    pallas_call x1, Pallas kernels, experts(): pl.pallas_call(experts_body, name='experts', grid=(LOCAL + 1,), in_specs=...  45.7 us

profile of v5, /device:TPU:0, one launch (start us, length us, event | category | flops | bytes accessed | tf_op | source)
XLA Modules:
  0.0 272.2 jit_solution(17438523017208731536)
XLA Ops:
  0.6 0.8 copy.27
  1.4 0.8 copy.28
  2.2 0.8 copy.26
  3.0 1.5 concatenate.3
  4.5 109.3 %head.1 = (bf16[1024,1024]{1,0:T(8,128)(2,1)}, bf16[1,1024,512]{2,1,0:T(8,128)(2,1)}, bf16[4,1024,512]{2,1,0:T(8,128)(2,1)}, bf16[4,1024,512]{2,1,0:T(8,128)(2,1...) custom-call(s32[1,3]{1,0:T(1,128)} %lengths.3, ...), custom_call_target="tpu_custom_call" | custom-call | tf_op jit(solution)/shard_map/head/pallas_call | solution.py:643
  113.8 45.7 %experts.1 = (bf16[1024,1024]{1,0:T(8,128)(2,1)}, bf16[1024,1152]{1,0:T(8,128)(2,1)}, bf16[4,3,8,64,512]{4,3,2,1,0:T(8,128)(2,1)}) custom-call(bf16[1024,1024]{1,0:T(8,128)(2,1)} %get-tuple-element.55.tokens_ref, bf16[1024,1024]{1,0:T(8,128)(2,1)} %get-tuple-element.56.dy_ref, bf16[1,1024,512]{2,1,0:T(8,128)(2,1)} %get-tuple-element.57.router_ref.w_in, ...), custom_call_target="tpu_custom_call" | custom-call | tf_op jit(solution)/shard_map/experts/pallas_call | solution.py:983
  159.5 108.1 %tail.1 = (bf16[128,1024]{1,0:T(8,128)(2,1)}, f32[128,1024]{1,0:T(8,128)}, f32[8,128]{1,0:T(8,128)}, f32[64,384]{1,0:T(8,128)}, f32[4,64,512]{2,1,0:T(8,128)}, /...) custom-call(s32[1,3]{1,0:T(1,128)} %lengths.3, bf16[1024,1152]{1,0:T(8,128)(2,1)} %get-tuple-element.64.grads_ref, ...), custom_call_target="tpu_custom_call" | custom-call | tf_op jit(solution)/shard_map/tail/pallas_call | solution.py:818
  267.6 3.1 %finish.1 = (bf16[128,1024]{1,0:T(8,128)(2,1)}, f32[128,1024]{1,0:T(8,128)}, f32[64,128]{1,0:T(8,128)}, f32[64,64]{1,0:T(8,128)}, f32[64,64]{1,0:T(8,128)}, /*in...) custom-call(bf16[128,1024]{1,0:T(8,128)(2,1)} %get-tuple-element.79., ...), custom_call_target="tpu_custom_call" | custom-call | tf_op jit(solution)/shard_map/finish/pallas_call | solution.py:1052
  270.7 1.5 copy.29
  (1 shorter events, 0.0 us)

commit v6 on v5

--- a/solution.py
+++ b/solution.py
@@ -520,7 +520,6 @@
     GatherFsdp(LOCAL, HIDDEN),
     GatherFsdp(LOCAL, HIDDEN),
     GatherFsdp(LOCAL, HIDDEN),
-    GatherTp(ROWS, D),
     GatherTp(D, ROWS),
     ExchangeTp(),
     GatherTp(ROWS, D),
@@ -528,10 +527,10 @@
 
 
 def head_body(
-    lengths, x_ref, small_ref, gate_ref, up_ref, down_ref, dy_ref, routes_ref,
-    x_out, w_out, gate_all, up_all, down_all, dy_out, tokens,
+    lengths, x_ref, small_ref, gate_ref, up_ref, down_ref, routes_ref,
+    x_out, w_out, gate_all, up_all, down_all, tokens,
     normed_out, query_out, pair_out, lse_ref, mixed_ref, middle_ref, own_ref, chosen_out, rank_out, rank_t_out, gains_ref, cos_out, sin_out, output_out,
-    x_all, w_all, dy_all, normed_ref, query_ref, pair_ref, chosen_ref, rank_ref, rank_t, cos_ref, sin_ref, store_sem,
+    x_all, w_all, normed_ref, query_ref, pair_ref, chosen_ref, rank_ref, rank_t, cos_ref, sin_ref, store_sem,
     mixed_t, mixed_rows, mixed_own, output_all, *scratch,
 ):
     scratch = list(scratch)
@@ -544,10 +543,10 @@
     greet()
     pairs = (
         (x_ref, x_all), (small_ref, w_all), (gate_ref, gate_all), (up_ref, up_all), (down_ref, down_all),
-        (dy_ref, dy_all), (w_all.at[0, :, 256:384], output_all),
+        (w_all.at[0, :, 256:384], output_all),
         (functools.partial(part, mixed_rows), lambda tp: mixed_own.at[tp]), (own_ref, tokens),
     )
-    x_run, w_run, gate_run, up_run, down_run, dy_run, output_run, mixed_run, token_run = [
+    x_run, w_run, gate_run, up_run, down_run, output_run, mixed_run, token_run = [
         run_task(task, scratch, *pair) for task, pair in zip(HEAD_TASKS, pairs)
     ]
     front = [x_run, w_run]
@@ -590,14 +589,14 @@
     drain(x_run)
     pump(behind)
     store(x_all, x_out)
-    far = [output_run, dy_run]
+    far = [output_run]
     pump(far)
     calls = [0]
 
     def between():
         calls[0] += 1
         if calls[0] in (3, 4, 5):
-            pump(far[:1])
+            pump(far)
         if calls[0] in (2, 5):
             pump(behind)
 
@@ -618,22 +617,16 @@
     middle_ref[...] = middle
     own_ref[...] = (middle * inverse_root(middle) * gains_ref[1:2, :]).astype(BF16)
     next(token_run)
-    far = [dy_run]
     pump(behind)
-    pump(far)
     pump(behind)
-    pump(far)
-    drain(token_run, far + behind)
-    while pump(far):
-        pass
-    store(dy_all, dy_out)
+    drain(token_run, behind)
     while pump(behind):
         pass
     for copy in stores:
         copy.wait()
 
 
-def head(lengths, x, small, gate, up, down, dy, routes):
+def head(lengths, x, small, gate, up, down, routes):
     def shape(*dims, dtype=BF16):
         return jax.ShapeDtypeStruct(dims, dtype)
 
@@ -649,7 +642,6 @@
             weight,
             weight,
             weight,
-            shape(GROUP, D),
             shape(GROUP, D),
             shape(GROUP, D),
             shape(GROUP, 128),
@@ -666,12 +658,11 @@
             shape(GROUP, 128, dtype=F32),
             shape(8 * D, ROWS),
         ],
-        in_specs=[pl.BlockSpec(memory_space=pltpu.SMEM)] + [vmem] * 7,
-        out_specs=[far] * 6 + [vmem] + [far] * 3 + [vmem] * 4 + [far] * 3 + [vmem] + [far] * 3,
+        in_specs=[pl.BlockSpec(memory_space=pltpu.SMEM)] + [vmem] * 6,
+        out_specs=[far] * 5 + [vmem] + [far] * 3 + [vmem] * 4 + [far] * 3 + [vmem] + [far] * 3,
         scratch_shapes=[
             pltpu.VMEM((GROUP, D), BF16),
             pltpu.VMEM((1, D, 512), BF16),
-            pltpu.VMEM((GROUP, D), BF16),
             pltpu.VMEM((GROUP, D), BF16),
             pltpu.VMEM((GROUP, 128), BF16),
             pltpu.VMEM((GROUP, 128), BF16),
@@ -690,7 +681,7 @@
         compiler_params=pltpu.CompilerParams(
             collective_id=1, has_side_effects=True, vmem_limit_bytes=56 * 2**20
         ),
-    )(lengths, x, small, gate, up, down, dy, routes)
+    )(lengths, x, small, gate, up, down, routes)
 
 
 TAIL_TASKS = (
@@ -701,19 +692,18 @@
     ExchangeTp(),
     GatherTp(ROWS, D),
     SumTp(ROWS, D),
-    SumTp(ROWS, D),
     SumFsdp(384, BF16),
     SumAll(128),
 )
 
 
 def tail_body(
-    lengths, grads_ref, combined_in, pairs_ref,
+    lengths, grads_ref, moe_sum, pairs_ref,
     x_ref, dy_ref, middle_ref, own_ref, chosen_ref, gains_ref, lse_ref, mixed_ref,
     x_in, w_in, normed_in, query_in, pair_in, cos_in, sin_in, output_in,
     outputs_ref, input_grad, small_grad, attention_grad, gate_grad, up_grad, down_grad,
-    x_all, w_all, normed_ref, query_ref, pair_ref, cos_ref, sin_ref, output_all, combined_ref, dmixed_own, load_sem,
-    grads_sum, moe_sum, datt_own, datt_all, dmiddle_ref, dnormed_part, dnormed_sum, weights_part, small_part, gain_grads,
+    x_all, w_all, normed_ref, query_ref, pair_ref, cos_ref, sin_ref, output_all, dmixed_own, load_sem,
+    grads_sum, datt_own, datt_all, dmiddle_ref, dnormed_part, dnormed_sum, weights_part, small_part, gain_grads,
     gain_row, dmixed_ref, dquery_t, dpair_ref, raw_ref, raw_t, *scratch,
 ):
     scratch = list(scratch)
@@ -721,10 +711,10 @@
     pairs = (
         (grads_ref, grads_sum), (pairs_ref, gate_grad), (pairs_ref, up_grad), (pairs_ref, down_grad),
         (lambda tp: dmixed_own.at[tp], functools.partial(part, dmixed_ref)),
-        (datt_own, datt_all), (combined_ref, moe_sum), (dnormed_part, dnormed_sum),
+        (datt_own, datt_all), (dnormed_part, dnormed_sum),
         (weights_part, attention_grad), (small_part, small_grad),
     )
-    grads_run, gate_run, up_run, down_run, dmixed_run, datt_run, moe_run, dnormed_run, weights_run, small_run = [
+    grads_run, gate_run, up_run, down_run, dmixed_run, datt_run, dnormed_run, weights_run, small_run = [
         run_task(task, scratch, *pair) for task, pair in zip(TAIL_TASKS, pairs)
     ]
     behind = [gate_run, up_run, down_run]
@@ -735,7 +725,6 @@
         (
             (w_in, w_all), (x_in, x_all), (normed_in, normed_ref), (query_in, query_ref),
             (pair_in, pair_ref), (cos_in, cos_ref), (sin_in, sin_ref), (output_in, output_all),
-            (combined_in, combined_ref),
         )
     ):
         loads.append(pltpu.make_async_copy(src, dst, load_sem.at[k]))
@@ -769,14 +758,14 @@
     gain_grads[...] = jnp.zeros_like(gain_grads)
     gain_grads[EXPERTS : EXPERTS + 1, :] = jnp.sum(dtokens * unit, axis=0, keepdims=True)
     drain(dmixed_run)
-    far = [datt_run, moe_run]
+    far = [datt_run]
     pump(far)
     calls = [0]
 
     def between():
         calls[0] += 1
         if calls[0] in (2, 3, 4):
-            pump(far[:1])
+            pump(far)
         if calls[0] == 2:
             pump(behind)
 
@@ -799,7 +788,7 @@
         into_output = dot(mixed_ref[...], datt_all[:, at]).T.astype(BF16)
         weights_part[chips, :, :, 256:384] = into_output.reshape(2, 2, BLOCK, 128)
 
-    last = [dnormed_run, weights_run, small_run, moe_run] + behind
+    last = [dnormed_run, weights_run, small_run] + behind
     while pump(last):
         pass
     outputs_ref[...] = (middle_ref[...] + moe_sum[...]).astype(BF16)
@@ -827,7 +816,7 @@
             weight,
             weight,
         ],
-        in_specs=[pl.BlockSpec(memory_space=pltpu.SMEM)] + [vmem] + [far] * 2 + [vmem] * 8 + [far] * 8,
+        in_specs=[pl.BlockSpec(memory_space=pltpu.SMEM)] + [vmem] * 2 + [far] + [vmem] * 8 + [far] * 8,
         out_specs=[vmem] * 7,
         scratch_shapes=[
             pltpu.VMEM((GROUP, D), BF16),
@@ -838,11 +827,9 @@
             pltpu.VMEM((GROUP, 128), F32),
             pltpu.VMEM((GROUP, 128), F32),
             pltpu.VMEM((8 * D, ROWS), BF16),
-            pltpu.VMEM((GROUP, D), BF16),
             pltpu.VMEM((8, ROWS, 128), BF16),
             dma(9),
             pltpu.VMEM((ROWS, WIDE), F32),
-            pltpu.VMEM((ROWS, D), F32),
             pltpu.VMEM((ROWS, D), BF16),
             pltpu.VMEM((GROUP, D), BF16),
             pltpu.VMEM((ROWS, D), F32),
@@ -865,23 +852,128 @@
     )(*arrays)
 
 
+class StepGather:
+    scratch = [dma(7), dma(7), pltpu.SemaphoreType.DMA(())]
+
+    def __init__(self, src, out, send_sem, recv_sem, own_sem):
+        self.src, self.out, self.send_sem, self.recv_sem = src, out, send_sem, recv_sem
+        self.own = pltpu.make_async_copy(src, part(out, lax.axis_index("tp")), own_sem)
+
+    def copy(self, k):
+        place, target, _ = GATHER[k]
+        block = part(self.out, tp_at(*place))
+        return pltpu.make_async_remote_copy(
+            src_ref=self.src if place == (0, 0) else block,
+            dst_ref=block,
+            send_sem=self.send_sem.at[k],
+            recv_sem=self.recv_sem.at[k],
+            device_id={"tp": tp_at(*target)},
+            device_id_type=MESH,
+        )
+
+    def stage(self, number):
+        if number == 0:
+            self.own.start()
+            for k in (0, 1, 2):
+                self.copy(k).start()
+        elif number == 1:
+            self.copy(0).wait_recv()
+            self.copy(3).start()
+            self.copy(4).start()
+        elif number == 2:
+            self.copy(1).wait_recv()
+            self.copy(5).start()
+            self.copy(4).wait_recv()
+            self.copy(6).start()
+        else:
+            for k in (2, 3, 5, 6):
+                self.copy(k).wait_recv()
+            for k in range(7):
+                self.copy(k).wait_send()
+            self.own.wait()
+
+
+class StepSum:
+    scratch = [dma(7), dma(7), pltpu.VMEM((7, ROWS, D), BF16)]
+
+    def __init__(self, src, out, send_sem, recv_sem, landed):
+        self.src, self.out, self.landed = src, out, landed
+        self.send_sem, self.recv_sem = send_sem, recv_sem
+
+    def copy(self, k):
+        place, target, others = SUM[k]
+        return pltpu.make_async_remote_copy(
+            src_ref=self.landed.at[others[0]] if others else part(self.src, tp_at(*place)),
+            dst_ref=self.landed.at[k],
+            send_sem=self.send_sem.at[k],
+            recv_sem=self.recv_sem.at[k],
+            device_id={"tp": tp_at(*target)},
+            device_id_type=MESH,
+        )
+
+    def total(self, place, others, dst):
+        start = tp_at(*place) * ROWS
+
+        @pl.loop(0, ROWS // 16)
+        def _(i):
+            at = pl.multiple_of(i * 16, 16)
+            value = self.src[pl.ds(pl.multiple_of(start + at, 16), 16), :].astype(F32)
+            for k in others:
+                value = value + self.landed[k, pl.ds(at, 16), :].astype(F32)
+            dst[pl.ds(at, 16), :] = value.astype(dst.dtype)
+
+    def relay(self, k):
+        place, _, others = SUM[k]
+        for other in others:
+            self.copy(other).wait_recv()
+        self.total(place, others, self.landed.at[others[0]])
+        self.copy(k).start()
+
+    def stage(self, number):
+        if number == 0:
+            for k in range(4):
+                self.copy(k).start()
+        elif number == 1:
+            self.relay(4)
+            self.relay(5)
+        elif number == 2:
+            self.relay(6)
+        else:
+            for k in LAST:
+                self.copy(k).wait_recv()
+            self.total((0, 0), LAST, self.out)
+            for k in range(7):
+                self.copy(k).wait_send()
+
+
 def experts_body(
     tokens_ref, dy_ref, router_ref, chosen_ref, rank_ref, rank_t,
     gate_ref, up_ref, down_ref,
-    combined_ref, grad_ref, pair_ref,
-    give_all, out_all, dpicked_all, dgate_all, gates_ref, parts, got, send_sem, recv_sem,
+    moe_ref, grad_ref, pair_ref,
+    give_all, slots_all, dgate_all, gates_ref, parts, got, send_sem, recv_sem,
+    picked_all, gate_parts, up_parts, slot_gates, dy_all, combined_ref, *scratch,
 ):
     step = pl.program_id(0)
     lane = lax.broadcasted_iota(jnp.int32, (1, 128), 1)
     core = lax.rem(lax.axis_index("fsdp"), 2)
-
-    def across(expert):
-        slot = lax.rem(expert, 2)
+    dy_gather = StepGather(dy_ref, dy_all, *scratch[:3])
+    moe_sum = StepSum(combined_ref, moe_ref, *scratch[3:])
+    local = lax.rem(step, LOCAL)
+    expert = lax.axis_index("tp") * LOCAL + local
+    expert_lane = lane == expert
+    rows = pl.ds(pl.multiple_of(local * PLACES, PLACES), SLOTS)
+
+    def take():
+        slot = lax.broadcasted_iota(jnp.int32, (SLOTS, GROUP), 0)
+        return jnp.where(slot == rank_t[pl.ds(expert, 1), :].astype(jnp.int32), 1.0, 0.0).astype(BF16)
+
+    def across(number):
+        slot = lax.rem(number, 2)
         return pltpu.make_async_remote_copy(
             src_ref=parts.at[slot, :, :, 1 - core],
-            dst_ref=got.at[expert],
+            dst_ref=got.at[number],
             send_sem=send_sem.at[slot],
-            recv_sem=recv_sem.at[expert],
+            recv_sem=recv_sem.at[number],
             device_id={"fsdp": core_partner()},
             device_id_type=MESH,
         )
@@ -889,10 +981,11 @@
     @pl.when(step == 0)
     def _():
         barrier = pltpu.get_barrier_semaphore()
-        pl.semaphore_signal(barrier, inc=1, device_id={"fsdp": core_partner()}, device_id_type=MESH)
-        pl.semaphore_wait(barrier, 1)
-        out_all[...] = jnp.zeros_like(out_all)
-        dpicked_all[...] = jnp.zeros_like(dpicked_all)
+        for device in ({"tp": tp_at(1, 0)}, {"tp": tp_at(3, 0)}, {"tp": tp_at(0, 1)}, {"fsdp": core_partner()}):
+            pl.semaphore_signal(barrier, inc=1, device_id=device, device_id_type=MESH)
+        pl.semaphore_wait(barrier, 4)
+        dy_gather.stage(0)
+        slots_all[...] = jnp.zeros_like(slots_all)
         dgate_all[...] = jnp.zeros_like(dgate_all)
         logits = jnp.where(chosen_ref[...] > 0.0, dot(tokens_ref[...], router_ref[0]), -1e30)
         raised = jnp.exp(logits - jnp.max(logits, axis=-1, keepdims=True))
@@ -901,25 +994,48 @@
         gates_ref[:, 0:128] = high
         gates_ref[:, 128:256] = (gates - high.astype(F32)).astype(BF16)
 
+    for number, at in ((1, 1), (2, 2), (3, LOCAL)):
+        pl.when(step == at)(functools.partial(dy_gather.stage, number))
+
     @pl.when(step < LOCAL)
     def _():
-        expert = lax.axis_index("tp") * LOCAL + step
-        expert_lane = lane == expert
-        slot = lax.broadcasted_iota(jnp.int32, (SLOTS, GROUP), 0)
-        rank_row = rank_t[pl.ds(expert, 1), :].astype(jnp.int32)
-        rank_column = jnp.sum(jnp.where(expert_lane, rank_ref[...], 0.0), axis=1, keepdims=True)
-        take = jnp.where(slot == rank_row, 1.0, 0.0).astype(BF16)
-        slot_gates = dot(take, gates_ref[...])
-        slot_gates = slot_gates[:, 0:128] + slot_gates[:, 128:256]
-        slot_gate = jnp.sum(jnp.where(expert_lane, slot_gates, 0.0), axis=1, keepdims=True)
-        picked = dot(take, tokens_ref[...]).astype(BF16)
-        dy = dot(take, dy_ref[...]).astype(BF16)
-
+        taken = take()
+        slot_gate = dot(taken, gates_ref[...])
+        slot_gate = jnp.where(expert_lane, slot_gate[:, 0:128] + slot_gate[:, 128:256], 0.0)
+        slot_gate = jnp.sum(slot_gate, axis=1, keepdims=True)
+        slot_gates[local] = jnp.broadcast_to(slot_gate, (SLOTS, 128))
+        picked = dot(taken, tokens_ref[...]).astype(BF16)
+        picked_all[local] = picked
         gate_part = dot(picked, gate_ref[0])
         up_part = dot(picked, up_ref[0])
+        gate_parts[local] = gate_part
+        up_parts[local] = up_part
+        hidden = gate_part * (1.0 / (1.0 + jnp.exp(-gate_part))) * up_part
+        weighted = (hidden * slot_gate).astype(BF16)
+        slots_all[rows, :] = dot(weighted, down_ref[0], ((1,), (1,))).astype(BF16)
+        rank_column = jnp.sum(jnp.where(expert_lane, rank_ref[...], 0.0), axis=1, keepdims=True)
+        place = lax.broadcasted_iota(jnp.int32, (GROUP, PLACES), 1)
+        give = jnp.where(place == rank_column.astype(jnp.int32), 1.0, 0.0)
+        give_all[:, pl.ds(pl.multiple_of(local * PLACES, PLACES), PLACES)] = give.astype(BF16)
+
+    @pl.when(step == LOCAL - 1)
+    def _():
+        for i in range(4):
+            columns = slice(256 * i, 256 * (i + 1))
+            combined_ref[:, columns] = dot(give_all[...], slots_all[:, columns]).astype(BF16)
+        moe_sum.stage(0)
+
+    for number, at in ((1, LOCAL + 2), (2, LOCAL + 3)):
+        pl.when(step == at)(functools.partial(moe_sum.stage, number))
+
+    @pl.when((step >= LOCAL) & (step < 2 * LOCAL))
+    def _():
+        slot_gate = slot_gates[local][:, 0:1]
+        gate_part, up_part = gate_parts[local], up_parts[local]
         sigmoid = 1.0 / (1.0 + jnp.exp(-gate_part))
         silu = gate_part * sigmoid
         hidden = silu * up_part
+        dy = dot(take(), dy_all[...]).astype(BF16)
         dhidden = dot(dy, down_ref[0])
         dgate = jnp.sum(hidden * dhidden, axis=1, keepdims=True)
         weighted = (hidden * slot_gate).astype(BF16)
@@ -927,50 +1043,45 @@
         dgate_part = (dhidden * up_part * (sigmoid * (1.0 + gate_part * (1.0 - sigmoid)))).astype(BF16)
         dup_part = (dhidden * silu).astype(BF16)
 
-        @pl.when(step >= 2)
+        @pl.when(local >= 2)
         def _():
-            across(step - 2).wait_send()
-
-        slot_now = lax.rem(step, 2)
-        picked_t, dy_t = picked.T, dy.T
+            across(local - 2).wait_send()
+
+        slot_now = lax.rem(local, 2)
+        picked_t, dy_t = picked_all[local].T, dy.T
         for k, (left, right) in enumerate(
             ((picked_t, dgate_part), (picked_t, dup_part), (dy_t, weighted))
         ):
             parts[slot_now, k] = dot(left, right).astype(BF16).reshape(8, 2, BLOCK, HIDDEN)
-        across(step).start()
-
-        rows = pl.ds(pl.multiple_of(step * PLACES, PLACES), SLOTS)
-        out_all[rows, :] = dot(weighted, down_ref[0], ((1,), (1,))).astype(BF16)
+        across(local).start()
         dpicked = dot(dgate_part, gate_ref[0], ((1,), (1,)))
-        dpicked_all[rows, :] = (dpicked + dot(dup_part, up_ref[0], ((1,), (1,)))).astype(BF16)
+        slots_all[rows, :] = (dpicked + dot(dup_part, up_ref[0], ((1,), (1,)))).astype(BF16)
         dgate_all[rows, :] = jnp.where(expert_lane, dgate, 0.0).astype(BF16)
-        place = lax.broadcasted_iota(jnp.int32, (GROUP, PLACES), 1)
-        give = jnp.where(place == rank_column.astype(jnp.int32), 1.0, 0.0)
-        give_all[:, pl.ds(pl.multiple_of(step * PLACES, PLACES), PLACES)] = give.astype(BF16)
-
-    @pl.when(step == LOCAL)
+
+    @pl.when(step == 2 * LOCAL)
     def _():
         for i in range(4):
             columns = slice(256 * i, 256 * (i + 1))
-            combined_ref[:, columns] = dot(give_all[...], out_all[:, columns]).astype(BF16)
-            grad_ref[:, columns] = dot(give_all[...], dpicked_all[:, columns]).astype(BF16)
+            grad_ref[:, columns] = dot(give_all[...], slots_all[:, columns]).astype(BF16)
         grad_ref[:, D:WIDE] = dot(give_all[...], dgate_all[...]).astype(BF16)
-
-    @pl.when(step >= 1)
+        moe_sum.stage(3)
+
+    @pl.when(step >= LOCAL + 1)
     def _():
-        across(step - 1).wait_recv()
-        slot_before = lax.rem(step - 1, 2)
+        before = step - LOCAL - 1
+        across(before).wait_recv()
+        slot_before = lax.rem(before, 2)
 
         @pl.loop(0, 24)
         def _(i):
             kind, chip = i // 8, lax.rem(i, 8)
-            total = parts[slot_before, kind, chip, core].astype(F32) + got[step - 1, kind, chip].astype(F32)
+            total = parts[slot_before, kind, chip, core].astype(F32) + got[before, kind, chip].astype(F32)
             pair_ref[0, kind, chip] = total.astype(BF16)
 
-    @pl.when(step == LOCAL)
+    @pl.when(step == 2 * LOCAL)
     def _():
-        for expert in (LOCAL - 2, LOCAL - 1):
-            across(expert).wait_send()
+        for number in (LOCAL - 2, LOCAL - 1):
+            across(number).wait_send()
 
 
 def experts(tokens, dy, router, chosen, rank, rank_t, gate, up, down):
@@ -978,15 +1089,19 @@
         return pl.BlockSpec(shape, lambda i: (0,) * len(shape))
 
     def own(*shape):
-        return pl.BlockSpec((1,) + shape, lambda i: (jnp.minimum(i, LOCAL - 1),) + (0,) * len(shape))
-
+        return pl.BlockSpec(
+            (1,) + shape,
+            lambda i: (lax.rem(jnp.minimum(i, 2 * LOCAL - 1), LOCAL),) + (0,) * len(shape),
+        )
+
+    slots = LOCAL * PLACES
     return pl.pallas_call(
         experts_body,
         name="experts",
-        grid=(LOCAL + 1,),
+        grid=(2 * LOCAL + 1,),
         in_specs=[
             whole(GROUP, D),
-            whole(GROUP, D),
+            whole(ROWS, D),
             pl.BlockSpec((1, D, 128), lambda i: (0, 0, 3)),
             whole(GROUP, 128),
             whole(GROUP, 128),
@@ -996,28 +1111,37 @@
             own(D, HIDDEN),
         ],
         out_specs=[
-            whole(GROUP, D),
+            whole(ROWS, D),
             whole(GROUP, WIDE),
-            pl.BlockSpec((1, 3, 8, BLOCK, HIDDEN), lambda i: (jnp.maximum(i - 1, 0), 0, 0, 0, 0)),
+            pl.BlockSpec(
+                (1, 3, 8, BLOCK, HIDDEN), lambda i: (jnp.maximum(i - LOCAL - 1, 0), 0, 0, 0, 0)
+            ),
         ],
         scratch_shapes=[
-            pltpu.VMEM((GROUP, LOCAL * PLACES), BF16),
-            pltpu.VMEM((LOCAL * PLACES, D), BF16),
-            pltpu.VMEM((LOCAL * PLACES, D), BF16),
-            pltpu.VMEM((LOCAL * PLACES, 128), BF16),
+            pltpu.VMEM((GROUP, slots), BF16),
+            pltpu.VMEM((slots, D), BF16),
+            pltpu.VMEM((slots, 128), BF16),
             pltpu.VMEM((GROUP, 256), BF16),
             pltpu.VMEM((2, 3, 8, 2, BLOCK, HIDDEN), BF16),
             pltpu.VMEM((LOCAL, 3, 8, BLOCK, HIDDEN), BF16),
             dma(2),
             dma(LOCAL),
-        ],
+            pltpu.VMEM((LOCAL, SLOTS, D), BF16),
+            pltpu.VMEM((LOCAL, SLOTS, HIDDEN), F32),
+            pltpu.VMEM((LOCAL, SLOTS, HIDDEN), F32),
+            pltpu.VMEM((LOCAL, SLOTS, 128), F32),
+            pltpu.VMEM((GROUP, D), BF16),
+            pltpu.VMEM((GROUP, D), BF16),
+        ]
+        + StepGather.scratch
+        + StepSum.scratch,
         out_shape=[
-            jax.ShapeDtypeStruct((GROUP, D), BF16),
+            jax.ShapeDtypeStruct((ROWS, D), F32),
             jax.ShapeDtypeStruct((GROUP, WIDE), BF16),
             jax.ShapeDtypeStruct((LOCAL, 3, 8, BLOCK, HIDDEN), BF16),
         ],
         compiler_params=pltpu.CompilerParams(
-            collective_id=3, has_side_effects=True, vmem_limit_bytes=60 * 2**20
+            collective_id=3, has_side_effects=True, vmem_limit_bytes=62 * 2**20
         ),
     )(tokens, dy, router, chosen, rank, rank_t, gate, up, down)
 
@@ -1101,17 +1225,17 @@
         axis=1,
     )
     (
-        x_all, w_all, gate_all, up_all, down_all, dy_all, tokens,
+        x_all, w_all, gate_all, up_all, down_all, tokens,
         normed, query, pair, lse, mixed, middle, own, chosen, rank, rank_t, gains, cosine, sine, output_all,
     ) = head(
         lengths, inputs, small[None], gate_weight, up_weight, down_weight.transpose(0, 2, 1),
-        cotangent, routes.T,
+        routes.T,
     )
-    combined, grads, pairs = experts(
-        tokens, dy_all, w_all, chosen, rank, rank_t, gate_all, up_all, down_all
+    moe, grads, pairs = experts(
+        tokens, cotangent, w_all, chosen, rank, rank_t, gate_all, up_all, down_all
     )
     results = tail(
-        lengths, grads, combined, pairs,
+        lengths, grads, moe, pairs,
         inputs, cotangent, middle, own, chosen, gains, lse, mixed,
         x_all, w_all, normed, query, pair, cosine, sine, output_all,
     )

time: 273 us -> 256 us (0.938)
  Pallas kernels: 266 us -> 249 us
    pallas_call x1, Pallas kernels: 109 us -> 90.3 us  [head(): pl.pallas_call(head_body, name='head', out_shape=[shape(GROUP, D), shape(...]
    pallas_call x1, Pallas kernels: 45.7 us -> 58.2 us  [experts(): pl.pallas_call(experts_body, name='experts', grid=(2 * LOCAL + 1,), in_sp...]
    pallas_call x1, Pallas kernels: 108 us -> 97 us  [tail(): pl.pallas_call(tail_body, name='tail', out_shape=[shape(ROWS, D, dtype=BF...]
where the time goes in v6:
time: 256 us; the launch traced here: 255 us
  Pallas kernels  249 us (97%)
  local copies, waits for them, and re-layouts  5.36 us (2%)
    pallas_call x1, Pallas kernels, tail(): pl.pallas_call(tail_body, name='tail', out_shape=[shape(ROWS, D, dtype=BF...  97 us
    pallas_call x1, Pallas kernels, head(): pl.pallas_call(head_body, name='head', out_shape=[shape(GROUP, D), shape(...  90.3 us
    pallas_call x1, Pallas kernels, experts(): pl.pallas_call(experts_body, name='experts', grid=(2 * LOCAL + 1,), in_sp...  58.2 us

profile of v6, /device:TPU:0, one launch (start us, length us, event | category | flops | bytes accessed | tf_op | source)
XLA Modules:
  0.0 254.6 jit_solution(17813897728869150914)
XLA Ops:
  0.6 0.8 copy.27
  1.4 0.8 copy.28
  2.2 0.8 copy.26
  3.0 1.5 concatenate.3
  4.5 90.3 %head.1 = (bf16[1024,1024]{1,0:T(8,128)(2,1)}, bf16[1,1024,512]{2,1,0:T(8,128)(2,1)}, bf16[4,1024,512]{2,1,0:T(8,128)(2,1)}, bf16[4,1024,512]{2,1,0:T(8,128)(2,1...) custom-call(s32[1,3]{1,0:T(1,128)} %lengths.3, ...), custom_call_target="tpu_custom_call" | custom-call | tf_op jit(solution)/shard_map/head/pallas_call | solution.py:636
  94.8 58.2 %experts.1 = (f32[128,1024]{1,0:T(8,128)}, bf16[1024,1152]{1,0:T(8,128)(2,1)}, bf16[4,3,8,64,512]{4,3,2,1,0:T(8,128)(2,1)}) custom-call(bf16[1024,1024]{1,0:T(8,128)(2,1)} %get-tuple-element.54.tokens_ref, bf16[128,1024]{1,0:T(8,128)(2,1)} %dy_ref.3, bf16[1,1024,512]{2,1,0:T(8,128)(2,1)} %get-tuple-element.55.router_ref.w_in, ...), custom_call_target="tpu_custom_call" | custom-call | tf_op jit(solution)/shard_map/experts/pallas_call | solution.py:1098
  153.0 97.0 %tail.1 = (bf16[128,1024]{1,0:T(8,128)(2,1)}, f32[128,1024]{1,0:T(8,128)}, f32[8,128]{1,0:T(8,128)}, f32[64,384]{1,0:T(8,128)}, f32[4,64,512]{2,1,0:T(8,128)}, /...) custom-call(s32[1,3]{1,0:T(1,128)} %lengths.3, bf16[1024,1152]{1,0:T(8,128)(2,1)} %get-tuple-element.62.grads_ref, ...), custom_call_target="tpu_custom_call" | custom-call | tf_op jit(solution)/shard_map/tail/pallas_call | solution.py:807
  249.9 3.1 %finish.1 = (bf16[128,1024]{1,0:T(8,128)(2,1)}, f32[128,1024]{1,0:T(8,128)}, f32[64,128]{1,0:T(8,128)}, f32[64,64]{1,0:T(8,128)}, f32[64,64]{1,0:T(8,128)}, /*in...) custom-call(bf16[128,1024]{1,0:T(8,128)(2,1)} %get-tuple-element.77., ...), custom_call_target="tpu_custom_call" | custom-call | tf_op jit(solution)/shard_map/finish/pallas_call | solution.py:1176
  253.1 1.5 copy.29
  (1 shorter events, 0.0 us)

commit v7 on v6

--- a/solution.py
+++ b/solution.py
@@ -617,7 +617,6 @@
     middle_ref[...] = middle
     own_ref[...] = (middle * inverse_root(middle) * gains_ref[1:2, :]).astype(BF16)
     next(token_run)
-    pump(behind)
     pump(behind)
     drain(token_run, behind)
     while pump(behind):
@@ -764,9 +763,9 @@
 
     def between():
         calls[0] += 1
-        if calls[0] in (2, 3, 4):
+        if calls[0] in (3, 4):
             pump(far)
-        if calls[0] == 2:
+        if calls[0] == 4:
             pump(behind)
 
     attend_back(
@@ -883,6 +882,7 @@
         elif number == 2:
             self.copy(1).wait_recv()
             self.copy(5).start()
+        elif number == 3:
             self.copy(4).wait_recv()
             self.copy(6).start()
         else:
@@ -994,7 +994,7 @@
         gates_ref[:, 0:128] = high
         gates_ref[:, 128:256] = (gates - high.astype(F32)).astype(BF16)
 
-    for number, at in ((1, 1), (2, 2), (3, LOCAL)):
+    for number, at in ((1, 1), (2, 2), (3, 3), (4, LOCAL)):
         pl.when(step == at)(functools.partial(dy_gather.stage, number))
 
     @pl.when(step < LOCAL)

time: 256 us -> 244 us (0.953)
  Pallas kernels: 249 us -> 237 us
    pallas_call x1, Pallas kernels: 97 us -> 89 us  [tail(): pl.pallas_call(tail_body, name='tail', out_shape=[shape(ROWS, D, dtype=BF...]
    pallas_call x1, Pallas kernels: 58.2 us -> 54.7 us  [experts(): pl.pallas_call(experts_body, name='experts', grid=(2 * LOCAL + 1,), in_sp...]
where the time goes in v7:
time: 244 us; the launch traced here: 243 us
  Pallas kernels  237 us (97%)
  local copies, waits for them, and re-layouts  5.36 us (2%)
    pallas_call x1, Pallas kernels, head(): pl.pallas_call(head_body, name='head', out_shape=[shape(GROUP, D), shape(...  90.4 us
    pallas_call x1, Pallas kernels, tail(): pl.pallas_call(tail_body, name='tail', out_shape=[shape(ROWS, D, dtype=BF...  89 us
    pallas_call x1, Pallas kernels, experts(): pl.pallas_call(experts_body, name='experts', grid=(2 * LOCAL + 1,), in_sp...  54.7 us

profile of v7, /device:TPU:0, one launch (start us, length us, event | category | flops | bytes accessed | tf_op | source)
XLA Modules:
  0.0 243.2 jit_solution(12207809523679295247)
XLA Ops:
  0.6 0.8 copy.27
  1.4 0.8 copy.28
  2.2 0.8 copy.26
  3.0 1.5 concatenate.3
  4.5 90.4 %head.1 = (bf16[1024,1024]{1,0:T(8,128)(2,1)}, bf16[1,1024,512]{2,1,0:T(8,128)(2,1)}, bf16[4,1024,512]{2,1,0:T(8,128)(2,1)}, bf16[4,1024,512]{2,1,0:T(8,128)(2,1...) custom-call(s32[1,3]{1,0:T(1,128)} %lengths.3, ...), custom_call_target="tpu_custom_call" | custom-call | tf_op jit(solution)/shard_map/head/pallas_call | solution.py:635
  94.8 54.7 %experts.1 = (f32[128,1024]{1,0:T(8,128)}, bf16[1024,1152]{1,0:T(8,128)(2,1)}, bf16[4,3,8,64,512]{4,3,2,1,0:T(8,128)(2,1)}) custom-call(bf16[1024,1024]{1,0:T(8,128)(2,1)} %get-tuple-element.54.tokens_ref, bf16[128,1024]{1,0:T(8,128)(2,1)} %dy_ref.3, bf16[1,1024,512]{2,1,0:T(8,128)(2,1)} %get-tuple-element.55.router_ref.w_in, ...), custom_call_target="tpu_custom_call" | custom-call | tf_op jit(solution)/shard_map/experts/pallas_call | solution.py:1098
  149.5 89.0 %tail.1 = (bf16[128,1024]{1,0:T(8,128)(2,1)}, f32[128,1024]{1,0:T(8,128)}, f32[8,128]{1,0:T(8,128)}, f32[64,384]{1,0:T(8,128)}, f32[4,64,512]{2,1,0:T(8,128)}, /...) custom-call(s32[1,3]{1,0:T(1,128)} %lengths.3, bf16[1024,1152]{1,0:T(8,128)(2,1)} %get-tuple-element.62.grads_ref, ...), custom_call_target="tpu_custom_call" | custom-call | tf_op jit(solution)/shard_map/tail/pallas_call | solution.py:806
  238.6 3.1 %finish.1 = (bf16[128,1024]{1,0:T(8,128)(2,1)}, f32[128,1024]{1,0:T(8,128)}, f32[64,128]{1,0:T(8,128)}, f32[64,64]{1,0:T(8,128)}, f32[64,64]{1,0:T(8,128)}, /*in...) custom-call(bf16[128,1024]{1,0:T(8,128)(2,1)} %get-tuple-element.77., ...), custom_call_target="tpu_custom_call" | custom-call | tf_op jit(solution)/shard_map/finish/pallas_call | solution.py:1176
  241.7 1.5 copy.29
  (1 shorter events, 0.0 us)

commit v8 on v7

--- a/solution.py
+++ b/solution.py
@@ -582,6 +582,7 @@
     for pair in ((chosen_ref, chosen_out), (rank_ref, rank_out), (rank_t, rank_t_out), (cos_ref, cos_out), (sin_ref, sin_out)):
         store(*pair)
     drain(w_run)
+    pump([x_run])
     behind = [gate_run, up_run, down_run]
     pump(behind)
     store(w_all, w_out)
@@ -985,7 +986,8 @@
             pl.semaphore_signal(barrier, inc=1, device_id=device, device_id_type=MESH)
         pl.semaphore_wait(barrier, 4)
         dy_gather.stage(0)
-        slots_all[...] = jnp.zeros_like(slots_all)
+        for i in range(LOCAL):
+            slots_all[i * PLACES + SLOTS : (i + 1) * PLACES, :] = jnp.zeros((PLACES - SLOTS, D), BF16)
         dgate_all[...] = jnp.zeros_like(dgate_all)
         logits = jnp.where(chosen_ref[...] > 0.0, dot(tokens_ref[...], router_ref[0]), -1e30)
         raised = jnp.exp(logits - jnp.max(logits, axis=-1, keepdims=True))

time: 244 us -> 244 us (level)
  no operation moved by 1% of the time
where the time goes in v8:
time: 244 us; the launch traced here: 243 us
  Pallas kernels  237 us (97%)
  local copies, waits for them, and re-layouts  5.36 us (2%)
    pallas_call x1, Pallas kernels, head(): pl.pallas_call(head_body, name='head', out_shape=[shape(GROUP, D), shape(...  90.4 us
    pallas_call x1, Pallas kernels, tail(): pl.pallas_call(tail_body, name='tail', out_shape=[shape(ROWS, D, dtype=BF...  89.2 us
    pallas_call x1, Pallas kernels, experts(): pl.pallas_call(experts_body, name='experts', grid=(2 * LOCAL + 1,), in_sp...  54.7 us

profile of v8, /device:TPU:0, one launch (start us, length us, event | category | flops | bytes accessed | tf_op | source)
XLA Modules:
  0.0 243.4 jit_solution(8049909524050022095)
XLA Ops:
  0.6 0.8 copy.27
  1.4 0.8 copy.28
  2.2 0.8 copy.26
  3.0 1.5 concatenate.3
  4.5 90.4 %head.1 = (bf16[1024,1024]{1,0:T(8,128)(2,1)}, bf16[1,1024,512]{2,1,0:T(8,128)(2,1)}, bf16[4,1024,512]{2,1,0:T(8,128)(2,1)}, bf16[4,1024,512]{2,1,0:T(8,128)(2,1...) custom-call(s32[1,3]{1,0:T(1,128)} %lengths.3, ...), custom_call_target="tpu_custom_call" | custom-call | tf_op jit(solution)/shard_map/head/pallas_call | solution.py:636
  94.8 54.7 %experts.1 = (f32[128,1024]{1,0:T(8,128)}, bf16[1024,1152]{1,0:T(8,128)(2,1)}, bf16[4,3,8,64,512]{4,3,2,1,0:T(8,128)(2,1)}) custom-call(bf16[1024,1024]{1,0:T(8,128)(2,1)} %get-tuple-element.54.tokens_ref, bf16[128,1024]{1,0:T(8,128)(2,1)} %dy_ref.3, bf16[1,1024,512]{2,1,0:T(8,128)(2,1)} %get-tuple-element.55.router_ref.w_in, ...), custom_call_target="tpu_custom_call" | custom-call | tf_op jit(solution)/shard_map/experts/pallas_call | solution.py:1100
  149.5 89.2 %tail.1 = (bf16[128,1024]{1,0:T(8,128)(2,1)}, f32[128,1024]{1,0:T(8,128)}, f32[8,128]{1,0:T(8,128)}, f32[64,384]{1,0:T(8,128)}, f32[4,64,512]{2,1,0:T(8,128)}, /...) custom-call(s32[1,3]{1,0:T(1,128)} %lengths.3, bf16[1024,1152]{1,0:T(8,128)(2,1)} %get-tuple-element.62.grads_ref, ...), custom_call_target="tpu_custom_call" | custom-call | tf_op jit(solution)/shard_map/tail/pallas_call | solution.py:807
  238.7 3.1 %finish.1 = (bf16[128,1024]{1,0:T(8,128)(2,1)}, f32[128,1024]{1,0:T(8,128)}, f32[64,128]{1,0:T(8,128)}, f32[64,64]{1,0:T(8,128)}, f32[64,64]{1,0:T(8,128)}, /*in...) custom-call(bf16[128,1024]{1,0:T(8,128)(2,1)} %get-tuple-element.77., ...), custom_call_target="tpu_custom_call" | custom-call | tf_op jit(solution)/shard_map/finish/pallas_call | solution.py:1178
  241.8 1.5 copy.29
  (1 shorter events, 0.0 us)
